TPU v7x, 32 devices: a whole 2x2x4 slice. The times are simulated.
32 devices in a mesh: dp: 2 (over x), seq: 4 (over z), chan: 4 (over y, core).
Axes of the slice: x: 2, y: 2, z: 4, core: 2. Of those that a mesh axis runs over, the one named last changes fastest.
Arguments:
- tokens: bfloat16 [2, 4096, 1536], P('dp', 'seq'), may hold values from -6 to 6
- segment_ids: int32 [2, 4096], P('dp'), may hold values from 0 to 4095, as said below
- first_gain: bfloat16 [1536], replicated, may hold values from 0.5 to 1.5
- input_proj: bfloat16 [1536, 3072], P(None, 'chan'), may hold values from -0.15625 to 0.15625
- gate_proj: bfloat16 [1536, 3072], P(None, 'chan'), may hold values from -0.15625 to 0.15625
- conv_weight: bfloat16 [3072, 4], P('chan'), may hold values from -3 to 3
- conv_bias: bfloat16 [3072], P('chan'), may hold values from -3 to 3
- state_proj: bfloat16 [3072, 128], P('chan'), may hold values from -0.109375 to 0.109375
- step_proj: bfloat16 [96, 3072], P(None, 'chan'), may hold values from -0.625 to 0.625
- step_bias: bfloat16 [3072], P('chan'), may hold values from -6 to -2
- decay_log: bfloat16 [3072, 16], P('chan'), may hold values from -6 to 1
- skip_gain: bfloat16 [3072], P('chan'), may hold values from 0.5 to 1.5
- output_proj: bfloat16 [3072, 1536], P('chan'), may hold values from -0.3125 to 0.3125
- second_gain: bfloat16 [1536], replicated, may hold values from 0.5 to 1.5
- hidden_gate: bfloat16 [1536, 4096], P(None, 'chan'), may hold values from -0.15625 to 0.15625
- hidden_up: bfloat16 [1536, 4096], P(None, 'chan'), may hold values from -0.15625 to 0.15625
- hidden_down: bfloat16 [4096, 1536], P('chan'), may hold values from -0.1875 to 0.1875
- upstream: bfloat16 [2, 4096, 1536], P('dp', 'seq'), may hold values from -6 to 6
Outputs:
- result: bfloat16 [2, 4096, 1536], P('dp', 'seq')
- tokens_grad: float32 [2, 4096, 1536], P('dp', 'seq')
- first_gain_grad: float32 [1536], P(('dp', 'seq'))
- input_proj_grad: float32 [1536, 3072], P(('dp', 'seq'), 'chan')
- gate_proj_grad: float32 [1536, 3072], P(('dp', 'seq'), 'chan')
- conv_weight_grad: float32 [3072, 4], P('chan')
- conv_bias_grad: float32 [3072], P('chan')
- state_proj_grad: float32 [3072, 96], P('chan', ('dp', 'seq'))
- state_io_grad: float32 [3072, 32], P('chan')
- step_proj_grad: float32 [96, 3072], P(('dp', 'seq'), 'chan')
- step_bias_grad: float32 [3072], P('chan')
- decay_log_grad: float32 [3072, 16], P('chan')
- skip_gain_grad: float32 [3072], P('chan')
- output_proj_grad: float32 [3072, 1536], P('chan', ('dp', 'seq'))
- second_gain_grad: float32 [1536], P(('dp', 'seq'))
- hidden_gate_grad: float32 [1536, 4096], P(('dp', 'seq'), 'chan')
- hidden_up_grad: float32 [1536, 4096], P(('dp', 'seq'), 'chan')
- hidden_down_grad: float32 [4096, 1536], P('chan', ('dp', 'seq'))
Inputs may be any that keep to these rules, and one draw needn't show every extreme that they name: `segment_ids`: each token's id is the position, within its sequence, of the last token of its document, so ids never fall along a sequence; token 0 is a document by itself; in every sequence one document covers tokens 1024 - 1 through 4096 - 1024.
All inputs are finite; a program needn't handle non-finite values.
Results may differ from a plain program's by a relative error of at most 0.019.
Values may be sent and summed in bfloat16 or wider, within the bound.
No kernel may reach another device: no remote copies, remote signals or barrier semaphores. Data moves between devices by JAX's collectives and lax.ppermute only.
A program may use at most 256 MiB of HBM per device.

v0:
```python
import jax
import jax.numpy as jnp
from jax import lax
from jax.sharding import PartitionSpec as P

epsilon = 1e-05
block_span = 16


def from_behind(value, axis, by):
    devices = lax.axis_size(axis)
    pairs = [(i, i + by) for i in range(devices) if 0 <= i + by < devices]
    return lax.ppermute(value, axis, pairs)


def silu_slope(values):
    sigma = jax.nn.sigmoid(values)
    return sigma * (1.0 + values * (1.0 - sigma))


def matmul(left, right):
    return jnp.dot(left, right, preferred_element_type=jnp.float32)


def transposed_left(left, right):
    return lax.dot_general(
        left, right, (((0,), (0,)), ((), ())), preferred_element_type=jnp.float32
    )


def transposed_right(left, right):
    return lax.dot_general(
        left, right, (((1,), (1,)), ((), ())), preferred_element_type=jnp.float32
    )


def combine_pair(earlier, later):
    return (earlier[0] * later[0], later[1] + later[0] * earlier[1])


def channel_sum(partial_value):
    return lax.psum(partial_value, "chan")


def chain_states(product, state, backward):
    carried = jnp.zeros_like(state)
    for section in range(lax.axis_size("seq") - 1):
        carried = from_behind(state + product * carried, "seq", -1 if backward else 1)
    return carried


def step_factor(rates, keep, decay, position):
    return jnp.exp(rates[:, position, None, :] * decay[None]) * keep[:, position, None, None]


def forward_sweep(start, rates, drive, entry, readout, keep, decay):
    state = start
    product = jnp.ones_like(start)
    outputs = []
    for position in range(block_span):
        factor = step_factor(rates, keep, decay, position)
        state = factor * state + drive[:, position, None, :] * entry[:, position, :, None]
        product = product * factor
        outputs.append(jnp.sum(readout[:, position, :, None] * state, axis=1))
    return (state, product, jnp.stack(outputs, axis=1))


def head_gradient(rates, readout, keep, decay, grad_scan):
    carried = jnp.zeros((rates.shape[0], decay.shape[0], decay.shape[1]), jnp.float32)
    for position in reversed(range(block_span)):
        incoming = carried + readout[:, position, :, None] * grad_scan[:, position, None, :]
        carried = incoming * step_factor(rates, keep, decay, position)
    return carried


def backward_sweep(start, end_grads, rates, drive, entry, readout, keep, decay, grad_scan):
    states = [start]
    for position in range(block_span):
        states.append(
            step_factor(rates, keep, decay, position) * states[-1]
            + drive[:, position, None, :] * entry[:, position, :, None]
        )
    carried = end_grads
    decay_grad = jnp.zeros(decay.shape, jnp.float32)
    rate_parts = []
    drive_parts = []
    entry_parts = []
    readout_parts = []
    for position in reversed(range(block_span)):
        factor = step_factor(rates, keep, decay, position)
        carried = carried + readout[:, position, :, None] * grad_scan[:, position, None, :]
        scaled = carried * states[position] * factor
        rate_parts.insert(0, jnp.sum(scaled * decay[None], axis=1))
        decay_grad = decay_grad + jnp.sum(scaled * rates[:, position, None, :], axis=0)
        entry_parts.insert(0, jnp.sum(carried * drive[:, position, None, :], axis=2))
        drive_parts.insert(0, jnp.sum(carried * entry[:, position, :, None], axis=1))
        readout_parts.insert(
            0, jnp.sum(grad_scan[:, position, None, :] * states[position + 1], axis=2)
        )
        carried = carried * factor
    return (
        jnp.stack(rate_parts, axis=1),
        jnp.stack(drive_parts, axis=1),
        jnp.stack(entry_parts, axis=1),
        jnp.stack(readout_parts, axis=1),
        decay_grad,
    )


def per_device(
    tokens,
    segment_ids,
    first_gain,
    input_proj,
    gate_proj,
    conv_weight,
    conv_bias,
    state_proj,
    step_proj,
    step_bias,
    decay_log,
    skip_gain,
    output_proj,
    second_gain,
    hidden_gate,
    hidden_up,
    hidden_down,
    upstream,
):
    rows = tokens[0].astype(jnp.float32)
    count = rows.shape[0]
    width = conv_weight.shape[1]
    rank = step_proj.shape[0]
    state_size = decay_log.shape[1]
    channels = input_proj.shape[1]
    stretches = count // block_span
    place = lax.axis_index("seq")
    padded_ids = jnp.concatenate([jnp.full((width - 1,), -1, jnp.int32), segment_ids[0]], axis=0)
    window_ids = lax.dynamic_slice_in_dim(padded_ids, place * count, count + width - 1)
    own_ids = window_ids[width - 1 :]
    keep = (window_ids[width - 2 : width - 2 + count] == own_ids).astype(jnp.float32)

    def blocked(values):
        return values.reshape((stretches, block_span) + values.shape[1:])

    gain_one = first_gain.astype(jnp.float32)
    scale_one = lax.rsqrt(jnp.mean(rows * rows, axis=-1, keepdims=True) + epsilon)
    unit_one = rows * scale_one
    normed = (unit_one * gain_one).astype(jnp.bfloat16)
    inner = matmul(normed, input_proj).astype(jnp.bfloat16)
    gate_in = matmul(normed, gate_proj)
    rim = from_behind(inner[count - width + 1 :], "seq", 1)
    extended = jnp.concatenate([rim, inner], axis=0).astype(jnp.float32)
    taps = conv_weight.astype(jnp.float32)
    masks = [
        (window_ids[offset : offset + count] == own_ids).astype(jnp.float32)[:, None]
        for offset in range(width)
    ]
    convolved = conv_bias.astype(jnp.float32) + sum(
        (
            extended[offset : offset + count] * taps[:, offset] * masks[offset]
            for offset in range(width)
        )
    )
    mixed = jax.nn.silu(convolved).astype(jnp.bfloat16)
    mixed_wide = mixed.astype(jnp.float32)
    projected = channel_sum(matmul(mixed, state_proj))
    step_low = projected[:, :rank].astype(jnp.bfloat16)
    entry = projected[:, rank : rank + state_size]
    readout = projected[:, rank + state_size :]
    step_pre = matmul(step_low, step_proj) + step_bias.astype(jnp.float32)
    rates = jax.nn.softplus(step_pre)
    decay = -jnp.exp(decay_log.astype(jnp.float32)).T
    drive = rates * mixed_wide
    rate_blocks = blocked(rates)
    drive_blocks = blocked(drive)
    entry_blocks = blocked(entry)
    readout_blocks = blocked(readout)
    keep_blocks = blocked(keep)
    zero_state = jnp.zeros((stretches, state_size, channels), jnp.float32)
    local_end, local_product, unused = forward_sweep(
        zero_state, rate_blocks, drive_blocks, entry_blocks, readout_blocks, keep_blocks, decay
    )
    prefix_product, prefix_state = lax.associative_scan(
        combine_pair, (local_product, local_end), axis=0
    )
    arriving = chain_states(prefix_product[-1], prefix_state[-1], False)
    before_product = jnp.concatenate(
        [jnp.ones_like(prefix_product[:1]), prefix_product[:-1]], axis=0
    )
    before_state = jnp.concatenate([jnp.zeros_like(prefix_state[:1]), prefix_state[:-1]], axis=0)
    starts = before_state + before_product * arriving[None]
    ended, ignored, scanned = forward_sweep(
        starts, rate_blocks, drive_blocks, entry_blocks, readout_blocks, keep_blocks, decay
    )
    scanned = scanned.reshape(count, channels)
    skip = skip_gain.astype(jnp.float32)
    gate_act = jax.nn.silu(gate_in)
    ssm_sum = scanned + skip * mixed_wide
    gated = (ssm_sum * gate_act).astype(jnp.bfloat16)
    hidden_one = rows + lax.psum(matmul(gated, output_proj), "chan")
    gain_two = second_gain.astype(jnp.float32)
    scale_two = lax.rsqrt(jnp.mean(hidden_one * hidden_one, axis=-1, keepdims=True) + epsilon)
    unit_two = hidden_one * scale_two
    normed_local = (unit_two * gain_two).astype(jnp.bfloat16)
    gate_ffn = matmul(normed_local, hidden_gate)
    up_ffn = matmul(normed_local, hidden_up)
    gate_act_ffn = jax.nn.silu(gate_ffn)
    active = (gate_act_ffn * up_ffn).astype(jnp.bfloat16)
    result_local = hidden_one + lax.psum(
        matmul(active, hidden_down).astype(jnp.bfloat16), "chan"
    ).astype(jnp.float32)
    grad_low = upstream[0]
    grad_out = grad_low.astype(jnp.float32)
    grad_active = transposed_right(grad_low, hidden_down)
    down_grad = transposed_left(active, grad_low)
    grad_gate_ffn = (grad_active * up_ffn * silu_slope(gate_ffn)).astype(jnp.bfloat16)
    grad_up_ffn = (grad_active * gate_act_ffn).astype(jnp.bfloat16)
    gate_ffn_grad = transposed_left(normed_local, grad_gate_ffn)
    up_ffn_grad = transposed_left(normed_local, grad_up_ffn)
    grad_normed_two = lax.psum(
        (
            transposed_right(grad_gate_ffn, hidden_gate) + transposed_right(grad_up_ffn, hidden_up)
        ).astype(jnp.bfloat16),
        "chan",
    ).astype(jnp.float32)
    gain_two_grad = jnp.sum(grad_normed_two * unit_two, axis=0)
    grad_unit_two = grad_normed_two * gain_two
    grad_hidden = grad_out + scale_two * (
        grad_unit_two - unit_two * jnp.mean(grad_unit_two * unit_two, axis=-1, keepdims=True)
    )
    hidden_local = grad_hidden.astype(jnp.bfloat16)
    result = result_local.astype(jnp.bfloat16)
    output_weight_grad = transposed_left(gated, hidden_local)
    grad_gated = transposed_right(hidden_local, output_proj)
    grad_scanned = grad_gated * gate_act
    grad_gate_in = (grad_gated * ssm_sum * silu_slope(gate_in)).astype(jnp.bfloat16)
    skip_grad = jnp.sum(grad_scanned * mixed_wide, axis=0)
    grad_blocks = blocked(grad_scanned)
    heads = head_gradient(rate_blocks, readout_blocks, keep_blocks, decay, grad_blocks)
    after_all_product, after_all_state = lax.associative_scan(
        combine_pair, (local_product, heads), reverse=True, axis=0
    )
    leaving = chain_states(after_all_product[0], after_all_state[0], True)
    after_product = jnp.concatenate(
        [after_all_product[1:], jnp.ones_like(after_all_product[:1])], axis=0
    )
    after_state = jnp.concatenate(
        [after_all_state[1:], jnp.zeros_like(after_all_state[:1])], axis=0
    )
    end_grads = after_state + after_product * leaving[None]
    rate_grad, drive_grad, entry_grad, readout_grad, decay_grad = backward_sweep(
        starts,
        end_grads,
        rate_blocks,
        drive_blocks,
        entry_blocks,
        readout_blocks,
        keep_blocks,
        decay,
        grad_blocks,
    )
    drive_grad = drive_grad.reshape(count, channels)
    rates_grad = rate_grad.reshape(count, channels) + drive_grad * mixed_wide
    pre_grad = rates_grad * jax.nn.sigmoid(step_pre)
    step_bias_grad = jnp.sum(pre_grad, axis=0)
    pre_low = pre_grad.astype(jnp.bfloat16)
    step_weight_grad = transposed_left(step_low, pre_low)
    local_proj_grad = jnp.concatenate(
        [
            transposed_right(pre_low, step_proj),
            entry_grad.reshape(count, state_size),
            readout_grad.reshape(count, state_size),
        ],
        axis=1,
    )
    grad_projected = channel_sum(local_proj_grad).astype(jnp.bfloat16)
    state_weight_grad = transposed_left(mixed, grad_projected)
    state_rank_grad = state_weight_grad[:, :rank]
    state_edge_grad = state_weight_grad[:, rank:]
    grad_mixed = (
        transposed_right(grad_projected, state_proj) + drive_grad * rates + skip * grad_scanned
    )
    grad_conv = grad_mixed * silu_slope(convolved)
    conv_bias_grad = jnp.sum(grad_conv, axis=0)
    conv_taps_grad = jnp.stack(
        [
            jnp.sum(grad_conv * extended[offset : offset + count] * masks[offset], axis=0)
            for offset in range(width)
        ],
        axis=0,
    )
    grad_extended = jnp.zeros((count + width - 1, channels), jnp.float32)
    for offset in range(width):
        grad_extended = grad_extended.at[offset : offset + count].add(
            grad_conv * taps[:, offset] * masks[offset]
        )
    returned = from_behind(grad_extended[: width - 1], "seq", -1)
    grad_inner = grad_extended[width - 1 :] + jnp.concatenate(
        [jnp.zeros((count - width + 1, channels), jnp.float32), returned], axis=0
    )
    inner_low = grad_inner.astype(jnp.bfloat16)
    input_weight_grad = transposed_left(normed, inner_low)
    gate_weight_grad = transposed_left(normed, grad_gate_in)
    grad_normed = lax.psum(
        (
            transposed_right(inner_low, input_proj) + transposed_right(grad_gate_in, gate_proj)
        ).astype(jnp.bfloat16),
        "chan",
    ).astype(jnp.float32)
    gain_one_grad = jnp.sum(grad_normed * unit_one, axis=0)
    grad_unit_one = grad_normed * gain_one
    tokens_local = grad_hidden + scale_one * (
        grad_unit_one - unit_one * jnp.mean(grad_unit_one * unit_one, axis=-1, keepdims=True)
    )
    decay_scaled = decay_grad * decay
    vectors = (
        lax.psum(conv_taps_grad.astype(jnp.bfloat16), ("dp", "seq")).astype(jnp.float32),
        lax.psum(conv_bias_grad.astype(jnp.bfloat16), ("dp", "seq")).astype(jnp.float32),
        lax.psum(step_bias_grad.astype(jnp.bfloat16), ("dp", "seq")).astype(jnp.float32),
        lax.psum(decay_scaled.astype(jnp.bfloat16), ("dp", "seq")).astype(jnp.float32),
        lax.psum(skip_grad.astype(jnp.bfloat16), ("dp", "seq")).astype(jnp.float32),
        lax.psum(state_edge_grad.astype(jnp.bfloat16), ("dp", "seq")).astype(jnp.float32),
    )
    summed = tuple(
        (
            lax.psum_scatter(
                gain_one_grad.astype(jnp.bfloat16), ("dp", "seq"), scatter_dimension=0, tiled=True
            ).astype(jnp.float32),
            lax.psum_scatter(
                input_weight_grad.astype(jnp.bfloat16),
                ("dp", "seq"),
                scatter_dimension=0,
                tiled=True,
            ).astype(jnp.float32),
            lax.psum_scatter(
                gate_weight_grad.astype(jnp.bfloat16),
                ("dp", "seq"),
                scatter_dimension=0,
                tiled=True,
            ).astype(jnp.float32),
            lax.psum_scatter(
                state_rank_grad.astype(jnp.bfloat16), ("dp", "seq"), scatter_dimension=1, tiled=True
            ).astype(jnp.float32),
            lax.psum_scatter(
                step_weight_grad.astype(jnp.bfloat16),
                ("dp", "seq"),
                scatter_dimension=0,
                tiled=True,
            ).astype(jnp.float32),
            lax.psum_scatter(
                output_weight_grad.astype(jnp.bfloat16),
                ("dp", "seq"),
                scatter_dimension=1,
                tiled=True,
            ).astype(jnp.float32),
            lax.psum_scatter(
                gain_two_grad.astype(jnp.bfloat16), ("dp", "seq"), scatter_dimension=0, tiled=True
            ).astype(jnp.float32),
            lax.psum_scatter(
                gate_ffn_grad.astype(jnp.bfloat16), ("dp", "seq"), scatter_dimension=0, tiled=True
            ).astype(jnp.float32),
            lax.psum_scatter(
                up_ffn_grad.astype(jnp.bfloat16), ("dp", "seq"), scatter_dimension=0, tiled=True
            ).astype(jnp.float32),
            lax.psum_scatter(
                down_grad.astype(jnp.bfloat16), ("dp", "seq"), scatter_dimension=1, tiled=True
            ).astype(jnp.float32),
        )
    )
    return (
        result[None],
        tokens_local[None],
        summed[0],
        summed[1],
        summed[2],
        vectors[0].T,
        vectors[1],
        summed[3],
        vectors[5],
        summed[4],
        vectors[2],
        vectors[3].T,
        vectors[4],
        summed[5],
        summed[6],
        summed[7],
        summed[8],
        summed[9],
    )


def solution(mesh):
    return jax.shard_map(
        per_device,
        mesh=mesh,
        in_specs=(
            P("dp", "seq", None),
            P("dp", None),
            P(),
            P(None, "chan"),
            P(None, "chan"),
            P("chan", None),
            P("chan"),
            P("chan", None),
            P(None, "chan"),
            P("chan"),
            P("chan", None),
            P("chan"),
            P("chan", None),
            P(),
            P(None, "chan"),
            P(None, "chan"),
            P("chan", None),
            P("dp", "seq", None),
        ),
        out_specs=(
            P("dp", "seq", None),
            P("dp", "seq", None),
            P(("dp", "seq")),
            P(("dp", "seq"), "chan"),
            P(("dp", "seq"), "chan"),
            P("chan", None),
            P("chan"),
            P("chan", ("dp", "seq")),
            P("chan", None),
            P(("dp", "seq"), "chan"),
            P("chan"),
            P("chan", None),
            P("chan"),
            P("chan", ("dp", "seq")),
            P(("dp", "seq")),
            P(("dp", "seq"), "chan"),
            P(("dp", "seq"), "chan"),
            P("chan", ("dp", "seq")),
        ),
        check_vma=False,
    )
```

profile of v0, /device:TPU:0, one launch (start us, length us, event | category | flops | bytes accessed | tf_op | source)
XLA Modules:
  0.0 1780.6 jit_solution(7165895701650573133)
XLA Ops:
  32.5 33.5 %all-reduce.71.cloned.1.call-done = f32[1024,128]{1,0:T(8,128)} async-done(((f32[1024,128]{1,0:T(8,128)}), f32[1024,128]{1,0:T(8,128)}) %all-reduce.71.cloned.1.call-update) | async-done | bytes 524304 | tf_op jit(solution)/shard_map/psum | solution.py:42
  80.9 10.1 multiply_multiply_fusion.18
  92.3 15.2 multiply_add_fusion.32
  235.4 17.5 pad.368
  253.0 17.6 pad.186
  273.2 17.6 pad.185
  290.8 17.6 pad.370
  320.1 17.6 pad.174
  337.6 17.5 pad.173
  369.0 31.7 %multiply_reduce_fusion.85 = (f32[64,768]{1,0:T(8,128)}, f32[64,768]{1,0:T(8,128)}, f32[64,768]{1,0:T(8,128)}, f32[64,768]{1,0:T(8,128)}, f32[64,16,768]{2,1,0:T...) fusion(f32[64,16]{1,0:T(8,128)} %bitcast.547, ...), kind=kLoop, calls=%fused_computation.262 | loop fusion | flops 70582272 | bytes 38621184 | tf_op jit(solution)/shard_map/reduce_sum | solution.py:64
  433.6 118.2 %all-reduce.73.cloned.1.call-done = f32[1024,1536]{1,0:T(8,128)} async-done(((f32[1024,1536]{1,0:T(8,128)}), f32[1024,1536]{1,0:T(8,128)}) %all-reduce.73.cloned.1.call-update) | async-done | bytes 6291472 | tf_op jit(solution)/shard_map/psum | solution.py:201
  592.3 61.9 %all-reduce.75.cloned.1.call-done = bf16[1024,1536]{1,0:T(8,128)(2,1)} async-done(((bf16[1024,1536]{1,0:T(8,128)(2,1)}), bf16[1024,1536]{1,0:T(8,128)(2,1)}) %all-reduce.75.cloned.1.call-update) | async-done | bytes 3145744 | tf_op jit(solution)/shard_map/psum | solution.py:221
  679.0 14.8 fusion.50
  778.2 11.6 pad.374
  789.8 11.6 pad.198
  822.3 11.7 pad.197
  834.0 11.6 pad.372
  856.1 11.6 pad.210
  867.6 18.0 %pad.209 = f32[64,16,768]{2,1,0:T(8,128)} pad(f32[32,16,768]{2,1,0:T(8,128)} %pad_maximum_fusion.3, f32[]{:T(128)} %constant.138.clone.1), padding=0_1_1x0_0_0x0_0_0 | pad | bytes 4718596 | tf_op jit(solution)/shard_map/pad | solution.py:241
  900.1 14.2 multiply_reduce_fusion.15
  914.5 10.8 multiply_reduce_fusion.13
  945.7 9.9 multiply_reduce_fusion.7
  965.8 11.1 multiply_reduce_fusion.3
  1060.4 17.0 all-reduce.80
  1132.0 116.2 %all-reduce.79.cloned.1.call-done = (bf16[1024,1536]{1,0:T(8,128)(2,1)}, bf16[1024,1536]{1,0:T(8,128)(2,1)}) async-done(((bf16[1024,1536]{1,0:T(8,128)(2,1)}, bf16[1024,1536]{1,0:T(8,128)(2,1)}), (bf16[1024,1536]{1,0:T(8,128)(2,1)}, bf16[1024,1536]{1,0:T(8,128)(2,1)})) %all-reduce.79.cloned.1.call-update) | async-done | bytes 6291472 | tf_op jit(solution)/shard_map/psum | solution.py:210
  1297.5 26.6 %fusion.111 = (bf16[768,16]{0,1:T(8,128)(2,1)S(1)}, bf16[16,768]{1,0:T(8,128)(2,1)S(1)}) fusion(bf16[768,96]{0,1:T(8,128)(2,1)S(1)} %slice-done.2, bf16[96,768]{1,0:T(8,128)(2,1)S(1)} %convolution_convert_fusion.9), kind=kCustom, calls=%all-reduce-scatter.2 | all-reduce-scatter fusion | flops 196609 | bytes 344576
  1362.5 40.1 %reduce-scatter.19.cloned.1.call-done = bf16[192,1024]{1,0:T(8,128)(2,1)} async-done(((bf16[1536,1024]{1,0:T(8,128)(2,1)}), bf16[192,1024]{1,0:T(8,128)(2,1)}) %reduce-scatter.19.cloned.1.call-update) | async-done | bytes 393232 | tf_op jit(solution)/shard_map/reduce_scatter | solution.py:363
  1404.6 75.4 %reduce-scatter.17.cloned.1.call-done = bf16[192,1024]{1,0:T(8,128)(2,1)} async-done(((bf16[1536,1024]{1,0:T(8,128)(2,1)}), bf16[192,1024]{1,0:T(8,128)(2,1)}) %reduce-scatter.17.cloned.1.call-update) | async-done | bytes 393232 | tf_op jit(solution)/shard_map/reduce_scatter | solution.py:360
  1482.0 75.2 %reduce-scatter.21.cloned.1.call-done = bf16[1024,192]{0,1:T(8,128)(2,1)} async-done(((bf16[1024,1536]{0,1:T(8,128)(2,1)}), bf16[1024,192]{0,1:T(8,128)(2,1)}) %reduce-scatter.21.cloned.1.call-update) | async-done | bytes 393232 | tf_op jit(solution)/shard_map/reduce_scatter | solution.py:366
  1559.1 69.9 %reduce-scatter.15.cloned.1.call-done = bf16[768,192]{0,1:T(8,128)(2,1)} async-done(((bf16[768,1536]{0,1:T(8,128)(2,1)}), bf16[768,192]{0,1:T(8,128)(2,1)}) %reduce-scatter.15.cloned.1.call-update) | async-done | bytes 294928 | tf_op jit(solution)/shard_map/reduce_scatter | solution.py:351
  1630.9 69.5 %reduce-scatter.13.cloned.1.call-done = bf16[192,768]{1,0:T(8,128)(2,1)} async-done(((bf16[1536,768]{1,0:T(8,128)(2,1)}), bf16[192,768]{1,0:T(8,128)(2,1)}) %reduce-scatter.13.cloned.1.call-update) | async-done | bytes 294928 | tf_op jit(solution)/shard_map/reduce_scatter | solution.py:336
  1702.2 69.6 %reduce-scatter.11.cloned.1.call-done = bf16[192,768]{1,0:T(8,128)(2,1)} async-done(((bf16[1536,768]{1,0:T(8,128)(2,1)}), bf16[192,768]{1,0:T(8,128)(2,1)}) %reduce-scatter.11.cloned.1.call-update) | async-done | bytes 294928 | tf_op jit(solution)/shard_map/reduce_scatter | solution.py:330
  (1113 shorter events, 687.5 us)
Async XLA Ops:
  7.2 561.8 %copy-start = (bf16[1024,1536]{1,0:T(8,128)(2,1)S(1)}, bf16[1024,1536]{1,0:T(8,128)(2,1)}, u32[]{:S(2)}) copy-start(bf16[1024,1536]{1,0:T(8,128)(2,1)} %param.42) | copy-start | bytes 9437188
  7.2 58.7 %all-reduce.71.cloned.1.call-start = ((), (), s32[]{:S(2)}) async-start(), calls=%async_computation.6 | async-start | bytes 1048576 | tf_op jit(solution)/shard_map/psum | solution.py:42
  15.8 6.3 collective-permute-start
  30.7 521.1 %all-reduce.73.cloned.1.call-start = ((), (), s32[]{:S(2)}) async-start(), calls=%async_computation.7 | async-start | bytes 12582912 | tf_op jit(solution)/shard_map/psum | solution.py:201
  309.8 45.3 %copy-start.238 = (f32[1,16,768]{2,1,0:T(8,128)}, f32[1,16,768]{2,1,0:T(8,128)S(1)}, u32[]{:S(2)}) copy-start(f32[1,16,768]{2,1,0:T(8,128)S(1)} %get-tuple-element.257) | copy-start | bytes 147460
  309.8 45.3 %copy-start.240 = (f32[1,16,768]{2,1,0:T(8,128)}, f32[1,16,768]{2,1,0:T(8,128)S(1)}, u32[]{:S(2)}) copy-start(f32[1,16,768]{2,1,0:T(8,128)S(1)} %get-tuple-element.258) | copy-start | bytes 147460
  309.8 45.3 %collective-permute-start.1 = (f32[16,768]{1,0:T(8,128)}, f32[16,768]{1,0:T(8,128)S(1)}, u32[]{:S(2)}, u32[]{:S(2)}) collective-permute-start(f32[16,768]{1,0:T(8,128)} %get-tuple-element.256), channel_id=1, source_target_pairs={{0,4},{4,8},{8,12},{1,5},{5,9},{9,13},{2,6},{6,10},{10,14},{3,7},{... | collective-permute-start | bytes 147464 | tf_op jit(solution)/shard_map/ppermute | solution.py:13
  355.3 8.6 collective-permute-start.2
  363.9 5.1 collective-permute-start.3
  433.0 221.3 %all-reduce.75.cloned.1.call-start = ((), (), s32[]{:S(2)}) async-start(), calls=%async_computation.8 | async-start | bytes 6291456 | tf_op jit(solution)/shard_map/psum | solution.py:221
  585.4 662.7 %all-reduce.79.cloned.1.call-start = ((), (), s32[]{:S(2)}) async-start(), calls=%async_computation.16 | async-start | bytes 12582912 | tf_op jit(solution)/shard_map/psum | solution.py:210
  592.3 67.4 %copy-start.108 = (bf16[1,1024,1536]{2,1,0:T(8,128)(2,1)S(1)}, bf16[1,1024,1536]{2,1,0:T(8,128)(2,1)}, u32[]{:S(2)}) copy-start(bf16[1,1024,1536]{2,1,0:T(8,128)(2,1)} %param.43) | copy-start | bytes 9437188
  846.5 6.4 collective-permute-start.4
  853.5 32.1 %collective-permute-start.5 = (f32[16,768]{1,0:T(8,128)}, f32[16,768]{1,0:T(8,128)S(1)}, u32[]{:S(2)}, u32[]{:S(2)}) collective-permute-start(f32[16,768]{1,0:T(8,128)} %fusion.94), channel_id=1, source_target_pairs={{4,0},{8,4},{12,8},{5,1},{9,5},{13,9},{6,2},{10,6},{14,10},{7,3},{... | collective-permute-start | bytes 147464 | tf_op jit(solution)/shard_map/ppermute | solution.py:13
  886.3 13.0 collective-permute-start.6
  965.8 50.2 %copy-start.243 = (f32[64,1,16]{2,1,0:T(1,128)S(1)}, f32[64,1,16]{2,1,0:T(1,128)}, u32[]{:S(2)}) copy-start(f32[64,1,16]{2,1,0:T(1,128)} %get-tuple-element.362) | copy-start | bytes 12292
  1112.4 7.1 collective-permute-start.7
  1125.5 122.7 %copy-start.7 = (bf16[1,1024,1536]{2,1,0:T(8,128)(2,1)S(1)}, bf16[1,1024,1536]{2,1,0:T(8,128)(2,1)}, u32[]{:S(2)}) copy-start(bf16[1,1024,1536]{2,1,0:T(8,128)(2,1)} %param.26) | copy-start | bytes 9437188
  1125.5 122.7 %copy-start.301 = (f32[1536]{0:T(1024)S(1)}, f32[1536]{0:T(1024)}, u32[]{:S(2)}) copy-start(f32[1536]{0:T(1024)} %copy-done.299) | copy-start | bytes 18436
  1125.5 122.7 %copy-start.319 = (f32[1024]{0:T(1024)S(1)}, f32[1024]{0:T(1024)}, u32[]{:S(2)}) copy-start(f32[1024]{0:T(1024)} %copy-done.317) | copy-start | bytes 12292
  1125.6 226.3 %all-reduce.77.cloned.1.call-start = ((), (), s32[]{:S(2)}) async-start(), calls=%async_computation.15 | async-start | bytes 188416
  1252.6 150.0 %reduce-scatter.19.cloned.1.call-start = ((), (), s32[]{:S(2)}) async-start(), calls=%async_computation.13 | async-start | bytes 3538944 | tf_op jit(solution)/shard_map/reduce_scatter | solution.py:363
  1260.6 219.4 %reduce-scatter.17.cloned.1.call-start = ((), (), s32[]{:S(2)}) async-start(), calls=%async_computation.12 | async-start | bytes 3538944 | tf_op jit(solution)/shard_map/reduce_scatter | solution.py:360
  1268.4 288.8 %reduce-scatter.21.cloned.1.call-start = ((), (), s32[]{:S(2)}) async-start(), calls=%async_computation.14 | async-start | bytes 3538944 | tf_op jit(solution)/shard_map/reduce_scatter | solution.py:366
  1276.1 353.0 %reduce-scatter.15.cloned.1.call-start = ((), (), s32[]{:S(2)}) async-start(), calls=%async_computation.11 | async-start | bytes 2654208 | tf_op jit(solution)/shard_map/reduce_scatter | solution.py:351
  1283.8 416.6 %reduce-scatter.13.cloned.1.call-start = ((), (), s32[]{:S(2)}) async-start(), calls=%async_computation.10 | async-start | bytes 2654208 | tf_op jit(solution)/shard_map/reduce_scatter | solution.py:336
  1289.6 482.3 %reduce-scatter.11.cloned.1.call-start = ((), (), s32[]{:S(2)}) async-start(), calls=%async_computation.9 | async-start | bytes 2654208 | tf_op jit(solution)/shard_map/reduce_scatter | solution.py:330
  1324.1 13.7 collective-permute-start.8
  1325.4 12.7 collective-permute-start.10
  1327.1 10.6 collective-permute-start.9
  1333.9 4.2 collective-permute-start.11
  1358.2 415.4 %copy-start.1 = (bf16[1024,1536]{1,0:T(8,128)(2,1)S(1)}, bf16[1024,1536]{1,0:T(8,128)(2,1)}, u32[]{:S(2)}) copy-start(bf16[1024,1536]{1,0:T(8,128)(2,1)} %param.42) | copy-start | bytes 9437188
  (338 other events, 2958.4 us)
Sparse Core Ops, SparseCore 0:
  30.8 35.0 all-reduce.70
  433.1 118.6 all-reduce.72
  585.6 68.6 all-reduce.74
  1125.7 122.4 all-reduce.78
  1254.0 71.5 all-reduce.76
  1329.0 73.5 reduce-scatter.18
  1406.2 73.7 reduce-scatter.16
  1483.6 73.5 reduce-scatter.20
  1560.7 68.3 reduce-scatter.14
  1632.4 67.9 reduce-scatter.12
  1703.9 67.9 reduce-scatter.10
where the time goes:
time: 1810 us; the launch traced here: 1780 us
  waiting for transfers between devices  732 us (40%)
  local copies, waits for them, and re-layouts  470 us (26%)
  other arithmetic  358 us (20%)
  matrix products  122 us (7%)
  blocking collectives  43.6 us (2%)
  starting transfers between devices  34.9 us (2%)
  between operations  20.6 us (1%)
    pad x20, local copies, waits for them, and re-layouts, per_device(): lax.associative_scan(combine_pair, (local_product, local_end), axis=0)  152 us
    psum x1, waiting for transfers between devices, per_device(): hidden_one = rows + lax.psum(matmul(gated, output_proj), 'chan')  118 us
    psum x1, waiting for transfers between devices, per_device(): lax.psum(matmul(active, hidden_down).astype(jnp.bfloat16), 'chan')  116 us
    pad x20, local copies, waits for them, and re-layouts, per_device(): lax.associative_scan(combine_pair, (local_product, heads), reverse=True,...  114 us
    unnamed x804, local copies, waits for them, and re-layouts  103 us
    reduce_sum x8, other arithmetic, backward_sweep(): jnp.sum(scaled * rates[:, position, None, :], axis=0)  84.9 us
    reduce_scatter x1, waiting for transfers between devices, per_device(): lax.psum_scatter(gate_ffn_grad.astype(jnp.bfloat16), ('dp', 'seq'), scatt...  75.4 us
    reduce_scatter x1, waiting for transfers between devices, per_device(): lax.psum_scatter(down_grad.astype(jnp.bfloat16), ('dp', 'seq'), scatter_d...  75.2 us
  transfers between devices with their start and end apart: 23, of which 12 were waited for; matrix products, arithmetic and copies ran while one was open for 12% of the time, Pallas kernels for 0%

commit v1 on v0

v1 whole, which is shorter than its diff:
```python
import functools

import jax
import jax.numpy as jnp
from jax import lax
from jax.experimental import pallas as pl
from jax.experimental.pallas import tpu as pltpu
from jax.sharding import PartitionSpec as P

epsilon = 1e-05
pieces = 8
lanes = 128
far = 1e6
log2e = 1.4426950408889634
ln2 = 0.6931471805599453
vmem_bytes = 52 * 1024 * 1024
bf16 = jnp.bfloat16
f32 = jnp.float32


def silu_slope(values):
    sigma = jax.nn.sigmoid(values)
    return sigma * (1.0 + values * (1.0 - sigma))


def matmul(left, right):
    return jnp.dot(left, right, preferred_element_type=f32)


def transposed_left(left, right):
    return lax.dot_general(left, right, (((0,), (0,)), ((), ())), preferred_element_type=f32)


def transposed_right(left, right):
    return lax.dot_general(left, right, (((1,), (1,)), ((), ())), preferred_element_type=f32)


def swap(value, axis, mask):
    return lax.ppermute(value, axis, [(i, i ^ mask) for i in range(lax.axis_size(axis))])


def shifted(value, axis, by):
    size = lax.axis_size(axis)
    return lax.ppermute(value, axis, [(i, i + by) for i in range(size) if 0 <= i + by < size])


def bits_of(axis):
    return [1 << k for k in reversed(range(lax.axis_size(axis).bit_length() - 1))]


def bit_is_set(axis, mask):
    return ((lax.axis_index(axis) & mask) != 0).astype(jnp.int32)


def sum_all(value, axes):
    for axis, mask in axes:
        value = (value.astype(f32) + swap(value, axis, mask).astype(f32)).astype(bf16)
    return value


def sum_scatter(value, order, whole):
    value = value.reshape((2,) * len(whole) + (-1,) + value.shape[1:])
    left = list(whole)
    for axis, mask in order:
        at = left.index((axis, mask))
        left.pop(at)
        mine = bit_is_set(axis, mask)
        keep = lax.dynamic_index_in_dim(value, mine, at, keepdims=False)
        away = lax.dynamic_index_in_dim(value, 1 - mine, at, keepdims=False)
        total = keep.astype(f32) + swap(away, axis, mask).astype(f32)
        value = total.astype(bf16) if left else total
    return value


def chan_scatter(part):
    third = swap(part(3), "chan", 1)
    second = swap((part(2).astype(f32) + third.astype(f32)).astype(bf16), "chan", 2)
    first = swap(part(1), "chan", 1)
    return part(0).astype(f32) + first.astype(f32) + second.astype(f32)


def chan_gather(own):
    across = swap(own, "chan", 2)
    beside = swap(own, "chan", 1)
    return [own, beside, across, swap(across, "chan", 1)]


def chan_total(value):
    value = value + swap(value, "chan", 1)
    value = value.astype(bf16)
    return value.astype(f32) + swap(value, "chan", 2).astype(f32)


def spread(proj, out, first, count, steps):
    def fill(i, unused):
        rows = pl.ds(pl.multiple_of(i * pieces, pieces), pieces)
        tile = proj[rows, :]
        for n in range(count):
            out[n, rows, :] = jnp.broadcast_to(tile[:, first + n : first + n + 1], (pieces, lanes))
        return unused

    lax.fori_loop(0, steps, fill, 0)


def decay_rows(dec, count):
    return [jnp.broadcast_to(dec[n : n + 1, :], (pieces, lanes)) for n in range(count)]


def ends_kernel(size, rank, reff, drive, proj, dec, ends, sums, end_total, product_total, eb):
    steps = reff.shape[0] // pieces

    @pl.when(pl.program_id(0) == 0)
    def _():
        spread(proj, eb, rank, size, steps)

    decays = decay_rows(dec, size)

    def body(i, carry):
        states, total = carry
        rows = pl.ds(pl.multiple_of(i * pieces, pieces), pieces)
        rate = reff[rows, :]
        push = drive[rows, :]
        out = []
        for n in range(size):
            out.append(jnp.exp2(rate * decays[n]) * states[n] + push * eb[n, rows, :])
        return tuple(out), total + rate

    zero = jnp.zeros((pieces, lanes), f32)
    states, total = lax.fori_loop(0, steps, body, ((zero,) * size, zero), unroll=2)
    for n in range(size):
        ends[n] = states[n]
    sums[...] = total
    reached = ends[:, 0, :]
    for s in range(1, pieces):
        reached = ends[:, s, :] + jnp.exp2(dec[...] * sums[s : s + 1, :]) * reached
    end_total[...] = reached
    product_total[...] = jnp.exp2(dec[...] * jnp.sum(total, axis=0, keepdims=True))


def forward_kernel(
    size, rank, reff, drive, proj, dec, ends, sums, arriving, scanned, before, eb, rb, start
):
    steps = reff.shape[0] // pieces

    @pl.when(pl.program_id(0) == 0)
    def _():
        spread(proj, eb, rank, size, steps)
        spread(proj, rb, rank + size, size, steps)

    decays = decay_rows(dec, size)
    reached = arriving[...]
    for s in range(pieces):
        start[:, s, :] = reached
        reached = ends[:, s, :] + jnp.exp2(dec[...] * sums[s : s + 1, :]) * reached

    def body(i, states):
        rows = pl.ds(pl.multiple_of(i * 2 * pieces, 2 * pieces), 2 * pieces)
        rate = reff[rows, :]
        push = drive[rows, :]
        low = jnp.zeros((pieces, lanes), f32)
        high = low
        out = []
        for n in range(size):
            entry = eb[n, rows, :]
            readout = rb[n, rows, :]
            at_zero = states[n]
            at_one = jnp.exp2(rate[:pieces] * decays[n]) * at_zero + push[:pieces] * entry[:pieces]
            at_two = jnp.exp2(rate[pieces:] * decays[n]) * at_one + push[pieces:] * entry[pieces:]
            low = low + readout[:pieces] * at_one
            high = high + readout[pieces:] * at_two
            before[n, rows, :] = jnp.concatenate([at_zero, at_one], axis=0).astype(bf16)
            out.append(at_two)
        scanned[rows, :] = jnp.concatenate([low, high], axis=0)
        return tuple(out)

    states = lax.fori_loop(0, steps // 2, body, tuple(start[n] for n in range(size)))
    for n in range(size):
        last = jnp.concatenate([states[n], states[n]], axis=0).astype(bf16)
        before[n, pl.ds(steps * pieces, 2 * pieces), :] = last


def heads_kernel(size, rank, reff, slope, proj, dec, sums, heads, head_total, rb):
    steps = reff.shape[0] // pieces

    @pl.when(pl.program_id(0) == 0)
    def _():
        spread(proj, rb, rank + size, size, steps)

    decays = decay_rows(dec, size)

    def body(i, carried):
        rows = pl.ds(pl.multiple_of((steps - 1 - i) * pieces, pieces), pieces)
        rate = reff[rows, :]
        grad = slope[rows, :]
        return tuple(
            (carried[n] + rb[n, rows, :] * grad) * jnp.exp2(rate * decays[n]) for n in range(size)
        )

    zero = jnp.zeros((pieces, lanes), f32)
    carried = lax.fori_loop(0, steps, body, (zero,) * size, unroll=2)
    for n in range(size):
        heads[n] = carried[n]
    reached = heads[:, pieces - 1, :]
    for s in reversed(range(pieces - 1)):
        reached = heads[:, s, :] + jnp.exp2(dec[...] * sums[s : s + 1, :]) * reached
    head_total[...] = reached


def backward_kernel(
    size,
    rank,
    reff,
    drive,
    slope,
    proj,
    dec,
    heads,
    sums,
    leaving,
    before,
    rate_grad,
    drive_grad,
    proj_grad,
    decay_grad,
    eb,
    rb,
    stop,
    decay_sum,
    entry_terms,
    readout_terms,
):
    steps = reff.shape[0] // pieces
    pair = 2 * pieces

    @pl.when(pl.program_id(0) == 0)
    def _():
        spread(proj, eb, rank, size, steps)
        spread(proj, rb, rank + size, size, steps)
        proj_grad[...] = jnp.zeros_like(proj_grad)

    decays = decay_rows(dec, size)
    reached = leaving[...]
    for s in reversed(range(pieces)):
        stop[:, s, :] = reached
        reached = heads[:, s, :] + jnp.exp2(dec[...] * sums[s : s + 1, :]) * reached
    decay_sum[...] = jnp.zeros_like(decay_sum)

    def body(i, carried):
        at = pl.multiple_of((steps // 2 - 1 - i) * pair, pair)
        rows = pl.ds(at, pair)
        following = pl.ds(at + pair, pair)
        rate = reff[rows, :]
        push = drive[rows, :]
        grad = slope[rows, :]
        rate0, rate1 = rate[:pieces], rate[pieces:]
        push0, push1 = push[:pieces], push[pieces:]
        grad0, grad1 = grad[:pieces], grad[pieces:]
        zero = jnp.zeros((pieces, lanes), f32)
        rates0 = rates1 = drives0 = drives1 = zero
        out = []
        for n in range(size):
            entry = eb[n, rows, :]
            readout = rb[n, rows, :]
            state = before[n, rows, :].astype(f32)
            later = before[n, following, :].astype(f32)[:pieces]
            held1 = carried[n] + readout[pieces:] * grad1
            passed1 = held1 * jnp.exp2(rate1 * decays[n])
            scaled1 = passed1 * state[pieces:]
            held0 = passed1 + readout[:pieces] * grad0
            passed0 = held0 * jnp.exp2(rate0 * decays[n])
            scaled0 = passed0 * state[:pieces]
            rates1 = rates1 + scaled1 * decays[n]
            rates0 = rates0 + scaled0 * decays[n]
            drives1 = drives1 + held1 * entry[pieces:]
            drives0 = drives0 + held0 * entry[:pieces]
            decay_sum[n] += scaled1 * rate1 + scaled0 * rate0
            half = pl.ds((n % 2) * lanes, lanes)
            entry_terms[n // 2, rows, half] = jnp.concatenate(
                [held0 * push0, held1 * push1], axis=0
            ).astype(bf16)
            readout_terms[n // 2, rows, half] = jnp.concatenate(
                [grad0 * state[pieces:], grad1 * later], axis=0
            ).astype(bf16)
            out.append(passed0)
        rate_grad[rows, :] = jnp.concatenate([rates0, rates1], axis=0) * ln2
        drive_grad[rows, :] = jnp.concatenate([drives0, drives1], axis=0)
        return tuple(out)

    lax.fori_loop(0, steps // 2, body, tuple(stop[n] for n in range(size)))
    decay_grad[...] = jnp.sum(decay_sum[...], axis=1)

    source = lax.broadcasted_iota(jnp.int32, (2 * lanes, lanes), 0) // lanes
    target = lax.broadcasted_iota(jnp.int32, (2 * lanes, lanes), 1)
    tall = 256

    def gather(i, unused):
        rows = pl.ds(pl.multiple_of(i * tall, tall), tall)
        total = proj_grad[rows, :]
        for j in range(size // 2):
            pick = (target == source + (rank + 2 * j)).astype(f32).astype(bf16)
            total = total + jnp.dot(entry_terms[j, rows, :], pick, preferred_element_type=f32)
            pick = (target == source + (rank + size + 2 * j)).astype(f32).astype(bf16)
            total = total + jnp.dot(readout_terms[j, rows, :], pick, preferred_element_type=f32)
        proj_grad[rows, :] = total
        return unused

    lax.fori_loop(0, steps * pieces // tall, gather, 0)


def scan_calls(count, channels, size, rank):
    groups = channels // lanes
    steps = count // pieces
    tall = pl.BlockSpec((count, lanes), lambda g: (0, g))
    fixed = pl.BlockSpec((count, lanes), lambda g: (0, 0))
    small = pl.BlockSpec((size, lanes), lambda g: (0, g))
    ends = pl.BlockSpec((size, pieces, lanes), lambda g: (0, 0, g))
    sums = pl.BlockSpec((pieces, lanes), lambda g: (0, g))
    states = pl.BlockSpec((size, count + 2 * pieces, lanes), lambda g: (0, 0, g))
    wide = pltpu.VMEM((size, count, lanes), f32)
    tall_out = jax.ShapeDtypeStruct((count, channels), f32)
    small_out = jax.ShapeDtypeStruct((size, channels), f32)
    ends_out = jax.ShapeDtypeStruct((size, pieces, channels), f32)
    sums_out = jax.ShapeDtypeStruct((pieces, channels), f32)
    states_out = jax.ShapeDtypeStruct((size, count + 2 * pieces, channels), bf16)
    fixed_out = jax.ShapeDtypeStruct((count, lanes), f32)
    terms = pltpu.VMEM((size // 2, count, 2 * lanes), bf16)
    edge = pltpu.VMEM((size, pieces, lanes), f32)
    work = count * channels * size

    def call(kernel, name, ins, outs, out_shape, scratch, cost):
        return pl.pallas_call(
            functools.partial(kernel, size, rank),
            grid=(groups,),
            in_specs=ins,
            out_specs=outs,
            out_shape=out_shape,
            scratch_shapes=scratch,
            compiler_params=pltpu.CompilerParams(
                dimension_semantics=("arbitrary",), vmem_limit_bytes=vmem_bytes
            ),
            cost_estimate=pl.CostEstimate(
                flops=cost * work, bytes_accessed=20_000_000, transcendentals=work
            ),
            name=name,
        )

    return (
        call(
            ends_kernel,
            "scan_ends",
            [tall, tall, fixed, small],
            [ends, sums, small, small],
            [ends_out, sums_out, small_out, small_out],
            [wide],
            4,
        ),
        call(
            forward_kernel,
            "scan_forward",
            [tall, tall, fixed, small, ends, sums, small],
            [tall, states],
            [tall_out, states_out],
            [wide, wide, edge],
            6,
        ),
        call(
            heads_kernel,
            "scan_heads",
            [tall, tall, fixed, small, sums],
            [ends, small],
            [ends_out, small_out],
            [wide],
            4,
        ),
        call(
            backward_kernel,
            "scan_backward",
            [tall, tall, tall, fixed, small, ends, sums, small, states],
            [tall, tall, fixed, small],
            [tall_out, tall_out, fixed_out, small_out],
            [wide, wide, edge, edge, terms, terms],
            16,
        ),
    )


def chained(product, end, by):
    pair = jnp.stack([product, end])
    total = jnp.zeros_like(end)
    for distance in reversed(range(1, lax.axis_size("seq"))):
        got = shifted(pair, "seq", by * distance)
        total = got[1] + got[0] * total
    return total


def per_device(
    tokens,
    segment_ids,
    first_gain,
    input_proj,
    gate_proj,
    conv_weight,
    conv_bias,
    state_proj,
    step_proj,
    step_bias,
    decay_log,
    skip_gain,
    output_proj,
    second_gain,
    hidden_gate,
    hidden_up,
    hidden_down,
    upstream,
):
    count, features = tokens.shape[1:]
    width = conv_weight.shape[1]
    rank = step_proj.shape[0]
    size = decay_log.shape[1]
    channels = input_proj.shape[1]
    steps = count // pieces
    quarter = count // lax.axis_size("chan")
    me = lax.axis_index("chan")
    place = lax.axis_index("seq")
    dp_bits = [("dp", mask) for mask in bits_of("dp")]
    seq_bits = [("seq", mask) for mask in bits_of("seq")]
    shard_bits = dp_bits + seq_bits
    scan_ends, scan_forward, scan_heads, scan_backward = scan_calls(count, channels, size, rank)

    def mixed_order(values):
        return (
            values.reshape((pieces, steps) + values.shape[1:])
            .swapaxes(0, 1)
            .reshape(values.shape)
        )

    def block(values, r):
        return lax.dynamic_slice_in_dim(values, (me ^ r) * quarter, quarter)

    padded_ids = jnp.concatenate([jnp.full((width - 1,), -1, jnp.int32), segment_ids[0]], axis=0)
    window_ids = lax.dynamic_slice_in_dim(padded_ids, place * count, count + width - 1)
    own_ids = window_ids[width - 1 :]
    masks = [
        mixed_order((window_ids[offset : offset + count] == own_ids).astype(f32)[:, None])
        for offset in range(width)
    ]
    keep = masks[width - 2]

    rows = mixed_order(tokens[0])
    upper = mixed_order(upstream[0])

    def unit_of(values):
        scale = lax.rsqrt(jnp.mean(values * values, axis=-1, keepdims=True) + epsilon)
        return scale, values * scale

    gain_one = first_gain.astype(f32)
    gain_two = second_gain.astype(f32)
    normed = (unit_of(rows.astype(f32))[1] * gain_one).astype(bf16)
    inner = matmul(normed, input_proj).astype(bf16)

    reach = (width - 1) * pieces
    tail = inner[count - reach :].reshape(width - 1, pieces, channels)
    brought = shifted(tail[:, pieces - 1, :], "seq", 1)
    rim = jnp.concatenate([brought[:, None, :], tail[:, : pieces - 1, :]], axis=1)
    extended = jnp.concatenate([rim.reshape(reach, channels), inner], axis=0)
    taps = conv_weight.astype(f32).T

    def window(offset):
        return extended[offset * pieces : offset * pieces + count].astype(f32)

    convolved = conv_bias.astype(f32) + sum(
        window(offset) * taps[offset] * masks[offset] for offset in range(width)
    )
    mixed = jax.nn.silu(convolved).astype(bf16)
    mixed_wide = mixed.astype(f32)
    projected = chan_total(matmul(mixed, state_proj))
    gate_in = matmul(normed, gate_proj)
    step_low = projected[:, :rank].astype(bf16)
    step_pre = matmul(step_low, step_proj) + step_bias.astype(f32)
    rates = jax.nn.softplus(step_pre)
    decay = -jnp.exp(decay_log.astype(f32)).T
    decay_two = decay * log2e
    drive = rates * mixed_wide
    effective = jnp.where(keep > 0.0, rates, far)

    ends, sums, end_total, product_total = scan_ends(effective, drive, projected, decay_two)
    arriving = chained(product_total, end_total, 1)
    scanned, before = scan_forward(effective, drive, projected, decay_two, ends, sums, arriving)

    skip = skip_gain.astype(f32)
    gate_act = jax.nn.silu(gate_in)
    ssm_sum = scanned + skip * mixed_wide
    gated = (ssm_sum * gate_act).astype(bf16)

    hidden_sum = chan_scatter(lambda r: matmul(block(gated, r), output_proj).astype(bf16))
    rows_own = block(rows, 0).astype(f32)
    upper_own = block(upper, 0).astype(f32)
    hidden_one = rows_own + hidden_sum
    scale_two, unit_two = unit_of(hidden_one)
    normed_blocks = chan_gather((unit_two * gain_two).astype(bf16))
    upper_blocks = [block(upper, r) for r in range(4)]

    def feed_forward(normed_part, upper_part):
        gate_ffn = matmul(normed_part, hidden_gate)
        up_ffn = matmul(normed_part, hidden_up)
        gate_act_ffn = jax.nn.silu(gate_ffn)
        active = (gate_act_ffn * up_ffn).astype(bf16)
        grad_active = transposed_right(upper_part, hidden_down)
        grad_gate_ffn = (grad_active * up_ffn * silu_slope(gate_ffn)).astype(bf16)
        grad_up_ffn = (grad_active * gate_act_ffn).astype(bf16)
        grad_normed = (
            transposed_right(grad_gate_ffn, hidden_gate) + transposed_right(grad_up_ffn, hidden_up)
        ).astype(bf16)
        return active, grad_gate_ffn, grad_up_ffn, grad_normed

    halves = []
    for first in (0, 2):
        normed_half = jnp.concatenate(normed_blocks[first : first + 2], axis=0)
        upper_half = jnp.concatenate(upper_blocks[first : first + 2], axis=0)
        halves.append((normed_half, upper_half) + feed_forward(normed_half, upper_half))

    def quarter_of(items, r):
        return items[r // 2][(r % 2) * quarter : (r % 2 + 1) * quarter]

    grad_normed_two = chan_scatter(lambda r: quarter_of([half[5] for half in halves], r))
    normed_two, upper_two, active, grad_gate_ffn, grad_up_ffn = (
        jnp.concatenate([half[k] for half in halves], axis=0) for k in range(5)
    )

    def grad_scatter(value, order):
        return sum_scatter(value.astype(bf16), order, shard_bits)

    usual = dp_bits + seq_bits[::-1]
    other = seq_bits[-1:] + dp_bits + seq_bits[:-1]
    up_grad = grad_scatter(transposed_left(normed_two, grad_up_ffn), usual)
    gate_ffn_grad = grad_scatter(transposed_left(normed_two, grad_gate_ffn), usual)
    down_grad = grad_scatter(transposed_left(upper_two, active), usual)

    gain_two_grad = jnp.sum(grad_normed_two * unit_two, axis=0)
    grad_unit_two = grad_normed_two * gain_two
    grad_hidden = upper_own + scale_two * (
        grad_unit_two - unit_two * jnp.mean(grad_unit_two * unit_two, axis=-1, keepdims=True)
    )
    hidden_blocks = chan_gather(grad_hidden.astype(bf16))

    def placed(blocks):
        whole = jnp.zeros((count, blocks[0].shape[1]), blocks[0].dtype)
        for r, item in enumerate(blocks):
            whole = lax.dynamic_update_slice_in_dim(whole, item, (me ^ r) * quarter, 0)
        return whole

    def natural(own, dtype):
        item = own.reshape(steps // 4, pieces, features).swapaxes(0, 1)
        whole = jnp.zeros((pieces, steps, features), dtype)
        for r, got in enumerate(chan_gather(item)):
            whole = lax.dynamic_update_slice_in_dim(
                whole, got.astype(dtype), (me ^ r) * (steps // 4), 1
            )
        return whole.reshape(1, count, features)

    hidden_low = placed(hidden_blocks)
    grad_gated = transposed_right(hidden_low, output_proj)
    grad_scanned = grad_gated * gate_act
    grad_gate_in = (grad_gated * ssm_sum * silu_slope(gate_in)).astype(bf16)
    skip_grad = jnp.sum(grad_scanned * mixed_wide, axis=0)
    heads, head_total = scan_heads(effective, grad_scanned, projected, decay_two, sums)
    leaving = chained(product_total, head_total, -1)
    output_grad = grad_scatter(transposed_left(hidden_low, gated), usual)
    gate_grad = grad_scatter(transposed_left(normed, grad_gate_in), other)
    result_sum = chan_scatter(
        lambda r: matmul(quarter_of([half[2] for half in halves], r), hidden_down).astype(bf16)
    )
    result = natural((hidden_one + result_sum).astype(bf16), bf16)

    rate_grad, drive_grad, proj_terms, decay_grad = scan_backward(
        effective, drive, grad_scanned, projected, decay_two, heads, sums, leaving, before
    )
    rates_grad = rate_grad + drive_grad * mixed_wide
    pre_grad = rates_grad * jax.nn.sigmoid(step_pre)
    step_bias_grad = jnp.sum(pre_grad, axis=0)
    pre_low = pre_grad.astype(bf16)
    step_padded = jnp.pad(step_proj, ((0, 2 * size), (0, 0)))
    grad_projected = chan_total(transposed_right(pre_low, step_padded) + proj_terms).astype(bf16)
    step_weight_grad = transposed_left(step_low, pre_low)
    grad_mixed = (
        transposed_right(grad_projected, state_proj) + drive_grad * rates + skip * grad_scanned
    )
    grad_conv = grad_mixed * silu_slope(convolved)
    conv_bias_grad = jnp.sum(grad_conv, axis=0)
    conv_taps_grad = jnp.stack(
        [
            jnp.sum(grad_conv * window(offset) * masks[offset], axis=0)
            for offset in range(width)
        ],
        axis=0,
    )
    grad_extended = sum(
        jnp.pad(
            grad_conv * taps[offset] * masks[offset],
            ((offset * pieces, reach - offset * pieces), (0, 0)),
        )
        for offset in range(width)
    )
    spill = grad_extended[:reach].reshape(width - 1, pieces, channels)
    returned = shifted(spill[:, 0, :], "seq", -1)
    spill = jnp.concatenate([spill[:, 1:, :], returned[:, None, :]], axis=1)
    inner_low = (
        grad_extended[reach:]
        + jnp.pad(spill.reshape(reach, channels), ((count - reach, 0), (0, 0)))
    ).astype(bf16)

    def token_part(r):
        return (
            transposed_right(block(inner_low, r), input_proj)
            + transposed_right(block(grad_gate_in, r), gate_proj)
        ).astype(bf16)

    grad_normed = chan_scatter(token_part)
    input_grad = grad_scatter(transposed_left(normed, inner_low), usual)
    scale_one, unit_one = unit_of(rows_own)
    gain_one_grad = jnp.sum(grad_normed * unit_one, axis=0)
    grad_unit_one = grad_normed * gain_one
    tokens_grad = grad_hidden + scale_one * (
        grad_unit_one - unit_one * jnp.mean(grad_unit_one * unit_one, axis=-1, keepdims=True)
    )
    tokens_out = natural(tokens_grad.astype(bf16), f32)

    state_grad = transposed_left(grad_projected, mixed)
    chan_bits = [("chan", 1), ("chan", 2)]
    gain_two_sum = sum_all(gain_two_grad.astype(bf16), chan_bits + shard_bits).astype(f32)
    gain_one_sum = sum_all(gain_one_grad.astype(bf16), chan_bits + shard_bits).astype(f32)
    shards = lax.axis_size("dp") * lax.axis_size("seq")
    shard = lax.axis_index("dp") * lax.axis_size("seq") + place
    share = features // shards
    gain_one_out = lax.dynamic_slice_in_dim(gain_one_sum, shard * share, share)
    gain_two_out = lax.dynamic_slice_in_dim(gain_two_sum, shard * share, share)
    small = rank // shards
    low_parts = jnp.concatenate(
        [
            state_grad[:rank].reshape(shards, small, channels),
            step_weight_grad.reshape(shards, small, channels),
        ],
        axis=1,
    ).astype(bf16)
    low_sum = sum_scatter(low_parts, shard_bits, shard_bits).reshape(2 * small, channels)
    vectors = jnp.concatenate(
        [
            conv_taps_grad,
            conv_bias_grad[None],
            step_bias_grad[None],
            decay_grad * decay,
            skip_grad[None],
            state_grad[rank:],
        ],
        axis=0,
    ).astype(bf16)
    vectors = sum_all(vectors, shard_bits).astype(f32)
    at = width + 2
    return (
        result,
        tokens_out,
        gain_one_out,
        input_grad,
        gate_grad,
        vectors[:width].T,
        vectors[width],
        low_sum[:small].T,
        vectors[at + size + 1 :].T,
        low_sum[small:],
        vectors[width + 1],
        vectors[at : at + size].T,
        vectors[at + size],
        output_grad.T,
        gain_two_out,
        gate_ffn_grad,
        up_grad,
        down_grad.T,
    )


def solution(mesh):
    return jax.shard_map(
        per_device,
        mesh=mesh,
        in_specs=(
            P("dp", "seq", None),
            P("dp", None),
            P(),
            P(None, "chan"),
            P(None, "chan"),
            P("chan", None),
            P("chan"),
            P("chan", None),
            P(None, "chan"),
            P("chan"),
            P("chan", None),
            P("chan"),
            P("chan", None),
            P(),
            P(None, "chan"),
            P(None, "chan"),
            P("chan", None),
            P("dp", "seq", None),
        ),
        out_specs=(
            P("dp", "seq", None),
            P("dp", "seq", None),
            P(("dp", "seq")),
            P(("dp", "seq"), "chan"),
            P(("dp", "seq"), "chan"),
            P("chan", None),
            P("chan"),
            P("chan", ("dp", "seq")),
            P("chan", None),
            P(("dp", "seq"), "chan"),
            P("chan"),
            P("chan", None),
            P("chan"),
            P("chan", ("dp", "seq")),
            P(("dp", "seq")),
            P(("dp", "seq"), "chan"),
            P(("dp", "seq"), "chan"),
            P("chan", ("dp", "seq")),
        ),
        check_vma=False,
    )
```

time: 1810 us -> 749 us (0.41); the launches traced: 1780 us -> 742 us
  waiting for transfers between devices: 732 us -> 258 us
  local copies, waits for them, and re-layouts: 470 us -> 45.6 us
  other arithmetic: 358 us -> 44 us
  Pallas kernels: 0 us -> 174 us
  starting transfers between devices: 34.9 us -> 90 us
  blocking collectives: 43.6 us -> 0 us
    reduce_scatter x6 -> x0, waiting for transfers between devices: 400 us -> none  [the longest x1 75.4 us: per_device(): lax.psum_scatter(gate_ffn_grad.astype(jnp.bfloat16), ('dp', 'seq'), scatt...]
    psum x4 -> x0, waiting for transfers between devices: 330 us -> none  [the longest x1 118 us: per_device(): hidden_one = rows + lax.psum(matmul(gated, output_proj), 'chan')]
    pad x40 -> x0, local copies, waits for them, and re-layouts: 266 us -> none  [the longest x20 152 us: per_device(): lax.associative_scan(combine_pair, (local_product, local_end), axis=0)]
    ppermute x8 -> x70, waiting for transfers between devices: 2.65 us -> 258 us  [the longest x62 255 us: swap(): lax.ppermute(value, axis, [(i, i ^ mask) for i in range(lax.axis_size(axi...]
    pallas_call x0 -> x4, Pallas kernels: none -> 174 us  [the longest x1 80.2 us: per_device(): scan_backward(effective, drive, grad_scanned, projected, decay_two, heads...]
    reduce_sum x16 -> x2, other arithmetic: 151 us -> 6.11 us  [unit_of(): jnp.mean(values * values, axis=-1, keepdims=True) + epsilon]
    unnamed x804 -> x185, local copies, waits for them, and re-layouts: 103 us -> 10.4 us
    add x34 -> x9, other arithmetic: 77.3 us -> 7.15 us  [the longest x5 3.76 us: sum_scatter(): total = keep.astype(f32) + swap(away, axis, mask).astype(f32)]
  transfers between devices with their start and end apart: 23 -> 70, of which waited for: 12 -> 29; matrix products, arithmetic and copies ran while one was open for 12% -> 22% of each run, Pallas kernels for 0% -> 14%
where the time goes in v1:
time: 749 us; the launch traced here: 742 us
  waiting for transfers between devices  258 us (34%)
  Pallas kernels  174 us (23%)
  matrix products  127 us (17%)
  starting transfers between devices  90 us (12%)
  local copies, waits for them, and re-layouts  45.6 us (6%)
  other arithmetic  44 us (6%)
    ppermute x62, waiting for transfers between devices, swap(): lax.ppermute(value, axis, [(i, i ^ mask) for i in range(lax.axis_size(axi...  255 us
    pallas_call x1, Pallas kernels, per_device(): scan_backward(effective, drive, grad_scanned, projected, decay_two, heads...  80.2 us
    ppermute x62, starting transfers between devices, swap(): lax.ppermute(value, axis, [(i, i ^ mask) for i in range(lax.axis_size(axi...  69.1 us
    dot_general x16, matrix products, matmul(): return jnp.dot(left, right, preferred_element_type=f32)  60.3 us
    pallas_call x1, Pallas kernels, per_device(): scan_forward(effective, drive, projected, decay_two, ends, sums, arriving)  44.9 us
    dot_general x17, matrix products, transposed_right(): lax.dot_general(left, right, (((1,), (1,)), ((), ())), preferred_element_...  38.2 us
    dot_general x8, matrix products, transposed_left(): lax.dot_general(left, right, (((0,), (0,)), ((), ())), preferred_element_...  28.3 us
    pallas_call x1, Pallas kernels, per_device(): scan_heads(effective, grad_scanned, projected, decay_two, sums)  24.9 us
  transfers between devices with their start and end apart: 70, of which 29 were waited for; matrix products, arithmetic and copies ran while one was open for 22% of the time, Pallas kernels for 14%

profile of v1, /device:TPU:0, one launch (start us, length us, event | category | flops | bytes accessed | tf_op | source)
XLA Modules:
  0.0 741.7 jit_solution(7141738663989475716)
XLA Ops:
  4.6 6.3 convolution_convert_fusion.14
  12.1 4.9 collective-permute-start
  18.5 7.3 multiply_convert_fusion.3
  30.2 6.8 collective-permute-done.2
  41.9 24.5 %scan_ends.1 = (f32[16,8,768]{2,1,0:T(8,128)S(1)}, f32[8,768]{1,0:T(8,128)S(1)}, f32[16,768]{1,0:T(8,128)S(1)}, f32[16,768]{1,0:T(8,128)S(1)}) custom-call(f32[1024,768]{1,0:T(8,128)} %get-tuple-element.82.reff, f32[1024,768]{1,0:T(8,128)} %get-tuple-element.81.drive, f32[1024,128]{1,0:T(8,128)S(1)} %convert_add_fusion.21.proj, ...), custom_call_target="tpu_custom_call" | custom-call | flops 50331648 | bytes 20000000 | tf_op jit(solution)/shard_map/scan_ends/pallas_call | solution.py:486
  83.0 44.9 %scan_forward.1 = (f32[1024,768]{1,0:T(8,128)}, bf16[16,1040,768]{2,1,0:T(8,128)(2,1)}) custom-call(f32[1024,768]{1,0:T(8,128)} %get-tuple-element.82.reff, f32[1024,768]{1,0:T(8,128)} %get-tuple-element.81.drive, f32[1024,128]{1,0:T(8,128)S(1)} %copy-done.3, f32[16,768]{1,0:T(8,128)S(1)} %bitcast_multiply_fusion.1.dec, f32[16,8,768]{2,1,0:T(8,128)S(1)} %copy-done.8, ...), custom_call_target="tpu_custom_call" | custom-call | flops 75497472 | bytes 20000000 | tf_op jit(solution)/shard_map/scan_forward/pallas_call | solution.py:488
  127.9 9.4 %multiply_convert_fusion.2 = (bf16[1024,768]{1,0:T(8,128)(2,1)S(1)}, f32[1024,768]{1,0:T(8,128)}) fusion(f32[1024,768]{1,0:T(8,128)} %get-tuple-element.34, bf16[1024,768]{1,0:T(8,128)(2,1)S(1)} %copy-done.10, f32[768]{0:T(1024)S(1)} %convert_element_type.759, bf16[1536,768]{1,0:T(8,128)(2,1)S(1)} %copy-done.13, f32[1536]{0:T(1024)S(1)} %convert_element_type.743, ...), kind=kOutput, calls=%fused_computation.64 | convolution fusion | flops 2429288448 | bytes 14955520 | tf_op jit(solution)/shard_map/dot_general | solution.py:27
  147.5 5.4 copy.143
  183.4 12.8 %multiply_convert_fusion.6 = (bf16[512,1024]{1,0:T(8,128)(2,1)S(1)}, bf16[512,1024]{1,0:T(8,128)(2,1)S(1)}, bf16[512,1024]{1,0:T(8,128)(2,1)S(1)}) fusion(f32[512,1024]{1,0:T(8,128)S(1)} %copy-done.81, f32[512,1024]{1,0:T(8,128)S(1)} %fusion.82, bf16[1536,1024]{1,0:T(8,128)(2,1)S(1)} %copy-done, bf16[256,1536]{1,0:T(8,128)(2,1)} %collective-permute-done.9, ...), kind=kOutput, calls=%fused_computation.119 | convolution fusion | flops 1621622784 | bytes 12058624 | tf_op jit(solution)/shard_map/dot_general | solution.py:27
  219.4 4.9 convolution_convert_fusion.1
  231.7 4.9 convolution_convert_fusion.2
  239.6 10.2 %collective-permute-done.14 = bf16[256,1536]{1,0:T(8,128)(2,1)S(1)} collective-permute-done((bf16[256,1536]{1,0:T(8,128)(2,1)S(1)}, bf16[256,1536]{1,0:T(8,128)(2,1)S(1)}, u32[]{:S(2)}, u32[]{:S(2)}) %collective-permute-start.14) | collective-permute-done | bytes 786464 | tf_op jit(solution)/shard_map/ppermute | solution.py:39
  249.8 15.9 %collective-permute-done.20 = bf16[256,1536]{1,0:T(8,128)(2,1)S(1)} collective-permute-done((bf16[256,1536]{1,0:T(8,128)(2,1)S(1)}, bf16[256,1536]{1,0:T(8,128)(2,1)S(1)}, u32[]{:S(2)}, u32[]{:S(2)}) %collective-permute-start.20) | collective-permute-done | bytes 786464 | tf_op jit(solution)/shard_map/ppermute | solution.py:39
  275.9 20.4 %collective-permute-done.64 = bf16[2,2,192,1024]{3,2,0,1:T(8,128)(2,1)S(1)} collective-permute-done((bf16[2,2,192,1024]{3,2,0,1:T(8,128)(2,1)S(1)}, bf16[2,2,192,1024]{3,2,0,1:T(8,128)(2,1)S(1)}, u32[]{:S(2)}, u32[]{:S(2)}) %collective-permute-start.64) | collective-permute-done | bytes 1572896 | tf_op jit(solution)/shard_map/ppermute | solution.py:39
  301.4 28.0 %collective-permute-done.58 = bf16[1536]{0:T(1024)(128)(2,1)S(1)} collective-permute-done((bf16[1536]{0:T(1024)(128)(2,1)S(1)}, bf16[1536]{0:T(1024)(128)(2,1)S(1)}, u32[]{:S(2)}, u32[]{:S(2)}) %collective-permute-start.58) | collective-permute-done | bytes 3104 | tf_op jit(solution)/shard_map/ppermute | solution.py:39
  335.7 12.4 %collective-permute-done.59 = bf16[1536]{0:T(1024)(128)(2,1)S(1)} collective-permute-done((bf16[1536]{0:T(1024)(128)(2,1)S(1)}, bf16[1536]{0:T(1024)(128)(2,1)S(1)}, u32[]{:S(2)}, u32[]{:S(2)}) %collective-permute-start.59) | collective-permute-done | bytes 3104 | tf_op jit(solution)/shard_map/ppermute | solution.py:39
  359.0 24.8 %collective-permute-done.62 = bf16[2,192,1024]{2,1,0:T(8,128)(2,1)S(1)} collective-permute-done((bf16[2,192,1024]{2,1,0:T(8,128)(2,1)S(1)}, bf16[2,192,1024]{2,1,0:T(8,128)(2,1)S(1)}, u32[]{:S(2)}, u32[]{:S(2)}) %collective-permute-start.62) | collective-permute-done | bytes 786464 | tf_op jit(solution)/shard_map/ppermute | solution.py:39
  391.1 20.2 %collective-permute-done.66 = bf16[192,1024]{1,0:T(8,128)(2,1)S(1)} collective-permute-done((bf16[192,1024]{1,0:T(8,128)(2,1)S(1)}, bf16[192,1024]{1,0:T(8,128)(2,1)S(1)}, u32[]{:S(2)}, u32[]{:S(2)}) %collective-permute-start.66) | collective-permute-done | bytes 393248 | tf_op jit(solution)/shard_map/ppermute | solution.py:39
  412.3 7.3 collective-permute-done.63
  420.7 5.5 fusion.17
  426.3 24.9 %scan_heads.1 = (f32[16,8,768]{2,1,0:T(8,128)S(1)}, f32[16,768]{1,0:T(8,128)S(1)}) custom-call(f32[1024,768]{1,0:T(8,128)} %get-tuple-element.82.reff, f32[1024,768]{1,0:T(8,128)} %get-tuple-element.59.slope, f32[1024,128]{1,0:T(8,128)S(1)} %copy-done.4, f32[16,768]{1,0:T(8,128)S(1)} %bitcast_multiply_fusion.1.dec, f32[8,768]{1,0:T(8,128)S(1)} %get-tuple-element.31.sums), custom_call_target="tpu_custom_call" | custom-call | flops 50331648 | bytes 20000000 | tf_op jit(solution)/shard_map/scan_heads/pallas_call | solution.py:566
  455.1 5.8 convolution_convert_fusion.4
  465.0 80.2 %scan_backward.1 = (f32[1024,768]{1,0:T(8,128)}, f32[1024,768]{1,0:T(8,128)}, f32[1024,128]{1,0:T(8,128)S(1)}, f32[16,768]{1,0:T(8,128)S(1)}) custom-call(f32[1024,768]{1,0:T(8,128)} %get-tuple-element.82.reff, f32[1024,768]{1,0:T(8,128)} %get-tuple-element.81.drive, f32[1024,768]{1,0:T(8,128)} %get-tuple-element.59.slope, f32[1024,128]{1,0:T(8,128)S(1)} %copy-done.4, ...), custom_call_target="tpu_custom_call" | custom-call | flops 201326592 | bytes 20000000 | tf_op jit(solution)/shard_map/scan_backward/pallas_call | solution.py:575
  557.4 6.4 collective-permute-done.28
  563.9 10.3 %fusion.12 = (bf16[768]{0:T(1024)(128)(2,1)S(1)}, bf16[768]{0:T(1024)(128)(2,1)S(1)}, bf16[768]{0:T(1024)(128)(2,1)S(1)}, bf16[768]{0:T(1024)(128)(2,1)S(1)}, bf...) fusion(bf16[1024,768]{1,0:T(8,128)(2,1)} %copy-done.38, ...), kind=kOutput, calls=%fused_computation.36 | convolution fusion | flops 241955072 | bytes 27534848 | tf_op jit(solution)/shard_map/dot_general | solution.py:35
  608.6 5.9 collective-permute-done.51
  625.8 31.8 %collective-permute-done.45 = bf16[2,192,768]{2,1,0:T(8,128)(2,1)S(1)} collective-permute-done((bf16[2,192,768]{2,1,0:T(8,128)(2,1)S(1)}, bf16[2,192,768]{2,1,0:T(8,128)(2,1)S(1)}, u32[]{:S(2)}, u32[]{:S(2)}) %collective-permute-start.45) | collective-permute-done | bytes 589856 | tf_op jit(solution)/shard_map/ppermute | solution.py:39
  657.8 4.9 collective-permute-start.46
  665.1 9.0 %collective-permute-done.46 = bf16[192,768]{1,0:T(8,128)(2,1)S(1)} collective-permute-done((bf16[192,768]{1,0:T(8,128)(2,1)S(1)}, bf16[192,768]{1,0:T(8,128)(2,1)S(1)}, u32[]{:S(2)}, u32[]{:S(2)}) %collective-permute-start.46) | collective-permute-done | bytes 294944 | tf_op jit(solution)/shard_map/ppermute | solution.py:39
  693.3 8.4 %collective-permute-done.39 = bf16[1536]{0:T(1024)(128)(2,1)S(1)} collective-permute-done((bf16[1536]{0:T(1024)(128)(2,1)S(1)}, bf16[1536]{0:T(1024)(128)(2,1)S(1)}, u32[]{:S(2)}, u32[]{:S(2)}) %collective-permute-start.39) | collective-permute-done | bytes 3104 | tf_op jit(solution)/shard_map/ppermute | solution.py:39
  710.0 17.3 %collective-permute-done.55 = bf16[192,768]{1,0:T(8,128)(2,1)S(1)} collective-permute-done((bf16[192,768]{1,0:T(8,128)(2,1)S(1)}, bf16[192,768]{1,0:T(8,128)(2,1)S(1)}, u32[]{:S(2)}, u32[]{:S(2)}) %collective-permute-start.55) | collective-permute-done | bytes 294944 | tf_op jit(solution)/shard_map/ppermute | solution.py:39
  728.2 5.4 collective-permute-done.43
  (486 shorter events, 251.5 us)
Async XLA Ops:
  177.9 22.4 %collective-permute-start.11 = (bf16[256,1536]{1,0:T(8,128)(2,1)}, bf16[256,1536]{1,0:T(8,128)(2,1)S(1)}, u32[]{:S(2)}, u32[]{:S(2)}) collective-permute-start(bf16[256,1536]{1,0:T(8,128)(2,1)} %multiply_convert_fusion.10), channel_id=1, source_target_pairs={{0,2},{1,3},{2,0},{3,1},{4,6},{5,7},{6,4},{7,5},{8,10},{9,11},{10,... | collective-permute-start | bytes 2359304 | tf_op jit(solution)/shard_map/ppermute | solution.py:39
  200.0 37.5 %collective-permute-start.18 = (bf16[256,1536]{1,0:T(8,128)(2,1)S(1)}, bf16[256,1536]{1,0:T(8,128)(2,1)S(1)}, u32[]{:S(2)}, u32[]{:S(2)}) collective-permute-start(bf16[256,1536]{1,0:T(8,128)(2,1)S(1)} %slice.238), channel_id=1, source_target_pairs={{0,1},{1,0},{2,3},{3,2},{4,5},{5,4},{6,7},{7,6},{8,9},{9,8},{10,11... | collective-permute-start | bytes 2359304 | tf_op jit(solution)/shard_map/ppermute | solution.py:39
  202.5 36.1 %collective-permute-start.10 = (bf16[256,1536]{1,0:T(8,128)(2,1)}, bf16[256,1536]{1,0:T(8,128)(2,1)S(1)}, u32[]{:S(2)}, u32[]{:S(2)}) collective-permute-start(bf16[256,1536]{1,0:T(8,128)(2,1)} %convolution_convert_fusion.12), channel_id=1, source_target_pairs={{0,1},{1,0},{2,3},{3,2},{4,5},{5,4},{6,7},{7,6},{8,9},{9,8},{10,11... | collective-permute-start | bytes 2359304 | tf_op jit(solution)/shard_map/ppermute | solution.py:39
  225.3 47.3 %collective-permute-start.67 = (bf16[2,2,192,1024]{3,2,0,1:T(8,128)(2,1)S(1)}, bf16[2,2,192,1024]{3,2,0,1:T(8,128)(2,1)S(1)}, u32[]{:S(2)}, u32[]{:S(2)}) collective-permute-start(bf16[2,2,192,1024]{3,2,0,1:T(8,128)(2,1)S(1)} %bitcast.300), channel_id=1, source_target_pairs={{0,16},{16,0},{1,17},{17,1},{2,18},{18,2},{3,19},{19,3},{4,20},{20... | collective-permute-start | bytes 4718600 | tf_op jit(solution)/shard_map/ppermute | solution.py:39
  229.3 20.5 %collective-permute-start.14 = (bf16[256,1536]{1,0:T(8,128)(2,1)S(1)}, bf16[256,1536]{1,0:T(8,128)(2,1)S(1)}, u32[]{:S(2)}, u32[]{:S(2)}) collective-permute-start(bf16[256,1536]{1,0:T(8,128)(2,1)S(1)} %add_convert_fusion.3), channel_id=1, source_target_pairs={{0,2},{1,3},{2,0},{3,1},{4,6},{5,7},{6,4},{7,5},{8,10},{9,11},{10,... | collective-permute-start | bytes 2359304 | tf_op jit(solution)/shard_map/ppermute | solution.py:39
  230.1 35.6 %collective-permute-start.20 = (bf16[256,1536]{1,0:T(8,128)(2,1)S(1)}, bf16[256,1536]{1,0:T(8,128)(2,1)S(1)}, u32[]{:S(2)}, u32[]{:S(2)}) collective-permute-start(bf16[256,1536]{1,0:T(8,128)(2,1)S(1)} %add_convert_fusion.1), channel_id=1, source_target_pairs={{0,2},{1,3},{2,0},{3,1},{4,6},{5,7},{6,4},{7,5},{8,10},{9,11},{10,... | collective-permute-start | bytes 2359304 | tf_op jit(solution)/shard_map/ppermute | solution.py:39
  237.5 58.8 %collective-permute-start.64 = (bf16[2,2,192,1024]{3,2,0,1:T(8,128)(2,1)S(1)}, bf16[2,2,192,1024]{3,2,0,1:T(8,128)(2,1)S(1)}, u32[]{:S(2)}, u32[]{:S(2)}) collective-permute-start(bf16[2,2,192,1024]{3,2,0,1:T(8,128)(2,1)S(1)} %bitcast.298), channel_id=1, source_target_pairs={{0,16},{16,0},{1,17},{17,1},{2,18},{18,2},{3,19},{19,3},{4,20},{20... | collective-permute-start | bytes 4718600 | tf_op jit(solution)/shard_map/ppermute | solution.py:39
  238.6 93.0 %collective-permute-start.61 = (bf16[2,2,192,1024]{3,2,0,1:T(8,128)(2,1)S(1)}, bf16[2,2,192,1024]{3,2,0,1:T(8,128)(2,1)S(1)}, u32[]{:S(2)}, u32[]{:S(2)}) collective-permute-start(bf16[2,2,192,1024]{3,2,0,1:T(8,128)(2,1)S(1)} %bitcast.299), channel_id=1, source_target_pairs={{0,16},{16,0},{1,17},{17,1},{2,18},{18,2},{3,19},{19,3},{4,20},{20... | collective-permute-start | bytes 4718600 | tf_op jit(solution)/shard_map/ppermute | solution.py:39
  269.0 120.5 %collective-permute-start.21 = (bf16[256,1536]{1,0:T(8,128)(2,1)S(1)}, bf16[256,1536]{1,0:T(8,128)(2,1)S(1)}, u32[]{:S(2)}, u32[]{:S(2)}) collective-permute-start(bf16[256,1536]{1,0:T(8,128)(2,1)S(1)} %get-tuple-element.65), channel_id=1, source_target_pairs={{0,1},{1,0},{2,3},{3,2},{4,5},{5,4},{6,7},{7,6},{8,9},{9,8},{10,11... | collective-permute-start | bytes 2359304 | tf_op jit(solution)/shard_map/ppermute | solution.py:39
  269.0 120.5 %collective-permute-start.22 = (bf16[256,1536]{1,0:T(8,128)(2,1)S(1)}, bf16[256,1536]{1,0:T(8,128)(2,1)S(1)}, u32[]{:S(2)}, u32[]{:S(2)}) collective-permute-start(bf16[256,1536]{1,0:T(8,128)(2,1)S(1)} %get-tuple-element.65), channel_id=1, source_target_pairs={{0,2},{1,3},{2,0},{3,1},{4,6},{5,7},{6,4},{7,5},{8,10},{9,11},{10,... | collective-permute-start | bytes 2359304 | tf_op jit(solution)/shard_map/ppermute | solution.py:39
  273.7 80.7 %collective-permute-start.68 = (bf16[2,192,1024]{2,1,0:T(8,128)(2,1)S(1)}, bf16[2,192,1024]{2,1,0:T(8,128)(2,1)S(1)}, u32[]{:S(2)}, u32[]{:S(2)}) collective-permute-start(bf16[2,192,1024]{2,1,0:T(8,128)(2,1)S(1)} %dynamic-slice_bitcast_fusion.1), channel_id=1, source_target_pairs={{0,4},{4,0},{8,12},{12,8},{1,5},{5,1},{9,13},{13,9},{2,6},{6,2},{1... | collective-permute-start | bytes 2359304 | tf_op jit(solution)/shard_map/ppermute | solution.py:39
  299.9 29.5 %collective-permute-start.58 = (bf16[1536]{0:T(1024)(128)(2,1)S(1)}, bf16[1536]{0:T(1024)(128)(2,1)S(1)}, u32[]{:S(2)}, u32[]{:S(2)}) collective-permute-start(bf16[1536]{0:T(1024)(128)(2,1)S(1)} %add_convert_fusion.15), channel_id=1, source_target_pairs={{0,16},{16,0},{1,17},{17,1},{2,18},{18,2},{3,19},{19,3},{4,20},{20... | collective-permute-start | bytes 9224 | tf_op jit(solution)/shard_map/ppermute | solution.py:39
  329.4 25.8 %collective-permute-start.65 = (bf16[2,192,1024]{2,1,0:T(8,128)(2,1)S(1)}, bf16[2,192,1024]{2,1,0:T(8,128)(2,1)S(1)}, u32[]{:S(2)}, u32[]{:S(2)}) collective-permute-start(bf16[2,192,1024]{2,1,0:T(8,128)(2,1)S(1)} %dynamic-slice_bitcast_fusion.2), channel_id=1, source_target_pairs={{0,4},{4,0},{8,12},{12,8},{1,5},{5,1},{9,13},{13,9},{2,6},{6,2},{1... | collective-permute-start | bytes 2359304 | tf_op jit(solution)/shard_map/ppermute | solution.py:39
  354.5 29.6 %collective-permute-start.16 = (bf16[8,32,1536]{2,0,1:T(8,128)(2,1)S(1)}, bf16[8,32,1536]{2,0,1:T(8,128)(2,1)}, u32[]{:S(2)}, u32[]{:S(2)}) collective-permute-start(bf16[8,32,1536]{2,0,1:T(8,128)(2,1)S(1)} %get-tuple-element.99), channel_id=1, source_target_pairs={{0,2},{1,3},{2,0},{3,1},{4,6},{5,7},{6,4},{7,5},{8,10},{9,11},{10,... | collective-permute-start | bytes 2359304 | tf_op jit(solution)/shard_map/ppermute | solution.py:39
  355.3 28.4 %collective-permute-start.62 = (bf16[2,192,1024]{2,1,0:T(8,128)(2,1)S(1)}, bf16[2,192,1024]{2,1,0:T(8,128)(2,1)S(1)}, u32[]{:S(2)}, u32[]{:S(2)}) collective-permute-start(bf16[2,192,1024]{2,1,0:T(8,128)(2,1)S(1)} %dynamic-slice_bitcast_fusion.3), channel_id=1, source_target_pairs={{0,4},{4,0},{8,12},{12,8},{1,5},{5,1},{9,13},{13,9},{2,6},{6,2},{1... | collective-permute-start | bytes 2359304 | tf_op jit(solution)/shard_map/ppermute | solution.py:39
  357.8 32.4 %collective-permute-start.69 = (bf16[192,1024]{1,0:T(8,128)(2,1)S(1)}, bf16[192,1024]{1,0:T(8,128)(2,1)S(1)}, u32[]{:S(2)}, u32[]{:S(2)}) collective-permute-start(bf16[192,1024]{1,0:T(8,128)(2,1)S(1)} %dynamic-slice_bitcast_fusion.7), channel_id=1, source_target_pairs={{0,8},{4,12},{8,0},{12,4},{1,9},{5,13},{9,1},{13,5},{2,10},{6,14},... | collective-permute-start | bytes 1179656 | tf_op jit(solution)/shard_map/ppermute | solution.py:39
  383.7 27.6 %collective-permute-start.66 = (bf16[192,1024]{1,0:T(8,128)(2,1)S(1)}, bf16[192,1024]{1,0:T(8,128)(2,1)S(1)}, u32[]{:S(2)}, u32[]{:S(2)}) collective-permute-start(bf16[192,1024]{1,0:T(8,128)(2,1)S(1)} %dynamic-slice_bitcast_fusion.8), channel_id=1, source_target_pairs={{0,8},{4,12},{8,0},{12,4},{1,9},{5,13},{9,1},{13,5},{2,10},{6,14},... | collective-permute-start | bytes 1179656 | tf_op jit(solution)/shard_map/ppermute | solution.py:39
  384.1 35.5 %collective-permute-start.63 = (bf16[192,1024]{1,0:T(8,128)(2,1)S(1)}, bf16[192,1024]{1,0:T(8,128)(2,1)S(1)}, u32[]{:S(2)}, u32[]{:S(2)}) collective-permute-start(bf16[192,1024]{1,0:T(8,128)(2,1)S(1)} %dynamic-slice_bitcast_fusion.9), channel_id=1, source_target_pairs={{0,8},{4,12},{8,0},{12,4},{1,9},{5,13},{9,1},{13,5},{2,10},{6,14},... | collective-permute-start | bytes 1179656 | tf_op jit(solution)/shard_map/ppermute | solution.py:39
  389.5 163.5 %collective-permute-start.17 = (bf16[8,32,1536]{2,0,1:T(8,128)(2,1)}, bf16[8,32,1536]{2,0,1:T(8,128)(2,1)}, u32[]{:S(2)}, u32[]{:S(2)}) collective-permute-start(bf16[8,32,1536]{2,0,1:T(8,128)(2,1)} %collective-permute-done.16), channel_id=1, source_target_pairs={{0,1},{1,0},{2,3},{3,2},{4,5},{5,4},{6,7},{7,6},{8,9},{9,8},{10,11... | collective-permute-start | bytes 2359304 | tf_op jit(solution)/shard_map/ppermute | solution.py:39
  389.5 31.1 %collective-permute-start.23 = (bf16[256,1536]{1,0:T(8,128)(2,1)S(1)}, bf16[256,1536]{1,0:T(8,128)(2,1)S(1)}, u32[]{:S(2)}, u32[]{:S(2)}) collective-permute-start(bf16[256,1536]{1,0:T(8,128)(2,1)S(1)} %collective-permute-done.22), channel_id=1, source_target_pairs={{0,1},{1,0},{2,3},{3,2},{4,5},{5,4},{6,7},{7,6},{8,9},{9,8},{10,11... | collective-permute-start | bytes 2359304 | tf_op jit(solution)/shard_map/ppermute | solution.py:39
  550.9 69.7 %collective-permute-start.44 = (bf16[2,2,192,768]{3,2,1,0:T(8,128)(2,1)}, bf16[2,2,192,768]{3,2,1,0:T(8,128)(2,1)}, u32[]{:S(2)}, u32[]{:S(2)}) collective-permute-start(bf16[2,2,192,768]{3,2,1,0:T(8,128)(2,1)} %dynamic-slice_bitcast_fusion), channel_id=1, source_target_pairs={{0,4},{4,0},{8,12},{12,8},{1,5},{5,1},{9,13},{13,9},{2,6},{6,2},{1... | collective-permute-start | bytes 3538952 | tf_op jit(solution)/shard_map/ppermute | solution.py:39
  593.3 81.8 %collective-permute-start.53 = (bf16[2,2,192,768]{3,2,0,1:T(8,128)(2,1)S(1)}, bf16[2,2,192,768]{3,2,0,1:T(8,128)(2,1)S(1)}, u32[]{:S(2)}, u32[]{:S(2)}) collective-permute-start(bf16[2,2,192,768]{3,2,0,1:T(8,128)(2,1)S(1)} %bitcast.302), channel_id=1, source_target_pairs={{0,16},{16,0},{1,17},{17,1},{2,18},{18,2},{3,19},{19,3},{4,20},{20... | collective-permute-start | bytes 3538952 | tf_op jit(solution)/shard_map/ppermute | solution.py:39
  594.9 81.3 %collective-permute-start.41 = (bf16[2,2,192,768]{3,2,0,1:T(8,128)(2,1)S(1)}, bf16[2,2,192,768]{3,2,0,1:T(8,128)(2,1)S(1)}, u32[]{:S(2)}, u32[]{:S(2)}) collective-permute-start(bf16[2,2,192,768]{3,2,0,1:T(8,128)(2,1)S(1)} %bitcast.301), channel_id=1, source_target_pairs={{0,16},{16,0},{1,17},{17,1},{2,18},{18,2},{3,19},{19,3},{4,20},{20... | collective-permute-start | bytes 3538952 | tf_op jit(solution)/shard_map/ppermute | solution.py:39
  598.1 78.5 %collective-permute-start.30 = (bf16[256,1536]{1,0:T(8,128)(2,1)S(1)}, bf16[256,1536]{1,0:T(8,128)(2,1)S(1)}, u32[]{:S(2)}, u32[]{:S(2)}) collective-permute-start(bf16[256,1536]{1,0:T(8,128)(2,1)S(1)} %fusion.38), channel_id=1, source_target_pairs={{0,1},{1,0},{2,3},{3,2},{4,5},{5,4},{6,7},{7,6},{8,9},{9,8},{10,11... | collective-permute-start | bytes 2359304 | tf_op jit(solution)/shard_map/ppermute | solution.py:39
  622.4 35.3 %collective-permute-start.45 = (bf16[2,192,768]{2,1,0:T(8,128)(2,1)S(1)}, bf16[2,192,768]{2,1,0:T(8,128)(2,1)S(1)}, u32[]{:S(2)}, u32[]{:S(2)}) collective-permute-start(bf16[2,192,768]{2,1,0:T(8,128)(2,1)S(1)} %dynamic-slice_bitcast_fusion.5), channel_id=1, source_target_pairs={{0,16},{16,0},{1,17},{17,1},{2,18},{18,2},{3,19},{19,3},{4,20},{20... | collective-permute-start | bytes 1769480 | tf_op jit(solution)/shard_map/ppermute | solution.py:39
  625.2 37.5 %collective-permute-start.31 = (bf16[256,1536]{1,0:T(8,128)(2,1)S(1)}, bf16[256,1536]{1,0:T(8,128)(2,1)S(1)}, u32[]{:S(2)}, u32[]{:S(2)}) collective-permute-start(bf16[256,1536]{1,0:T(8,128)(2,1)S(1)} %fusion.41), channel_id=1, source_target_pairs={{0,1},{1,0},{2,3},{3,2},{4,5},{5,4},{6,7},{7,6},{8,9},{9,8},{10,11... | collective-permute-start | bytes 2359304 | tf_op jit(solution)/shard_map/ppermute | solution.py:39
  675.5 30.4 %collective-permute-start.54 = (bf16[2,192,768]{2,1,0:T(8,128)(2,1)S(1)}, bf16[2,192,768]{2,1,0:T(8,128)(2,1)S(1)}, u32[]{:S(2)}, u32[]{:S(2)}) collective-permute-start(bf16[2,192,768]{2,1,0:T(8,128)(2,1)S(1)} %dynamic-slice_bitcast_fusion.4), channel_id=1, source_target_pairs={{0,4},{4,0},{8,12},{12,8},{1,5},{5,1},{9,13},{13,9},{2,6},{6,2},{1... | collective-permute-start | bytes 1769480 | tf_op jit(solution)/shard_map/ppermute | solution.py:39
  682.2 24.0 %collective-permute-start.42 = (bf16[2,192,768]{2,1,0:T(8,128)(2,1)S(1)}, bf16[2,192,768]{2,1,0:T(8,128)(2,1)S(1)}, u32[]{:S(2)}, u32[]{:S(2)}) collective-permute-start(bf16[2,192,768]{2,1,0:T(8,128)(2,1)S(1)} %dynamic-slice_bitcast_fusion.6), channel_id=1, source_target_pairs={{0,4},{4,0},{8,12},{12,8},{1,5},{5,1},{9,13},{13,9},{2,6},{6,2},{1... | collective-permute-start | bytes 1769480 | tf_op jit(solution)/shard_map/ppermute | solution.py:39
  689.5 44.9 %collective-permute-start.33 = (bf16[8,32,1536]{2,0,1:T(8,128)(2,1)S(1)}, bf16[8,32,1536]{2,0,1:T(8,128)(2,1)S(1)}, u32[]{:S(2)}, u32[]{:S(2)}) collective-permute-start(bf16[8,32,1536]{2,0,1:T(8,128)(2,1)S(1)} %get-tuple-element.63), channel_id=1, source_target_pairs={{0,1},{1,0},{2,3},{3,2},{4,5},{5,4},{6,7},{7,6},{8,9},{9,8},{10,11... | collective-permute-start | bytes 2359304 | tf_op jit(solution)/shard_map/ppermute | solution.py:39
  689.6 45.1 %collective-permute-start.34 = (bf16[8,32,1536]{2,0,1:T(8,128)(2,1)S(1)}, bf16[8,32,1536]{2,0,1:T(8,128)(2,1)S(1)}, u32[]{:S(2)}, u32[]{:S(2)}) collective-permute-start(bf16[8,32,1536]{2,0,1:T(8,128)(2,1)S(1)} %get-tuple-element.63), channel_id=1, source_target_pairs={{0,2},{1,3},{2,0},{3,1},{4,6},{5,7},{6,4},{7,5},{8,10},{9,11},{10,... | collective-permute-start | bytes 2359304 | tf_op jit(solution)/shard_map/ppermute | solution.py:39
  706.1 21.2 %collective-permute-start.55 = (bf16[192,768]{1,0:T(8,128)(2,1)S(1)}, bf16[192,768]{1,0:T(8,128)(2,1)S(1)}, u32[]{:S(2)}, u32[]{:S(2)}) collective-permute-start(bf16[192,768]{1,0:T(8,128)(2,1)S(1)} %dynamic-slice_bitcast_fusion.10), channel_id=1, source_target_pairs={{0,8},{4,12},{8,0},{12,4},{1,9},{5,13},{9,1},{13,5},{2,10},{6,14},... | collective-permute-start | bytes 884744 | tf_op jit(solution)/shard_map/ppermute | solution.py:39
  706.4 27.2 %collective-permute-start.43 = (bf16[192,768]{1,0:T(8,128)(2,1)S(1)}, bf16[192,768]{1,0:T(8,128)(2,1)S(1)}, u32[]{:S(2)}, u32[]{:S(2)}) collective-permute-start(bf16[192,768]{1,0:T(8,128)(2,1)S(1)} %dynamic-slice_bitcast_fusion.12), channel_id=1, source_target_pairs={{0,8},{4,12},{8,0},{12,4},{1,9},{5,13},{9,1},{13,5},{2,10},{6,14},... | collective-permute-start | bytes 884744 | tf_op jit(solution)/shard_map/ppermute | solution.py:39
  (129 other events, 1589.2 us)

commit v2 on v1

v2 whole, which is shorter than its diff:
```python
import functools

import jax
import jax.numpy as jnp
from jax import lax
from jax.experimental import pallas as pl
from jax.experimental.pallas import tpu as pltpu
from jax.sharding import PartitionSpec as P

epsilon = 1e-05
pieces = 8
lanes = 128
far = 1e6
log2e = 1.4426950408889634
ln2 = 0.6931471805599453
vmem_bytes = 58 * 1024 * 1024
bf16 = jnp.bfloat16
f32 = jnp.float32


def silu_slope(values):
    sigma = jax.nn.sigmoid(values)
    return sigma * (1.0 + values * (1.0 - sigma))


def matmul(left, right):
    return jnp.dot(left, right, preferred_element_type=f32)


def transposed_left(left, right):
    return lax.dot_general(left, right, (((0,), (0,)), ((), ())), preferred_element_type=f32)


def transposed_right(left, right):
    return lax.dot_general(left, right, (((1,), (1,)), ((), ())), preferred_element_type=f32)


def swap(value, axis, mask):
    return lax.ppermute(value, axis, [(i, i ^ mask) for i in range(lax.axis_size(axis))])


def shifted(value, axis, by):
    size = lax.axis_size(axis)
    return lax.ppermute(value, axis, [(i, i + by) for i in range(size) if 0 <= i + by < size])


def bits_of(axis):
    return [1 << k for k in reversed(range(lax.axis_size(axis).bit_length() - 1))]


def bit_is_set(axis, mask):
    return ((lax.axis_index(axis) & mask) != 0).astype(jnp.int32)


def after(value, *others):
    if not others:
        return value
    return lax.optimization_barrier((value, others))[0]


def sum_all(value, axes):
    for axis, mask in axes:
        value = (value.astype(f32) + swap(value, axis, mask).astype(f32)).astype(bf16)
    return value


class Scatter:
    def __init__(self, value, order, whole):
        value = value.astype(bf16)
        self.terms = [value.reshape((2,) * len(whole) + (-1,) + value.shape[1:])]
        self.order = list(order)
        self.left = list(whole)

    def send(self, *others):
        axis, mask = self.order.pop(0)
        at = self.left.index((axis, mask))
        self.left.pop(at)
        mine = bit_is_set(axis, mask)
        if others:
            self.terms[-1] = after(self.terms[-1], *others)
        away = [lax.dynamic_index_in_dim(t, 1 - mine, at, keepdims=False) for t in self.terms]
        away = sum(t.astype(f32) for t in away).astype(bf16)
        self.terms = [
            lax.dynamic_index_in_dim(t, mine, at, keepdims=False) for t in self.terms
        ]
        self.terms.append(swap(away, axis, mask))
        return away

    def total(self, *others):
        while self.order:
            self.send(*others)
        if others:
            self.terms[-1] = after(self.terms[-1], *others)
        return sum(t.astype(f32) for t in self.terms)


def chan_scatter(part, fill=lambda begun: ()):
    third = swap(part(3), "chan", 1)
    middle = (part(2).astype(f32) + third.astype(f32)).astype(bf16)
    second = swap(middle, "chan", 2)
    first = swap(part(1), "chan", 1)
    own = part(0)
    second = after(second, own, *fill(middle))
    return own.astype(f32) + first.astype(f32) + second.astype(f32)


def chan_gather(own, fill=lambda begun: ()):
    across = swap(own, "chan", 2)
    beside = swap(own, "chan", 1)
    across = after(across, *fill(beside))
    return [own, beside, across, swap(across, "chan", 1)]


def in_order(own, beside):
    upper = bit_is_set("chan", 1) == 1
    return jnp.concatenate(
        [jnp.where(upper, beside, own), jnp.where(upper, own, beside)], axis=0
    )


def chan_total(value, near=lambda: (), distant=lambda begun: ()):
    got = swap(value, "chan", 1)
    value = (value + after(got, *near())).astype(bf16)
    got = swap(value, "chan", 2)
    got = after(got, *distant(value))
    return value.astype(f32) + got.astype(f32)


def step_rows(step, steps):
    return pl.ds(step, pieces, stride=steps)


def split_proj(proj, both, steps):
    def body(i, unused):
        tile = jnp.concatenate(
            [proj[step_rows(2 * i, steps), :], proj[step_rows(2 * i + 1, steps), :]], axis=0
        )
        high = tile.astype(bf16)
        rows = pl.ds(pl.multiple_of(i * 2 * pieces, 2 * pieces), 2 * pieces)
        both[rows, :lanes] = high
        both[rows, lanes:] = (tile - high.astype(f32)).astype(bf16)
        return unused

    lax.fori_loop(0, steps // 2, body, 0)


def spread(both, out, first, count):
    tall = min(256, both.shape[0])
    source = lax.broadcasted_iota(jnp.int32, (2 * lanes, 2 * lanes), 0) % lanes
    target = lax.broadcasted_iota(jnp.int32, (2 * lanes, 2 * lanes), 1) // lanes
    for n in range(0, count, 2):
        pick = (source == target + (first + n)).astype(f32).astype(bf16)
        for k in range(both.shape[0] // tall):
            rows = pl.ds(k * tall, tall)
            wide = jnp.dot(both[rows, :], pick, preferred_element_type=f32)
            out[n, rows, :] = wide[:, :lanes]
            if n + 1 < count:
                out[n + 1, rows, :] = wide[:, lanes:]


def decay_rows(dec, count):
    return [jnp.broadcast_to(dec[n : n + 1, :], (pieces, lanes)) for n in range(count)]


def ends_kernel(size, rank, rates, mixed, proj, dec, ends, sums, end_total, product_total, *scratch):
    both, eb, fb = scratch
    steps = rates.shape[0] // pieces

    @pl.when(pl.program_id(0) == 0)
    def _():
        split_proj(proj, both, steps)
        spread(both, eb, rank, size)
        spread(both, fb, 0, 1)

    decays = decay_rows(dec, size)

    def body(i, carry):
        states, total = carry
        rows = pl.ds(pl.multiple_of(i * pieces, pieces), pieces)
        rate = rates[step_rows(i, steps), :]
        push = rate * mixed[step_rows(i, steps), :]
        rate = rate + fb[0, rows, :]
        out = []
        for n in range(size):
            out.append(jnp.exp2(rate * decays[n]) * states[n] + push * eb[n, rows, :])
        return tuple(out), total + rate

    zero = jnp.zeros((pieces, lanes), f32)
    states, total = lax.fori_loop(0, steps, body, ((zero,) * size, zero), unroll=4)
    for n in range(size):
        ends[n] = states[n]
    sums[...] = total
    reached = ends[:, 0, :]
    for s in range(1, pieces):
        reached = ends[:, s, :] + jnp.exp2(dec[...] * sums[s : s + 1, :]) * reached
    end_total[...] = reached
    product_total[...] = jnp.exp2(dec[...] * jnp.sum(total, axis=0, keepdims=True))


def forward_kernel(
    size, rank, rates, mixed, proj, dec, ends, sums, arriving, gate_in, skip, *rest
):
    gated, summed, before, both, eb, rb, fb, start, scanned = rest
    steps = rates.shape[0] // pieces

    @pl.when(pl.program_id(0) == 0)
    def _():
        split_proj(proj, both, steps)
        spread(both, eb, rank, size)
        spread(both, rb, rank + size, size)
        spread(both, fb, 0, 1)

    decays = decay_rows(dec, size)
    reached = arriving[...]
    for s in range(pieces):
        start[:, s, :] = reached
        reached = ends[:, s, :] + jnp.exp2(dec[...] * sums[s : s + 1, :]) * reached

    def body(i, states):
        rows = pl.ds(pl.multiple_of(i * 2 * pieces, 2 * pieces), 2 * pieces)
        first, second = step_rows(2 * i, steps), step_rows(2 * i + 1, steps)
        rate0, rate1 = rates[first, :], rates[second, :]
        push0, push1 = rate0 * mixed[first, :], rate1 * mixed[second, :]
        apart = fb[0, rows, :]
        rate0, rate1 = rate0 + apart[:pieces], rate1 + apart[pieces:]
        low = jnp.zeros((pieces, lanes), f32)
        high = low
        out = []
        for n in range(size):
            entry = eb[n, rows, :]
            readout = rb[n, rows, :]
            at_zero = states[n]
            at_one = jnp.exp2(rate0 * decays[n]) * at_zero + push0 * entry[:pieces]
            at_two = jnp.exp2(rate1 * decays[n]) * at_one + push1 * entry[pieces:]
            low = low + readout[:pieces] * at_one
            high = high + readout[pieces:] * at_two
            before[n, rows, :] = jnp.concatenate([at_zero, at_one], axis=0).astype(bf16)
            out.append(at_two)
        scanned[first, :] = low
        scanned[second, :] = high
        return tuple(out)

    states = lax.fori_loop(0, steps // 2, body, tuple(start[n] for n in range(size)))
    for n in range(size):
        last = jnp.concatenate([states[n], states[n]], axis=0).astype(bf16)
        before[n, pl.ds(steps * pieces, 2 * pieces), :] = last

    def finish(i, unused):
        rows = pl.ds(pl.multiple_of(i * 64, 64), 64)
        total = scanned[rows, :] + skip[...] * mixed[rows, :]
        gate = gate_in[rows, :]
        gated[rows, :] = (total * (gate * jax.nn.sigmoid(gate))).astype(bf16)
        summed[rows, :] = total.astype(bf16)
        return unused

    lax.fori_loop(0, steps * pieces // 64, finish, 0)


def heads_kernel(size, rank, rates, slope, proj, dec, sums, heads, head_total, *scratch):
    both, rb, fb = scratch
    steps = rates.shape[0] // pieces

    @pl.when(pl.program_id(0) == 0)
    def _():
        split_proj(proj, both, steps)
        spread(both, rb, rank + size, size)
        spread(both, fb, 0, 1)

    decays = decay_rows(dec, size)

    def body(i, carried):
        step = steps - 1 - i
        rows = pl.ds(pl.multiple_of(step * pieces, pieces), pieces)
        rate = rates[step_rows(step, steps), :] + fb[0, rows, :]
        grad = slope[step_rows(step, steps), :]
        return tuple(
            (carried[n] + rb[n, rows, :] * grad) * jnp.exp2(rate * decays[n]) for n in range(size)
        )

    zero = jnp.zeros((pieces, lanes), f32)
    carried = lax.fori_loop(0, steps, body, (zero,) * size, unroll=4)
    for n in range(size):
        heads[n] = carried[n]
    reached = heads[:, pieces - 1, :]
    for s in reversed(range(pieces - 1)):
        reached = heads[:, s, :] + jnp.exp2(dec[...] * sums[s : s + 1, :]) * reached
    head_total[...] = reached


def backward_kernel(
    size,
    rank,
    rates,
    mixed,
    slope,
    proj,
    dec,
    heads,
    sums,
    leaving,
    before,
    skip,
    step_proj,
    *rest,
):
    pre_low, direct, proj_grad, decay_grad, bias_grad = rest[:5]
    both, eb, rb, fb, stop, decay_sum, entry_terms, readout_terms = rest[5:13]
    picks, rate_grad, drive_grad, terms_grad = rest[13:]
    steps = rates.shape[0] // pieces
    count = steps * pieces
    pair = 2 * pieces
    group = pl.program_id(0)

    @pl.when(group == 0)
    def _():
        split_proj(proj, both, steps)
        spread(both, eb, rank, size)
        spread(both, rb, rank + size, size)
        spread(both, fb, 0, 1)
        proj_grad[...] = jnp.zeros_like(proj_grad)
        target = lax.broadcasted_iota(jnp.int32, (lanes, lanes), 1)
        for n in range(2 * size):
            picks[pl.ds(n * lanes, lanes), :] = (target == rank + n).astype(f32).astype(bf16)

    decays = decay_rows(dec, size)
    reached = leaving[...]
    for s in reversed(range(pieces)):
        stop[:, s, :] = reached
        reached = heads[:, s, :] + jnp.exp2(dec[...] * sums[s : s + 1, :]) * reached
    decay_sum[...] = jnp.zeros_like(decay_sum)

    def body(fresh, i, carried):
        half = steps // 2 - 1 - i
        at = pl.multiple_of(half * pair, pair)
        rows = pl.ds(at, pair)
        following = pl.ds(at + pair, pair)
        first, second = step_rows(2 * half, steps), step_rows(2 * half + 1, steps)
        rate0, rate1 = rates[first, :], rates[second, :]
        push0, push1 = rate0 * mixed[first, :], rate1 * mixed[second, :]
        grad0, grad1 = slope[first, :], slope[second, :]
        apart = fb[0, rows, :]
        far0, far1 = rate0 + apart[:pieces], rate1 + apart[pieces:]
        zero = jnp.zeros((pieces, lanes), f32)
        rates0 = rates1 = drives0 = drives1 = zero
        out = []
        for n in range(size):
            entry = eb[n, rows, :]
            readout = rb[n, rows, :]
            state = before[n, rows, :].astype(f32)
            later = before[n, following, :].astype(f32)[:pieces]
            held1 = carried[n] + readout[pieces:] * grad1
            passed1 = held1 * jnp.exp2(far1 * decays[n])
            scaled1 = passed1 * state[pieces:]
            held0 = passed1 + readout[:pieces] * grad0
            passed0 = held0 * jnp.exp2(far0 * decays[n])
            scaled0 = passed0 * state[:pieces]
            rates1 = rates1 + scaled1 * decays[n]
            rates0 = rates0 + scaled0 * decays[n]
            drives1 = drives1 + held1 * entry[pieces:]
            drives0 = drives0 + held0 * entry[:pieces]
            decay_sum[n] += scaled1 * rate1 + scaled0 * rate0
            here = pl.ds(n * lanes, lanes)
            entries = jnp.concatenate([held0 * push0, held1 * push1], axis=0)
            readouts = jnp.concatenate([grad0 * state[pieces:], grad1 * later], axis=0)
            entry_terms[rows, here] = entries if fresh else entry_terms[rows, here] + entries
            readout_terms[rows, here] = (
                readouts if fresh else readout_terms[rows, here] + readouts
            )
            out.append(passed0)
        rate_grad[first, :] = rates0
        rate_grad[second, :] = rates1
        drive_grad[first, :] = drives0
        drive_grad[second, :] = drives1
        return tuple(out)

    def sweep(fresh):
        edges = tuple(stop[n] for n in range(size))
        lax.fori_loop(0, steps // 2, functools.partial(body, fresh), edges)

    pl.when(group == 0)(lambda: sweep(True))
    pl.when(group > 0)(lambda: sweep(False))
    decay_grad[...] = jnp.sum(decay_sum[...], axis=1)

    tall = min(256, count)
    bias_total = jnp.zeros((1, lanes), f32)
    for k in range(count // tall):
        rows = pl.ds(k * tall, tall)
        rate, drives = rates[rows, :], drive_grad[rows, :]
        pre = (rate_grad[rows, :] * ln2 + drives * mixed[rows, :]) * (1.0 - jnp.exp(-rate))
        bias_total = bias_total + jnp.sum(pre, axis=0, keepdims=True)
        low = pre.astype(bf16)
        pre_low[rows, :] = low
        direct[rows, :] = drives * rate + skip[...] * slope[rows, :]
        proj_grad[rows, :] += lax.dot_general(
            low, step_proj[...], (((1,), (1,)), ((), ())), preferred_element_type=f32
        )
    bias_grad[...] = bias_total

    @pl.when(group == pl.num_programs(0) - 1)
    def _():
        for k in range(count // tall):
            rows = pl.ds(k * tall, tall)
            terms_grad[rows, :] = jnp.dot(
                entry_terms[rows, :].astype(bf16),
                picks[: size * lanes, :],
                preferred_element_type=f32,
            ) + jnp.dot(
                readout_terms[rows, :].astype(bf16),
                picks[size * lanes :, :],
                preferred_element_type=f32,
            )

        def finish(i, unused):
            rows = pl.ds(pl.multiple_of(i * pieces, pieces), pieces)
            proj_grad[step_rows(i, steps), :] += terms_grad[rows, :]
            return unused

        lax.fori_loop(0, steps, finish, 0)


def scan_calls(count, channels, size, rank):
    groups = channels // lanes
    tall = pl.BlockSpec((count, lanes), lambda g: (0, g))
    fixed = pl.BlockSpec((count, lanes), lambda g: (0, 0))
    small = pl.BlockSpec((size, lanes), lambda g: (0, g))
    ends = pl.BlockSpec((size, pieces, lanes), lambda g: (0, 0, g))
    sums = pl.BlockSpec((pieces, lanes), lambda g: (0, g))
    line = pl.BlockSpec((1, lanes), lambda g: (0, g))
    square = pl.BlockSpec((lanes, lanes), lambda g: (0, g))
    states = pl.BlockSpec((size, count + 2 * pieces, lanes), lambda g: (0, 0, g))
    shape = jax.ShapeDtypeStruct
    tall_out = shape((count, channels), f32)
    tall_low = shape((count, channels), bf16)
    small_out = shape((size, channels), f32)
    ends_out = shape((size, pieces, channels), f32)
    sums_out = shape((pieces, channels), f32)
    states_out = shape((size, count + 2 * pieces, channels), bf16)
    fixed_out = shape((count, lanes), f32)
    line_out = shape((1, channels), f32)
    both = pltpu.VMEM((count, 2 * lanes), bf16)
    wide = pltpu.VMEM((size, count, lanes), f32)
    thin = pltpu.VMEM((1, count, lanes), f32)
    terms = pltpu.VMEM((count, size * lanes), f32)
    edge = pltpu.VMEM((size, pieces, lanes), f32)
    own = pltpu.VMEM((count, lanes), f32)
    picks = pltpu.VMEM((2 * size * lanes, lanes), bf16)
    work = count * channels * size

    def call(kernel, name, ins, outs, out_shape, scratch, span=groups, aliases={}):
        return pl.pallas_call(
            functools.partial(kernel, size, rank),
            grid=(span,),
            in_specs=ins,
            out_specs=outs,
            out_shape=out_shape,
            scratch_shapes=scratch,
            compiler_params=pltpu.CompilerParams(
                dimension_semantics=("arbitrary",), vmem_limit_bytes=vmem_bytes
            ),
            cost_estimate=pl.CostEstimate(flops=work, bytes_accessed=0, transcendentals=0),
            input_output_aliases=aliases,
            name=name,
        )

    def backward_call(first, span):
        def moved(spec):
            return pl.BlockSpec(spec.block_shape, lambda g: spec.index_map(g + first))

        ins = [tall, tall, tall, fixed, small, ends, sums, small, states, line, square]
        outs = [tall, tall, fixed, small, line]
        kept = [0, 1, 3, 4] if first else []
        aliases = {len(ins) + i: out for i, out in enumerate(kept)}
        held = [pl.BlockSpec(memory_space=pl.ANY)] * len(kept)

        def kernel(size, rank, *refs):
            refs = refs[: len(ins)] + refs[len(ins) + len(kept) :]
            backward_kernel(size, rank, *refs)

        return call(
            kernel,
            "scan_backward",
            [moved(spec) for spec in ins] + held,
            [moved(spec) for spec in outs],
            [tall_low, tall_out, fixed_out, small_out, line_out],
            [both, wide, wide, thin, edge, edge, terms, terms, picks, own, own, own],
            span,
            aliases,
        )

    part = groups // 2
    backward_parts = (backward_call(0, part), backward_call(part, groups - part))
    return (
        call(
            ends_kernel,
            "scan_ends",
            [tall, tall, fixed, small],
            [ends, sums, small, small],
            [ends_out, sums_out, small_out, small_out],
            [both, wide, thin],
        ),
        call(
            forward_kernel,
            "scan_forward",
            [tall, tall, fixed, small, ends, sums, small, tall, line],
            [tall, tall, states],
            [tall_low, tall_low, states_out],
            [both, wide, wide, thin, edge, own],
        ),
        call(
            heads_kernel,
            "scan_heads",
            [tall, tall, fixed, small, sums],
            [ends, small],
            [ends_out, small_out],
            [both, wide, thin],
        ),
        backward_parts,
    )


def norm_kernel(rows, gain, out):
    values = rows[...].astype(f32)
    scale = lax.rsqrt(jnp.mean(values * values, axis=-1, keepdims=True) + epsilon)
    out[...] = (values * scale * gain[...]).astype(bf16)


def norm_call(count, features):
    tall = min(count, 128)
    return pl.pallas_call(
        norm_kernel,
        grid=(count // tall,),
        in_specs=[
            pl.BlockSpec((tall, features), lambda i: (i, 0)),
            pl.BlockSpec((1, features), lambda i: (0, 0)),
        ],
        out_specs=pl.BlockSpec((tall, features), lambda i: (i, 0)),
        out_shape=jax.ShapeDtypeStruct((count, features), bf16),
        cost_estimate=pl.CostEstimate(
            flops=6 * count * features, bytes_accessed=4 * count * features, transcendentals=count
        ),
        name="norm_rows",
    )


def chained(product, end, by, fill=()):
    inside = jnp.stack([product, end])
    reach = 1
    outside = None
    while reach < lax.axis_size("seq"):
        got = shifted(inside, "seq", by * reach)
        if fill:
            got = after(got, *fill.pop(0)(inside))
        if outside is None:
            outside = got
        else:
            outside = jnp.stack([outside[0] * got[0], outside[1] + outside[0] * got[1]])
        inside = jnp.stack([product * outside[0], end + product * outside[1]])
        reach *= 2
    return outside[1]


def per_device(
    tokens,
    segment_ids,
    first_gain,
    input_proj,
    gate_proj,
    conv_weight,
    conv_bias,
    state_proj,
    step_proj,
    step_bias,
    decay_log,
    skip_gain,
    output_proj,
    second_gain,
    hidden_gate,
    hidden_up,
    hidden_down,
    upstream,
):
    count, features = tokens.shape[1:]
    width = conv_weight.shape[1]
    rank = step_proj.shape[0]
    size = decay_log.shape[1]
    channels = input_proj.shape[1]
    quarter = count // lax.axis_size("chan")
    half = count // 2
    me = lax.axis_index("chan")
    place = lax.axis_index("seq")
    dp_bits = [("dp", mask) for mask in bits_of("dp")]
    seq_bits = [("seq", mask) for mask in bits_of("seq")]
    shard_bits = dp_bits + seq_bits
    usual = dp_bits + seq_bits[::-1]
    other = seq_bits[-1:] + dp_bits + seq_bits[:-1]
    scan_ends, scan_forward, scan_heads, scan_backward = scan_calls(count, channels, size, rank)

    def block(values, r):
        return lax.dynamic_slice_in_dim(values, (me ^ r) * quarter, quarter)

    def own_half(values, r):
        return lax.dynamic_slice_in_dim(values, ((me >> 1) ^ r) * half, half)

    def scatter(value, order):
        return Scatter(value, order, shard_bits)

    padded_ids = jnp.concatenate([jnp.full((width - 1,), -1, jnp.int32), segment_ids[0]], axis=0)
    window_ids = lax.dynamic_slice_in_dim(padded_ids, place * count, count + width - 1)
    own_ids = window_ids[width - 1 :]
    masks = [
        (window_ids[offset : offset + count] == own_ids).astype(f32)[:, None]
        for offset in range(width)
    ]
    keep = masks[width - 2]

    rows = tokens[0]
    upper = upstream[0]

    def unit_of(values):
        scale = lax.rsqrt(jnp.mean(values * values, axis=-1, keepdims=True) + epsilon)
        return scale, values * scale

    gain_one = first_gain.astype(f32)
    gain_two = second_gain.astype(f32)
    normed = norm_call(count, features)(rows, gain_one[None])
    inner = matmul(normed, input_proj).astype(bf16)
    rim = shifted(inner[count - width + 1 :], "seq", 1)
    gate_in = matmul(normed, gate_proj)
    extended = jnp.concatenate([rim, after(inner, gate_in)], axis=0).astype(f32)
    taps = conv_weight.astype(f32).T
    convolved = conv_bias.astype(f32) + sum(
        extended[offset : offset + count] * taps[offset] * masks[offset]
        for offset in range(width)
    )
    mixed = jax.nn.silu(convolved).astype(bf16)
    mixed_wide = mixed.astype(f32)
    upper_halves = [own_half(upper, r) for r in range(2)]
    grad_actives = []

    def upstream_parts(begun):
        grad_actives.extend(
            transposed_right(after(item, begun), hidden_down) for item in upper_halves
        )
        return grad_actives

    projected = chan_total(matmul(mixed, state_proj), distant=upstream_parts)
    step_low = projected[:, :rank].astype(bf16)
    step_pre = matmul(step_low, step_proj) + step_bias.astype(f32)
    rates = jax.nn.softplus(step_pre)
    decay = -jnp.exp(decay_log.astype(f32)).T
    decay_two = decay * log2e
    column = lax.broadcasted_iota(jnp.int32, projected.shape, 1)
    scan_proj = jnp.where(column == 0, (1.0 - keep) * far, projected)

    ends, sums, end_total, product_total = scan_ends(rates, mixed_wide, scan_proj, decay_two)
    arriving = chained(product_total, end_total, 1)
    skip = skip_gain.astype(f32)[None]
    gated, ssm_sum, before = scan_forward(
        rates, mixed_wide, scan_proj, decay_two, ends, sums, arriving, gate_in, skip
    )

    hidden_sum = chan_scatter(lambda r: matmul(block(gated, r), output_proj).astype(bf16))
    rows_own = block(rows, 0).astype(f32)
    upper_own = block(upper, 0).astype(f32)
    hidden_one = rows_own + hidden_sum
    scale_two, unit_two = unit_of(hidden_one)

    def feed_forward(normed_part, grad_active):
        gate_ffn = matmul(normed_part, hidden_gate)
        up_ffn = matmul(normed_part, hidden_up)
        gate_act_ffn = jax.nn.silu(gate_ffn)
        active = (gate_act_ffn * up_ffn).astype(bf16)
        grad_gate_ffn = (grad_active * up_ffn * silu_slope(gate_ffn)).astype(bf16)
        grad_up_ffn = (grad_active * gate_act_ffn).astype(bf16)
        grad_normed = (
            transposed_right(grad_gate_ffn, hidden_gate) + transposed_right(grad_up_ffn, hidden_up)
        ).astype(bf16)
        return active, grad_gate_ffn, grad_up_ffn, grad_normed

    halves = []

    def half_forward(own, beside, r):
        normed_half = lax.optimization_barrier(in_order(own, beside))
        halves.append((normed_half,) + feed_forward(normed_half, grad_actives[r]))
        return halves[-1]

    normed_own = (unit_two * gain_two).astype(bf16)
    normed_blocks = chan_gather(normed_own, lambda beside: half_forward(normed_own, beside, 0))
    half_forward(*normed_blocks[2:], 1)

    def quarter_of(items, r):
        return lax.dynamic_slice_in_dim(items[r // 2], ((me ^ r) & 1) * quarter, quarter)

    normed_two, active, grad_gate_ffn, grad_up_ffn = (
        jnp.concatenate([item[k] for item in halves], axis=0) for k in range(4)
    )
    upper_two = jnp.concatenate(upper_halves, axis=0)
    ffn_sums = []

    def ffn_weights(begun):
        left, right = after((normed_two, upper_two), begun)
        sent = []
        for value, order in (
            (transposed_left(left, grad_up_ffn), usual),
            (transposed_left(left, grad_gate_ffn), usual),
            (transposed_left(right, active), other),
        ):
            ffn_sums.append(scatter(value, order))
            sent.append(ffn_sums[-1].send())
        return sent

    grad_normed_two = chan_scatter(
        lambda r: quarter_of([item[4] for item in halves], r), ffn_weights
    )
    grad_unit_two = grad_normed_two * gain_two
    grad_hidden = upper_own + scale_two * (
        grad_unit_two - unit_two * jnp.mean(grad_unit_two * unit_two, axis=-1, keepdims=True)
    )

    def placed(blocks, dtype):
        whole = jnp.zeros((count, features), dtype)
        for r, item in enumerate(blocks):
            whole = lax.dynamic_update_slice_in_dim(
                whole, item.astype(dtype), (me ^ r) * quarter, 0
            )
        return whole

    results = []

    def result_parts(begun):
        for item in halves:
            results.append(matmul(after(item[1], begun), hidden_down).astype(bf16))
        results.append(swap(quarter_of(results, 3), "chan", 1))
        results.append(swap(quarter_of(results, 1), "chan", 1))
        return results[:2]

    hidden_low = placed(chan_gather(grad_hidden.astype(bf16), result_parts), bf16)
    result_middle = (
        quarter_of(results, 2).astype(f32) + after(results[2], hidden_low).astype(f32)
    ).astype(bf16)
    result_far = swap(result_middle, "chan", 2)
    gate_act = jax.nn.silu(gate_in)
    grad_gated = transposed_right(hidden_low, output_proj)
    grad_scanned = grad_gated * gate_act
    grad_gate_in = (grad_gated * ssm_sum.astype(f32) * silu_slope(gate_in)).astype(bf16)
    skip_grad = jnp.sum(grad_scanned * mixed_wide, axis=0)
    heads, head_total = scan_heads(
        rates, after(grad_scanned, result_middle), scan_proj, decay_two, sums
    )

    mixer_sums = []

    def output_weights(begun):
        value = transposed_left(after(hidden_low, begun), gated)
        mixer_sums.append(scatter(value, usual))
        return [mixer_sums[0].send()]

    def gate_weights(begun):
        value = transposed_left(normed, after(grad_gate_in, begun))
        mixer_sums.append(scatter(value, other))
        return [mixer_sums[1].send()]

    leaving = chained(product_total, head_total, -1, [output_weights, gate_weights])
    sent = [item.send(leaving) for item in ffn_sums]
    result_sum = (
        quarter_of(results, 0).astype(f32)
        + results[3].astype(f32)
        + after(result_far, leaving).astype(f32)
    )
    result_own = (hidden_one + result_sum).astype(bf16)
    result_across = swap(result_own, "chan", 2)
    result_beside = swap(result_own, "chan", 1)
    step_padded = jnp.pad(step_proj, ((0, 2 * size), (0, 0)))
    scan_inputs = (rates, mixed_wide, grad_scanned, scan_proj, decay_two, heads, sums)
    first_scan, second_scan = scan_backward
    begin = after(leaving, sent, result_own)
    parts = first_scan(*scan_inputs, begin, before, skip, step_padded)
    terms = parts[2]
    sent = [item.send(terms) for item in ffn_sums]
    begin = after(leaving, sent)
    kept = [parts[k] for k in (0, 1, 3, 4)]
    pre_low, direct, more_terms, decay_grad, step_bias_grad = second_scan(
        *scan_inputs, begin, before, skip, step_padded, *kept
    )
    arrived = [item.terms[-1] for item in ffn_sums[:2] + mixer_sums]
    more_terms = after(more_terms, arrived, result_across)
    proj_terms = terms + more_terms

    step_weight_grad = []

    def step_weights():
        step_weight_grad.append(transposed_left(step_low, pre_low).astype(bf16))
        return step_weight_grad

    results_whole = []

    def result_place(begun):
        sent = [item.send(begun) for item in mixer_sums]
        across = after(result_across, begun, *sent)
        blocks = [result_own, result_beside, across, swap(across, "chan", 1)]
        results_whole.append(placed(blocks, bf16))
        return results_whole + [ffn_sums[2].terms[-1]]

    grad_projected = chan_total(proj_terms, step_weights, result_place).astype(bf16)
    grad_mixed = transposed_right(grad_projected, state_proj) + direct
    grad_conv = grad_mixed * silu_slope(convolved)
    conv_bias_grad = jnp.sum(grad_conv, axis=0)
    conv_taps_grad = jnp.stack(
        [
            jnp.sum(grad_conv * extended[offset : offset + count] * masks[offset], axis=0)
            for offset in range(width)
        ],
        axis=0,
    )
    grad_extended = sum(
        jnp.pad(
            grad_conv * taps[offset] * masks[offset], ((offset, width - 1 - offset), (0, 0))
        )
        for offset in range(width)
    )
    spill = grad_extended[: width - 1]
    returned = shifted(spill, "seq", -1)
    state_grad = transposed_left(after(grad_projected, spill), mixed).astype(bf16)
    few = jnp.concatenate(
        [
            conv_taps_grad,
            conv_bias_grad[None],
            step_bias_grad,
            decay_grad * decay,
            skip_grad[None],
        ],
        axis=0,
    )
    shards = lax.axis_size("dp") * lax.axis_size("seq")
    shard = lax.axis_index("dp") * lax.axis_size("seq") + place
    low_rows = rank // shards
    low_parts = jnp.concatenate(
        [
            state_grad[:rank].reshape(shards, low_rows, channels),
            step_weight_grad[0].reshape(shards, low_rows, channels),
        ],
        axis=1,
    )
    inner_low = (
        grad_extended[width - 1 :]
        + jnp.pad(after(returned, low_parts), ((count - width + 1, 0), (0, 0)))
    ).astype(bf16)

    def token_part(r):
        return (
            transposed_right(block(inner_low, r), input_proj)
            + transposed_right(block(grad_gate_in, r), gate_proj)
        ).astype(bf16)

    input_sums = []

    def third_round(begun):
        value = transposed_left(normed, after(inner_low, begun)).astype(bf16)
        sent = []
        value = jnp.concatenate([value.reshape(shards, -1, channels), low_parts], axis=1)
        for k, order in ((0, usual), (1, other)):
            part = value[:, :, k * (channels // 2) : (k + 1) * (channels // 2)]
            input_sums.append(scatter(part.reshape(-1, channels // 2), order))
            sent.append(input_sums[-1].send())
        return (
            sent
            + [item.send(*sent) for item in mixer_sums]
            + [item.total(*sent) for item in ffn_sums]
        )

    grad_normed = chan_scatter(token_part, third_round)
    scale_one, unit_one = unit_of(rows_own)
    gain_one_grad = jnp.sum(grad_normed * unit_one, axis=0)
    gain_two_grad = jnp.sum(grad_normed_two * unit_two, axis=0)
    grad_unit_one = grad_normed * gain_one
    tokens_grad = grad_hidden + scale_one * (
        grad_unit_one - unit_one * jnp.mean(grad_unit_one * unit_one, axis=-1, keepdims=True)
    )
    last = []

    def fourth_round(begun):
        last.extend(item.send(begun) for item in input_sums)
        gains = jnp.concatenate([gain_one_grad, gain_two_grad]).astype(bf16)
        gains = sum_all(gains, [("chan", 1), ("chan", 2)]).reshape(-1, channels)
        lines = jnp.concatenate([state_grad[rank:], few.astype(bf16), gains], axis=0)
        padded = jnp.pad(lines, ((0, -lines.shape[0] % 16), (0, 0)))
        last.extend(item.total(begun, *last) for item in mixer_sums)
        last.append(sum_all(padded, shard_bits).astype(f32))
        return last

    tokens_out = placed(chan_gather(tokens_grad.astype(bf16), fourth_round), f32)
    vectors = last[-1]
    input_parts = jnp.concatenate([item.total() for item in input_sums], axis=1)
    input_rows = features // shards

    def share(first):
        whole = vectors[first : first + features // channels].reshape(features)
        return lax.dynamic_slice_in_dim(whole, shard * input_rows, input_rows)

    at = 2 * size
    return (
        results_whole[0][None],
        tokens_out[None],
        share(at + width + size + 3),
        input_parts[:input_rows],
        mixer_sums[1].total(),
        vectors[at : at + width].T,
        vectors[at + width],
        input_parts[input_rows : input_rows + low_rows].T,
        vectors[:at].T,
        input_parts[input_rows + low_rows :],
        vectors[at + width + 1],
        vectors[at + width + 2 : at + width + 2 + size].T,
        vectors[at + width + size + 2],
        mixer_sums[0].total().T,
        share(at + width + size + 3 + features // channels),
        ffn_sums[1].total(),
        ffn_sums[0].total(),
        ffn_sums[2].total().T,
    )


def solution(mesh):
    return jax.shard_map(
        per_device,
        mesh=mesh,
        in_specs=(
            P("dp", "seq", None),
            P("dp", None),
            P(),
            P(None, "chan"),
            P(None, "chan"),
            P("chan", None),
            P("chan"),
            P("chan", None),
            P(None, "chan"),
            P("chan"),
            P("chan", None),
            P("chan"),
            P("chan", None),
            P(),
            P(None, "chan"),
            P(None, "chan"),
            P("chan", None),
            P("dp", "seq", None),
        ),
        out_specs=(
            P("dp", "seq", None),
            P("dp", "seq", None),
            P(("dp", "seq")),
            P(("dp", "seq"), "chan"),
            P(("dp", "seq"), "chan"),
            P("chan", None),
            P("chan"),
            P("chan", ("dp", "seq")),
            P("chan", None),
            P(("dp", "seq"), "chan"),
            P("chan"),
            P("chan", None),
            P("chan"),
            P("chan", ("dp", "seq")),
            P(("dp", "seq")),
            P(("dp", "seq"), "chan"),
            P(("dp", "seq"), "chan"),
            P("chan", ("dp", "seq")),
        ),
        check_vma=False,
    )
```

time: 749 us -> 588 us (0.79)
  waiting for transfers between devices: 258 us -> 125 us
  other arithmetic: 44 us -> 88.9 us
  starting transfers between devices: 90 us -> 59.8 us
  Pallas kernels: 174 us -> 147 us
  matrix products: 127 us -> 102 us
    ppermute x62 -> x54, waiting for transfers between devices: 255 us -> 115 us  [swap(): lax.ppermute(value, axis, [(i, i ^ mask) for i in range(lax.axis_size(axi...]
    ppermute x62 -> x54, starting transfers between devices: 69.1 us -> 40.6 us  [swap(): lax.ppermute(value, axis, [(i, i ^ mask) for i in range(lax.axis_size(axi...]
    pallas_call x4 -> x6, Pallas kernels: 174 us -> 147 us  [the longest x1 34.8 us: per_device(): second_scan(*scan_inputs, begin, before, skip, step_padded, *kept)]
    dot_general x16 -> x14, matrix products: 60.3 us -> 42.3 us  [matmul(): return jnp.dot(left, right, preferred_element_type=f32)]
    convert_element_type x28 -> x25, other arithmetic: 20.1 us -> 33.9 us  [the longest x14 24.6 us: send(): away = sum((t.astype(f32) for t in away)).astype(bf16)]
    unnamed x185 -> x250, local copies, waits for them, and re-layouts: 10.4 us -> 21.6 us
    add x9 -> x12, other arithmetic: 7.15 us -> 18 us  [the longest x7 13.9 us: total(): return sum((t.astype(f32) for t in self.terms))]
    dynamic_update_slice x1 -> x6, other arithmetic: 1.89 us -> 11.3 us  [placed(): lax.dynamic_update_slice_in_dim(whole, item.astype(dtype), (me ^ r) * qua...]
  transfers between devices with their start and end apart: 70 -> 60, of which waited for: 29 -> 26; matrix products, arithmetic and copies ran while one was open for 22% -> 29% of each run, Pallas kernels for 14% -> 16%
where the time goes in v2:
time: 588 us; the launch traced here: 577 us
  Pallas kernels  147 us (25%)
  waiting for transfers between devices  125 us (21%)
  matrix products  102 us (17%)
  other arithmetic  88.9 us (15%)
  starting transfers between devices  59.8 us (10%)
  local copies, waits for them, and re-layouts  51.3 us (9%)
    ppermute x54, waiting for transfers between devices, swap(): lax.ppermute(value, axis, [(i, i ^ mask) for i in range(lax.axis_size(axi...  115 us
    dot_general x14, matrix products, matmul(): return jnp.dot(left, right, preferred_element_type=f32)  42.3 us
    ppermute x54, starting transfers between devices, swap(): lax.ppermute(value, axis, [(i, i ^ mask) for i in range(lax.axis_size(axi...  40.6 us
    dot_general x16, matrix products, transposed_right(): lax.dot_general(left, right, (((1,), (1,)), ((), ())), preferred_element_...  37.3 us
    pallas_call x1, Pallas kernels, per_device(): second_scan(*scan_inputs, begin, before, skip, step_padded, *kept)  34.8 us
    pallas_call x1, Pallas kernels, per_device(): parts = first_scan(*scan_inputs, begin, before, skip, step_padded)  34.7 us
    pallas_call x1, Pallas kernels, per_device(): scan_forward(rates, mixed_wide, scan_proj, decay_two, ends, sums, arrivin...  31.4 us
    convert_element_type x14, other arithmetic, send(): away = sum((t.astype(f32) for t in away)).astype(bf16)  24.6 us
  transfers between devices with their start and end apart: 60, of which 26 were waited for; matrix products, arithmetic and copies ran while one was open for 29% of the time, Pallas kernels for 16%

profile of v2, /device:TPU:0, one launch (start us, length us, event | category | flops | bytes accessed | tf_op | source)
XLA Modules:
  0.0 577.4 jit_solution(1696989499486221088)
XLA Ops:
  2.1 6.7 %norm_rows.1 = bf16[1024,1536]{1,0:T(8,128)(2,1)} custom-call(bf16[1024,1536]{1,0:T(8,128)(2,1)} %bitcast.343, f32[1,1536]{1,0:T(1,128)} %broadcast_in_dim.60.gain), custom_call_target="tpu_custom_call" | custom-call | flops 9437184 | bytes 6291456 | tf_op jit(solution)/shard_map/norm_rows/pallas_call | solution.py:625
  8.9 5.4 convolution_convert_fusion.12
  15.4 4.9 collective-permute-start
  20.5 4.3 fusion.108.gate_in
  26.8 4.2 fusion.105
  43.2 3.5 compare_select_fusion.rates.refs_0_
  46.7 18.2 %scan_ends.1 = (f32[16,8,768]{2,1,0:T(8,128)}, f32[8,768]{1,0:T(8,128)}, f32[16,768]{1,0:T(8,128)}, f32[16,768]{1,0:T(8,128)}) custom-call(f32[1024,768]{1,0:T(8,128)} %compare_select_fusion.rates.refs_0_, f32[1024,768]{1,0:T(8,128)} %get-tuple-element.178.mixed.refs_1_, f32[1024,128]{1,0:T(8,128)} %broadcast_select_fusion.4.proj.refs_3_, ...), custom_call_target="tpu_custom_call" | custom-call | flops 12582912 | tf_op jit(solution)/shard_map/scan_ends/pallas_call | solution.py:655
  65.8 3.5 collective-permute-start.3
  73.0 6.4 %collective-permute-start.4 = (f32[2,16,768]{2,1,0:T(8,128)}, f32[2,16,768]{2,1,0:T(8,128)}, u32[]{:S(2)}, u32[]{:S(2)}) collective-permute-start(f32[2,16,768]{2,1,0:T(8,128)} %pad_maximum_fusion.7), channel_id=1, source_target_pairs={{0,8},{4,12},{1,9},{5,13},{2,10},{6,14},{3,11},{7,15},{16,24},{20,... | collective-permute-start | bytes 294920 | tf_op jit(solution)/shard_map/ppermute | solution.py:44
  82.4 31.4 %scan_forward.1 = (bf16[1024,768]{1,0:T(8,128)(2,1)}, bf16[1024,768]{1,0:T(8,128)(2,1)}, bf16[16,1040,768]{2,1,0:T(8,128)(2,1)}) custom-call(f32[1024,768]{1,0:T(8,128)} %compare_select_fusion.rates.refs_0_, f32[1024,768]{1,0:T(8,128)} %get-tuple-element.178.mixed.refs_1_, f32[1024,128]{1,0:T(8,128)} %broadcast_select_fusion.4.proj.refs_3_, ...), custom_call_target="tpu_custom_call" | custom-call | flops 12582912 | tf_op jit(solution)/shard_map/scan_forward/pallas_call | solution.py:658
  119.1 3.6 add_convert_fusion.3
  129.5 13.1 %collective-permute-done.7 = bf16[256,1536]{1,0:T(8,128)(2,1)} collective-permute-done((bf16[256,1536]{1,0:T(8,128)(2,1)}, bf16[256,1536]{1,0:T(8,128)(2,1)}, u32[]{:S(2)}, u32[]{:S(2)}) %collective-permute-start.7) | collective-permute-done | bytes 786464 | tf_op jit(solution)/shard_map/ppermute | solution.py:39
  155.9 3.7 multiply_convert_fusion.5
  175.6 3.9 multiply_convert_fusion.3
  192.1 3.7 convolution_convert_fusion.2
  195.8 3.7 convolution_convert_fusion.1
  203.2 3.9 convolution_convert_fusion
  211.2 3.2 constant_dynamic-update-slice_fusion.7
  224.3 4.0 convolution_convert_fusion.6
  230.2 11.0 %collective-permute-done.17 = bf16[256,1536]{1,0:T(8,128)(2,1)S(1)} collective-permute-done((bf16[256,1536]{1,0:T(8,128)(2,1)}, bf16[256,1536]{1,0:T(8,128)(2,1)S(1)}, u32[]{:S(2)}, u32[]{:S(2)}) %collective-permute-start.17) | collective-permute-done | bytes 786464 | tf_op jit(solution)/shard_map/ppermute | solution.py:39
  247.0 6.0 %multiply_reduce_fusion = (bf16[768]{0:T(1024)(128)(2,1)}, f32[1024,768]{1,0:T(8,128)}, bf16[1024,768]{1,0:T(8,128)(2,1)S(1)}) fusion(bf16[1024,768]{1,0:T(8,128)(2,1)S(1)} %copy-done.10, f32[1024,768]{1,0:T(8,128)S(1)} %copy-done.46, bf16[1024,768]{1,0:T(8,128)(2,1)S(1)} %copy-done.111, bf16[1024,1536]{1,0:T(8,128)(2,1)S(1)} %constant_dynamic-update-slice_fusion.4, ...), kind=kOutput, calls=%fused_computation.14 | convolution fusion | flops 2428501248 | bytes 16516608 | tf_op jit(solution)/shard_map/dot_general | solution.py:35
  253.1 21.0 %scan_heads.1 = (f32[16,8,768]{2,1,0:T(8,128)}, f32[16,768]{1,0:T(8,128)}) custom-call(f32[1024,768]{1,0:T(8,128)} %compare_select_fusion.rates.refs_0_, f32[1024,768]{1,0:T(8,128)} %get-tuple-element.101.slope.refs_2_, f32[1024,128]{1,0:T(8,128)} %broadcast_select_fusion.4.proj.refs_3_, f32[16,768]{1,0:T(8,128)} %bitcast_multiply_fusion.4.dec.refs_4_, ...), custom_call_target="tpu_custom_call" | custom-call | flops 12582912 | tf_op jit(solution)/shard_map/scan_heads/pallas_call | solution.py:747
  276.2 4.7 convolution_convert_fusion.5
  288.2 4.3 collective-permute-done.21
  305.1 6.4 %collective-permute-done.19 = bf16[256,1536]{1,0:T(8,128)(2,1)S(1)} collective-permute-done((bf16[256,1536]{1,0:T(8,128)(2,1)S(1)}, bf16[256,1536]{1,0:T(8,128)(2,1)S(1)}, u32[]{:S(2)}, u32[]{:S(2)}) %collective-permute-start.19) | collective-permute-done | bytes 786464 | tf_op jit(solution)/shard_map/ppermute | solution.py:39
  321.8 34.7 %scan_backward.2 = (bf16[1024,768]{1,0:T(8,128)(2,1)}, f32[1024,768]{1,0:T(8,128)}, f32[1024,128]{1,0:T(8,128)}, f32[16,768]{1,0:T(8,128)}, f32[1,768]{1,0:T(1,128)}) custom-call(f32[1024,768]{1,0:T(8,128)} %compare_select_fusion.rates.refs_0_, f32[1024,768]{1,0:T(8,128)} %get-tuple-element.178.mixed.refs_1_, f32[1024,768]{1,0:T(8,128)} %get-tuple-element.101.slope.refs_2_, ...), custom_call_target="tpu_custom_call" | custom-call | flops 12582912 | tf_op jit(solution)/shard_map/scan_backward/pallas_call | solution.py:777
  368.5 34.8 %scan_backward.3 = (bf16[1024,768]{1,0:T(8,128)(2,1)}, f32[1024,768]{1,0:T(8,128)}, f32[1024,128]{1,0:T(8,128)}, f32[16,768]{1,0:T(8,128)}, f32[1,768]{1,0:T(1,128)}) custom-call(f32[1024,768]{1,0:T(8,128)} %compare_select_fusion.rates.refs_0_, ...), custom_call_target="tpu_custom_call", output_to_operand_aliasing={{0}: (11, {}), {1}: (12, {}), {3}: (13, {}), {4}: (14, {})} | custom-call | flops 12582912 | tf_op jit(solution)/shard_map/scan_backward/pallas_call | solution.py:782
  425.7 12.0 %collective-permute-done.37 = bf16[192,1024]{1,0:T(8,128)(2,1)} collective-permute-done((bf16[192,1024]{1,0:T(8,128)(2,1)}, bf16[192,1024]{1,0:T(8,128)(2,1)}, u32[]{:S(2)}, u32[]{:S(2)}) %collective-permute-start.37) | collective-permute-done | bytes 393248 | tf_op jit(solution)/shard_map/ppermute | solution.py:39
  438.4 5.5 multiply_reduce_fusion.1
  495.0 26.8 %collective-permute-done.53 = bf16[64,768]{1,0:T(8,128)(2,1)S(1)} collective-permute-done((bf16[64,768]{1,0:T(8,128)(2,1)S(1)}, bf16[64,768]{1,0:T(8,128)(2,1)S(1)}, u32[]{:S(2)}, u32[]{:S(2)}) %collective-permute-start.53) | collective-permute-done | bytes 98336 | tf_op jit(solution)/shard_map/ppermute | solution.py:39
  541.9 10.4 %collective-permute-done.45 = bf16[256,1536]{1,0:T(8,128)(2,1)S(1)} collective-permute-done((bf16[256,1536]{1,0:T(8,128)(2,1)}, bf16[256,1536]{1,0:T(8,128)(2,1)S(1)}, u32[]{:S(2)}, u32[]{:S(2)}) %collective-permute-start.45) | collective-permute-done | bytes 786464 | tf_op jit(solution)/shard_map/ppermute | solution.py:39
  560.2 9.7 %collective-permute-done.57 = bf16[216,384]{1,0:T(8,128)(2,1)S(1)} collective-permute-done((bf16[216,384]{1,0:T(8,128)(2,1)S(1)}, bf16[216,384]{1,0:T(8,128)(2,1)S(1)}, u32[]{:S(2)}, u32[]{:S(2)}) %collective-permute-start.57) | collective-permute-done | bytes 165920 | tf_op jit(solution)/shard_map/ppermute | solution.py:39
  (514 shorter events, 255.8 us)
Async XLA Ops:
  122.7 19.9 %collective-permute-start.7 = (bf16[256,1536]{1,0:T(8,128)(2,1)}, bf16[256,1536]{1,0:T(8,128)(2,1)}, u32[]{:S(2)}, u32[]{:S(2)}) collective-permute-start(bf16[256,1536]{1,0:T(8,128)(2,1)} %add_convert_fusion.3), channel_id=1, source_target_pairs={{0,2},{1,3},{2,0},{3,1},{4,6},{5,7},{6,4},{7,5},{8,10},{9,11},{10,... | collective-permute-start | bytes 2359304 | tf_op jit(solution)/shard_map/ppermute | solution.py:39
  147.1 20.3 %collective-permute-start.10 = (bf16[256,1536]{1,0:T(8,128)(2,1)}, bf16[256,1536]{1,0:T(8,128)(2,1)}, u32[]{:S(2)}, u32[]{:S(2)}) collective-permute-start(bf16[256,1536]{1,0:T(8,128)(2,1)} %multiply_convert_fusion.8), channel_id=1, source_target_pairs={{0,2},{1,3},{2,0},{3,1},{4,6},{5,7},{6,4},{7,5},{8,10},{9,11},{10,... | collective-permute-start | bytes 2359304 | tf_op jit(solution)/shard_map/ppermute | solution.py:39
  186.1 24.2 %collective-permute-start.9 = (bf16[256,1536]{1,0:T(8,128)(2,1)S(1)}, bf16[256,1536]{1,0:T(8,128)(2,1)S(1)}, u32[]{:S(2)}, u32[]{:S(2)}) collective-permute-start(bf16[256,1536]{1,0:T(8,128)(2,1)S(1)} %get-tuple-element.197), channel_id=1, source_target_pairs={{0,1},{1,0},{2,3},{3,2},{4,5},{5,4},{6,7},{7,6},{8,9},{9,8},{10,11... | collective-permute-start | bytes 2359304 | tf_op jit(solution)/shard_map/ppermute | solution.py:39
  190.5 19.8 %collective-permute-start.13 = (bf16[256,1536]{1,0:T(8,128)(2,1)S(1)}, bf16[256,1536]{1,0:T(8,128)(2,1)S(1)}, u32[]{:S(2)}, u32[]{:S(2)}) collective-permute-start(bf16[256,1536]{1,0:T(8,128)(2,1)S(1)} %add_convert_fusion.2), channel_id=1, source_target_pairs={{0,2},{1,3},{2,0},{3,1},{4,6},{5,7},{6,4},{7,5},{8,10},{9,11},{10,... | collective-permute-start | bytes 2359304 | tf_op jit(solution)/shard_map/ppermute | solution.py:39
  217.8 76.9 %collective-permute-start.24 = (bf16[2,2,192,1024]{3,2,1,0:T(8,128)(2,1)}, bf16[2,2,192,1024]{3,2,1,0:T(8,128)(2,1)}, u32[]{:S(2)}, u32[]{:S(2)}) collective-permute-start(bf16[2,2,192,1024]{3,2,1,0:T(8,128)(2,1)} %dynamic-slice_bitcast_fusion.2), channel_id=1, source_target_pairs={{0,16},{16,0},{1,17},{17,1},{2,18},{18,2},{3,19},{19,3},{4,20},{20... | collective-permute-start | bytes 4718600 | tf_op jit(solution)/shard_map/ppermute | solution.py:39
  219.4 76.8 %collective-permute-start.25 = (bf16[2,2,192,1024]{3,2,1,0:T(8,128)(2,1)}, bf16[2,2,192,1024]{3,2,1,0:T(8,128)(2,1)}, u32[]{:S(2)}, u32[]{:S(2)}) collective-permute-start(bf16[2,2,192,1024]{3,2,1,0:T(8,128)(2,1)} %dynamic-slice_bitcast_fusion.1), channel_id=1, source_target_pairs={{0,16},{16,0},{1,17},{17,1},{2,18},{18,2},{3,19},{19,3},{4,20},{20... | collective-permute-start | bytes 4718600 | tf_op jit(solution)/shard_map/ppermute | solution.py:39
  219.9 80.6 %collective-permute-start.26 = (bf16[2,2,192,1024]{3,2,1,0:T(8,128)(2,1)}, bf16[2,2,192,1024]{3,2,1,0:T(8,128)(2,1)}, u32[]{:S(2)}, u32[]{:S(2)}) collective-permute-start(bf16[2,2,192,1024]{3,2,1,0:T(8,128)(2,1)} %dynamic-slice_bitcast_fusion), channel_id=1, source_target_pairs={{0,4},{4,0},{8,12},{12,8},{1,5},{5,1},{9,13},{13,9},{2,6},{6,2},{1... | collective-permute-start | bytes 4718600 | tf_op jit(solution)/shard_map/ppermute | solution.py:39
  221.9 19.3 %collective-permute-start.17 = (bf16[256,1536]{1,0:T(8,128)(2,1)}, bf16[256,1536]{1,0:T(8,128)(2,1)S(1)}, u32[]{:S(2)}, u32[]{:S(2)}) collective-permute-start(bf16[256,1536]{1,0:T(8,128)(2,1)} %get-tuple-element.172), channel_id=1, source_target_pairs={{0,2},{1,3},{2,0},{3,1},{4,6},{5,7},{6,4},{7,5},{8,10},{9,11},{10,... | collective-permute-start | bytes 2359304 | tf_op jit(solution)/shard_map/ppermute | solution.py:39
  243.5 67.9 %collective-permute-start.15 = (bf16[256,1536]{1,0:T(8,128)(2,1)}, bf16[256,1536]{1,0:T(8,128)(2,1)}, u32[]{:S(2)}, u32[]{:S(2)}) collective-permute-start(bf16[256,1536]{1,0:T(8,128)(2,1)} %constant_dynamic-slice_fusion.1), channel_id=1, source_target_pairs={{0,1},{1,0},{2,3},{3,2},{4,5},{5,4},{6,7},{7,6},{8,9},{9,8},{10,11... | collective-permute-start | bytes 2359304 | tf_op jit(solution)/shard_map/ppermute | solution.py:39
  292.5 18.9 %collective-permute-start.19 = (bf16[256,1536]{1,0:T(8,128)(2,1)S(1)}, bf16[256,1536]{1,0:T(8,128)(2,1)S(1)}, u32[]{:S(2)}, u32[]{:S(2)}) collective-permute-start(bf16[256,1536]{1,0:T(8,128)(2,1)S(1)} %add_convert_fusion.1), channel_id=1, source_target_pairs={{0,2},{1,3},{2,0},{3,1},{4,6},{5,7},{6,4},{7,5},{8,10},{9,11},{10,... | collective-permute-start | bytes 2359304 | tf_op jit(solution)/shard_map/ppermute | solution.py:39
  294.7 108.6 %collective-permute-start.32 = (bf16[2,2,192,768]{3,2,1,0:T(8,128)(2,1)}, bf16[2,2,192,768]{3,2,1,0:T(8,128)(2,1)}, u32[]{:S(2)}, u32[]{:S(2)}) collective-permute-start(bf16[2,2,192,768]{3,2,1,0:T(8,128)(2,1)} %dynamic-slice_bitcast_fusion.6), channel_id=1, source_target_pairs={{0,16},{16,0},{1,17},{17,1},{2,18},{18,2},{3,19},{19,3},{4,20},{20... | collective-permute-start | bytes 3538952 | tf_op jit(solution)/shard_map/ppermute | solution.py:39
  297.9 20.5 %collective-permute-start.27 = (bf16[2,192,1024]{2,1,0:T(8,128)(2,1)S(1)}, bf16[2,192,1024]{2,1,0:T(8,128)(2,1)S(1)}, u32[]{:S(2)}, u32[]{:S(2)}) collective-permute-start(bf16[2,192,1024]{2,1,0:T(8,128)(2,1)S(1)} %fusion.34), channel_id=1, source_target_pairs={{0,4},{4,0},{8,12},{12,8},{1,5},{5,1},{9,13},{13,9},{2,6},{6,2},{1... | collective-permute-start | bytes 2359304 | tf_op jit(solution)/shard_map/ppermute | solution.py:39
  300.5 102.8 %collective-permute-start.33 = (bf16[2,2,192,768]{3,2,1,0:T(8,128)(2,1)}, bf16[2,2,192,768]{3,2,1,0:T(8,128)(2,1)}, u32[]{:S(2)}, u32[]{:S(2)}) collective-permute-start(bf16[2,2,192,768]{3,2,1,0:T(8,128)(2,1)} %dynamic-slice_bitcast_fusion.5), channel_id=1, source_target_pairs={{0,4},{4,0},{8,12},{12,8},{1,5},{5,1},{9,13},{13,9},{2,6},{6,2},{1... | collective-permute-start | bytes 3538952 | tf_op jit(solution)/shard_map/ppermute | solution.py:39
  311.5 47.1 %collective-permute-start.28 = (bf16[2,192,1024]{2,1,0:T(8,128)(2,1)}, bf16[2,192,1024]{2,1,0:T(8,128)(2,1)}, u32[]{:S(2)}, u32[]{:S(2)}) collective-permute-start(bf16[2,192,1024]{2,1,0:T(8,128)(2,1)} %fusion.33), channel_id=1, source_target_pairs={{0,4},{4,0},{8,12},{12,8},{1,5},{5,1},{9,13},{13,9},{2,6},{6,2},{1... | collective-permute-start | bytes 2359304 | tf_op jit(solution)/shard_map/ppermute | solution.py:39
  311.5 50.1 %collective-permute-start.29 = (bf16[2,192,1024]{2,1,0:T(8,128)(2,1)}, bf16[2,192,1024]{2,1,0:T(8,128)(2,1)}, u32[]{:S(2)}, u32[]{:S(2)}) collective-permute-start(bf16[2,192,1024]{2,1,0:T(8,128)(2,1)} %fusion.32), channel_id=1, source_target_pairs={{0,16},{16,0},{1,17},{17,1},{2,18},{18,2},{3,19},{19,3},{4,20},{20... | collective-permute-start | bytes 2359304 | tf_op jit(solution)/shard_map/ppermute | solution.py:39
  319.3 84.1 %collective-permute-start.23 = (bf16[256,1536]{1,0:T(8,128)(2,1)}, bf16[256,1536]{1,0:T(8,128)(2,1)}, u32[]{:S(2)}, u32[]{:S(2)}) collective-permute-start(bf16[256,1536]{1,0:T(8,128)(2,1)} %get-tuple-element.170), channel_id=1, source_target_pairs={{0,2},{1,3},{2,0},{3,1},{4,6},{5,7},{6,4},{7,5},{8,10},{9,11},{10,... | collective-permute-start | bytes 2359304 | tf_op jit(solution)/shard_map/ppermute | solution.py:39
  359.9 43.4 %collective-permute-start.30 = (bf16[192,1024]{1,0:T(8,128)(2,1)S(1)}, bf16[192,1024]{1,0:T(8,128)(2,1)S(1)}, u32[]{:S(2)}, u32[]{:S(2)}) collective-permute-start(bf16[192,1024]{1,0:T(8,128)(2,1)S(1)} %fusion.42), channel_id=1, source_target_pairs={{0,8},{4,12},{8,0},{12,4},{1,9},{5,13},{9,1},{13,5},{2,10},{6,14},... | collective-permute-start | bytes 1179656 | tf_op jit(solution)/shard_map/ppermute | solution.py:39
  361.6 41.8 %collective-permute-start.31 = (bf16[192,1024]{1,0:T(8,128)(2,1)S(1)}, bf16[192,1024]{1,0:T(8,128)(2,1)S(1)}, u32[]{:S(2)}, u32[]{:S(2)}) collective-permute-start(bf16[192,1024]{1,0:T(8,128)(2,1)S(1)} %fusion.41), channel_id=1, source_target_pairs={{0,8},{4,12},{8,0},{12,4},{1,9},{5,13},{9,1},{13,5},{2,10},{6,14},... | collective-permute-start | bytes 1179656 | tf_op jit(solution)/shard_map/ppermute | solution.py:39
  416.8 20.9 %collective-permute-start.37 = (bf16[192,1024]{1,0:T(8,128)(2,1)}, bf16[192,1024]{1,0:T(8,128)(2,1)}, u32[]{:S(2)}, u32[]{:S(2)}) collective-permute-start(bf16[192,1024]{1,0:T(8,128)(2,1)} %fusion.40), channel_id=1, source_target_pairs={{0,8},{4,12},{8,0},{12,4},{1,9},{5,13},{9,1},{13,5},{2,10},{6,14},... | collective-permute-start | bytes 1179656 | tf_op jit(solution)/shard_map/ppermute | solution.py:39
  418.7 19.0 %collective-permute-start.36 = (bf16[1024,128]{1,0:T(8,128)(2,1)S(1)}, bf16[1024,128]{1,0:T(8,128)(2,1)S(1)}, u32[]{:S(2)}, u32[]{:S(2)}) collective-permute-start(bf16[1024,128]{1,0:T(8,128)(2,1)S(1)} %add_convert_fusion.5), channel_id=1, source_target_pairs={{0,2},{1,3},{2,0},{3,1},{4,6},{5,7},{6,4},{7,5},{8,10},{9,11},{10,... | collective-permute-start | bytes 786440 | tf_op jit(solution)/shard_map/ppermute | solution.py:39
  419.2 47.3 %collective-permute-start.42 = (bf16[2,192,768]{2,1,0:T(8,128)(2,1)}, bf16[2,192,768]{2,1,0:T(8,128)(2,1)}, u32[]{:S(2)}, u32[]{:S(2)}) collective-permute-start(bf16[2,192,768]{2,1,0:T(8,128)(2,1)} %fusion.36), channel_id=1, source_target_pairs={{0,4},{4,0},{8,12},{12,8},{1,5},{5,1},{9,13},{13,9},{2,6},{6,2},{1... | collective-permute-start | bytes 1769480 | tf_op jit(solution)/shard_map/ppermute | solution.py:39
  420.9 47.6 %collective-permute-start.43 = (bf16[2,192,768]{2,1,0:T(8,128)(2,1)}, bf16[2,192,768]{2,1,0:T(8,128)(2,1)}, u32[]{:S(2)}, u32[]{:S(2)}) collective-permute-start(bf16[2,192,768]{2,1,0:T(8,128)(2,1)} %fusion.35), channel_id=1, source_target_pairs={{0,16},{16,0},{1,17},{17,1},{2,18},{18,2},{3,19},{19,3},{4,20},{20... | collective-permute-start | bytes 1769480 | tf_op jit(solution)/shard_map/ppermute | solution.py:39
  457.9 21.9 %collective-permute-start.39 = (bf16[256,1536]{1,0:T(8,128)(2,1)S(1)}, bf16[256,1536]{1,0:T(8,128)(2,1)S(1)}, u32[]{:S(2)}, u32[]{:S(2)}) collective-permute-start(bf16[256,1536]{1,0:T(8,128)(2,1)S(1)} %fusion.5), channel_id=1, source_target_pairs={{0,1},{1,0},{2,3},{3,2},{4,5},{5,4},{6,7},{7,6},{8,9},{9,8},{10,11... | collective-permute-start | bytes 2359304 | tf_op jit(solution)/shard_map/ppermute | solution.py:39
  460.2 19.6 %collective-permute-start.41 = (bf16[256,1536]{1,0:T(8,128)(2,1)S(1)}, bf16[256,1536]{1,0:T(8,128)(2,1)S(1)}, u32[]{:S(2)}, u32[]{:S(2)}) collective-permute-start(bf16[256,1536]{1,0:T(8,128)(2,1)S(1)} %fusion.9), channel_id=1, source_target_pairs={{0,2},{1,3},{2,0},{3,1},{4,6},{5,7},{6,4},{7,5},{8,10},{9,11},{10,... | collective-permute-start | bytes 2359304 | tf_op jit(solution)/shard_map/ppermute | solution.py:39
  487.6 44.5 %collective-permute-start.46 = (bf16[2,2,216,384]{3,2,1,0:T(8,128)(2,1)}, bf16[2,2,216,384]{3,2,1,0:T(8,128)(2,1)}, u32[]{:S(2)}, u32[]{:S(2)}) collective-permute-start(bf16[2,2,216,384]{3,2,1,0:T(8,128)(2,1)} %dynamic-slice_bitcast_fusion.8), channel_id=1, source_target_pairs={{0,16},{16,0},{1,17},{17,1},{2,18},{18,2},{3,19},{19,3},{4,20},{20... | collective-permute-start | bytes 1990664 | tf_op jit(solution)/shard_map/ppermute | solution.py:39
  489.1 43.6 %collective-permute-start.47 = (bf16[2,2,216,384]{3,2,1,0:T(8,128)(2,1)}, bf16[2,2,216,384]{3,2,1,0:T(8,128)(2,1)}, u32[]{:S(2)}, u32[]{:S(2)}) collective-permute-start(bf16[2,2,216,384]{3,2,1,0:T(8,128)(2,1)} %dynamic-slice_bitcast_fusion.7), channel_id=1, source_target_pairs={{0,4},{4,0},{8,12},{12,8},{1,5},{5,1},{9,13},{13,9},{2,6},{6,2},{1... | collective-permute-start | bytes 1990664 | tf_op jit(solution)/shard_map/ppermute | solution.py:39
  490.4 47.2 %collective-permute-start.48 = (bf16[192,768]{1,0:T(8,128)(2,1)}, bf16[192,768]{1,0:T(8,128)(2,1)}, u32[]{:S(2)}, u32[]{:S(2)}) collective-permute-start(bf16[192,768]{1,0:T(8,128)(2,1)} %fusion.49), channel_id=1, source_target_pairs={{0,8},{4,12},{8,0},{12,4},{1,9},{5,13},{9,1},{13,5},{2,10},{6,14},... | collective-permute-start | bytes 884744 | tf_op jit(solution)/shard_map/ppermute | solution.py:39
  490.4 49.4 %collective-permute-start.49 = (bf16[192,768]{1,0:T(8,128)(2,1)}, bf16[192,768]{1,0:T(8,128)(2,1)S(1)}, u32[]{:S(2)}, u32[]{:S(2)}) collective-permute-start(bf16[192,768]{1,0:T(8,128)(2,1)} %fusion.48), channel_id=1, source_target_pairs={{0,8},{4,12},{8,0},{12,4},{1,9},{5,13},{9,1},{13,5},{2,10},{6,14},... | collective-permute-start | bytes 884744 | tf_op jit(solution)/shard_map/ppermute | solution.py:39
  494.2 27.6 %collective-permute-start.53 = (bf16[64,768]{1,0:T(8,128)(2,1)S(1)}, bf16[64,768]{1,0:T(8,128)(2,1)S(1)}, u32[]{:S(2)}, u32[]{:S(2)}) collective-permute-start(bf16[64,768]{1,0:T(8,128)(2,1)S(1)} %add_convert_fusion.9), channel_id=1, source_target_pairs={{0,8},{4,12},{8,0},{12,4},{1,9},{5,13},{9,1},{13,5},{2,10},{6,14},... | collective-permute-start | bytes 294920 | tf_op jit(solution)/shard_map/ppermute | solution.py:39
  532.1 20.2 %collective-permute-start.45 = (bf16[256,1536]{1,0:T(8,128)(2,1)}, bf16[256,1536]{1,0:T(8,128)(2,1)S(1)}, u32[]{:S(2)}, u32[]{:S(2)}) collective-permute-start(bf16[256,1536]{1,0:T(8,128)(2,1)} %get-tuple-element.168), channel_id=1, source_target_pairs={{0,2},{1,3},{2,0},{3,1},{4,6},{5,7},{6,4},{7,5},{8,10},{9,11},{10,... | collective-permute-start | bytes 2359304 | tf_op jit(solution)/shard_map/ppermute | solution.py:39
  537.1 19.1 %collective-permute-start.58 = (bf16[2,216,384]{2,1,0:T(8,128)(2,1)S(1)}, bf16[2,216,384]{2,1,0:T(8,128)(2,1)S(1)}, u32[]{:S(2)}, u32[]{:S(2)}) collective-permute-start(bf16[2,216,384]{2,1,0:T(8,128)(2,1)S(1)} %fusion.43), channel_id=1, source_target_pairs={{0,16},{16,0},{1,17},{17,1},{2,18},{18,2},{3,19},{19,3},{4,20},{20... | collective-permute-start | bytes 995336 | tf_op jit(solution)/shard_map/ppermute | solution.py:39
  552.3 23.4 %collective-permute-start.55 = (bf16[256,1536]{1,0:T(8,128)(2,1)S(1)}, bf16[256,1536]{1,0:T(8,128)(2,1)S(1)}, u32[]{:S(2)}, u32[]{:S(2)}) collective-permute-start(bf16[256,1536]{1,0:T(8,128)(2,1)S(1)} %collective-permute-done.45), channel_id=1, source_target_pairs={{0,1},{1,0},{2,3},{3,2},{4,5},{5,4},{6,7},{7,6},{8,9},{9,8},{10,11... | collective-permute-start | bytes 2359304 | tf_op jit(solution)/shard_map/ppermute | solution.py:39
  (153 other events, 1195.1 us)

commit v3 on v2

--- a/solution.py
+++ b/solution.py
@@ -9,6 +9,7 @@
 
 epsilon = 1e-05
 pieces = 8
+chunks = 1
 lanes = 128
 far = 1e6
 log2e = 1.4426950408889634
@@ -58,16 +59,14 @@
     return lax.optimization_barrier((value, others))[0]
 
 
-def sum_all(value, axes):
-    for axis, mask in axes:
-        value = (value.astype(f32) + swap(value, axis, mask).astype(f32)).astype(bf16)
-    return value
+def sum_step(value, bit, *others):
+    got = after(swap(value, *bit), *others)
+    return (value.astype(f32) + got.astype(f32)).astype(bf16)
 
 
 class Scatter:
     def __init__(self, value, order, whole):
-        value = value.astype(bf16)
-        self.terms = [value.reshape((2,) * len(whole) + (-1,) + value.shape[1:])]
+        self.terms = [value.astype(bf16).reshape((2,) * len(whole) + value.shape[1:])]
         self.order = list(order)
         self.left = list(whole)
 
@@ -75,40 +74,48 @@
         axis, mask = self.order.pop(0)
         at = self.left.index((axis, mask))
         self.left.pop(at)
-        mine = bit_is_set(axis, mask)
-        if others:
-            self.terms[-1] = after(self.terms[-1], *others)
-        away = [lax.dynamic_index_in_dim(t, 1 - mine, at, keepdims=False) for t in self.terms]
-        away = sum(t.astype(f32) for t in away).astype(bf16)
-        self.terms = [
-            lax.dynamic_index_in_dim(t, mine, at, keepdims=False) for t in self.terms
-        ]
-        self.terms.append(swap(away, axis, mask))
+        mine = after(bit_is_set(axis, mask), *others)
+
+        def part(term, which):
+            return lax.dynamic_index_in_dim(term, which, at, keepdims=False)
+
+        away = sum(part(t, 1 - mine).astype(f32) for t in self.terms).astype(bf16)
+        self.terms = [part(t, mine) for t in self.terms] + [swap(away, axis, mask)]
         return away
+
+    @property
+    def got(self):
+        return self.terms[-1]
 
     def total(self, *others):
         while self.order:
             self.send(*others)
-        if others:
-            self.terms[-1] = after(self.terms[-1], *others)
+        self.terms[-1] = after(self.terms[-1], *others)
         return sum(t.astype(f32) for t in self.terms)
 
 
-def chan_scatter(part, fill=lambda begun: ()):
-    third = swap(part(3), "chan", 1)
-    middle = (part(2).astype(f32) + third.astype(f32)).astype(bf16)
-    second = swap(middle, "chan", 2)
-    first = swap(part(1), "chan", 1)
-    own = part(0)
-    second = after(second, own, *fill(middle))
-    return own.astype(f32) + first.astype(f32) + second.astype(f32)
-
-
-def chan_gather(own, fill=lambda begun: ()):
-    across = swap(own, "chan", 2)
-    beside = swap(own, "chan", 1)
-    across = after(across, *fill(beside))
-    return [own, beside, across, swap(across, "chan", 1)]
+class chan_scatter:
+    def __init__(self, part):
+        third = swap(part(3), "chan", 1)
+        self.middle = (part(2).astype(f32) + third.astype(f32)).astype(bf16)
+        self.second = swap(self.middle, "chan", 2)
+        self.first = swap(part(1), "chan", 1)
+        self.own = part(0)
+
+    def total(self, *others):
+        second = after(self.second, self.first, *others)
+        return self.own.astype(f32) + self.first.astype(f32) + second.astype(f32)
+
+
+class chan_gather:
+    def __init__(self, own):
+        self.own = own
+        self.across = swap(own, "chan", 2)
+        self.beside = swap(own, "chan", 1)
+
+    def blocks(self, *others):
+        across = after(self.across, self.beside, *others)
+        return [after(self.own, across), self.beside, across, swap(across, "chan", 1)]
 
 
 def in_order(own, beside):
@@ -197,11 +204,16 @@
     product_total[...] = jnp.exp2(dec[...] * jnp.sum(total, axis=0, keepdims=True))
 
 
-def forward_kernel(
-    size, rank, rates, mixed, proj, dec, ends, sums, arriving, gate_in, skip, *rest
-):
-    gated, summed, before, both, eb, rb, fb, start, scanned = rest
-    steps = rates.shape[0] // pieces
+def forward_kernel(size, rank, opening, rates, mixed, proj, dec, gate_in, skip, *rest):
+    if opening:
+        ends, sums, arriving = rest[:3]
+    else:
+        begin = rest[0]
+    gated, summed, before, final, both, eb, rb, fb, start, scanned = rest[-10:]
+    steps = rates.shape[1]
+    rates, mixed, proj, gate_in = (
+        item.reshape(pieces * steps, lanes) for item in (rates, mixed, proj, gate_in)
+    )
 
     @pl.when(pl.program_id(0) == 0)
     def _():
@@ -211,10 +223,12 @@
         spread(both, fb, 0, 1)
 
     decays = decay_rows(dec, size)
-    reached = arriving[...]
-    for s in range(pieces):
-        start[:, s, :] = reached
-        reached = ends[:, s, :] + jnp.exp2(dec[...] * sums[s : s + 1, :]) * reached
+    if opening:
+        reached = arriving[...]
+        for s in range(pieces):
+            start[:, s, :] = reached
+            reached = ends[:, s, :] + jnp.exp2(dec[...] * sums[s : s + 1, :]) * reached
+        begin = start
 
     def body(i, states):
         rows = pl.ds(pl.multiple_of(i * 2 * pieces, 2 * pieces), 2 * pieces)
@@ -240,20 +254,19 @@
         scanned[second, :] = high
         return tuple(out)
 
-    states = lax.fori_loop(0, steps // 2, body, tuple(start[n] for n in range(size)))
+    states = lax.fori_loop(0, steps // 2, body, tuple(begin[n] for n in range(size)))
     for n in range(size):
+        final[n] = states[n]
         last = jnp.concatenate([states[n], states[n]], axis=0).astype(bf16)
         before[n, pl.ds(steps * pieces, 2 * pieces), :] = last
 
-    def finish(i, unused):
-        rows = pl.ds(pl.multiple_of(i * 64, 64), 64)
+    tall = min(256, steps * pieces)
+    for k in range(steps * pieces // tall):
+        rows = pl.ds(k * tall, tall)
         total = scanned[rows, :] + skip[...] * mixed[rows, :]
         gate = gate_in[rows, :]
         gated[rows, :] = (total * (gate * jax.nn.sigmoid(gate))).astype(bf16)
         summed[rows, :] = total.astype(bf16)
-        return unused
-
-    lax.fori_loop(0, steps * pieces // 64, finish, 0)
 
 
 def heads_kernel(size, rank, rates, slope, proj, dec, sums, heads, head_total, *scratch):
@@ -298,11 +311,11 @@
     heads,
     sums,
     leaving,
-    before,
-    skip,
-    step_proj,
     *rest,
 ):
+    stored_states = rest[:chunks]
+    skip, step_proj = rest[chunks : chunks + 2]
+    rest = rest[chunks + 2 :]
     pre_low, direct, proj_grad, decay_grad, bias_grad = rest[:5]
     both, eb, rb, fb, stop, decay_sum, entry_terms, readout_terms = rest[5:13]
     picks, rate_grad, drive_grad, terms_grad = rest[13:]
@@ -329,11 +342,15 @@
         reached = heads[:, s, :] + jnp.exp2(dec[...] * sums[s : s + 1, :]) * reached
     decay_sum[...] = jnp.zeros_like(decay_sum)
 
-    def body(fresh, i, carried):
-        half = steps // 2 - 1 - i
-        at = pl.multiple_of(half * pair, pair)
-        rows = pl.ds(at, pair)
+    span = steps // 2 // chunks
+
+    def body(fresh, before, offset, i, carried):
+        place = span - 1 - i
+        at = pl.multiple_of(place * pair, pair)
+        stored = pl.ds(at, pair)
         following = pl.ds(at + pair, pair)
+        half = offset + place
+        rows = pl.ds(pl.multiple_of(half * pair, pair), pair)
         first, second = step_rows(2 * half, steps), step_rows(2 * half + 1, steps)
         rate0, rate1 = rates[first, :], rates[second, :]
         push0, push1 = rate0 * mixed[first, :], rate1 * mixed[second, :]
@@ -346,7 +363,7 @@
         for n in range(size):
             entry = eb[n, rows, :]
             readout = rb[n, rows, :]
-            state = before[n, rows, :].astype(f32)
+            state = before[n, stored, :].astype(f32)
             later = before[n, following, :].astype(f32)[:pieces]
             held1 = carried[n] + readout[pieces:] * grad1
             passed1 = held1 * jnp.exp2(far1 * decays[n])
@@ -374,8 +391,10 @@
         return tuple(out)
 
     def sweep(fresh):
-        edges = tuple(stop[n] for n in range(size))
-        lax.fori_loop(0, steps // 2, functools.partial(body, fresh), edges)
+        carried = tuple(stop[n] for n in range(size))
+        for k in reversed(range(chunks)):
+            step = functools.partial(body, fresh, stored_states[k], k * span)
+            carried = lax.fori_loop(0, span, step, carried)
 
     pl.when(group == 0)(lambda: sweep(True))
     pl.when(group > 0)(lambda: sweep(False))
@@ -427,14 +446,15 @@
     sums = pl.BlockSpec((pieces, lanes), lambda g: (0, g))
     line = pl.BlockSpec((1, lanes), lambda g: (0, g))
     square = pl.BlockSpec((lanes, lanes), lambda g: (0, g))
-    states = pl.BlockSpec((size, count + 2 * pieces, lanes), lambda g: (0, 0, g))
+    run = count // pieces // chunks
+    states = pl.BlockSpec((size, pieces * run + 2 * pieces, lanes), lambda g: (0, 0, g))
     shape = jax.ShapeDtypeStruct
     tall_out = shape((count, channels), f32)
     tall_low = shape((count, channels), bf16)
     small_out = shape((size, channels), f32)
     ends_out = shape((size, pieces, channels), f32)
     sums_out = shape((pieces, channels), f32)
-    states_out = shape((size, count + 2 * pieces, channels), bf16)
+    states_out = shape((size, pieces * run + 2 * pieces, channels), bf16)
     fixed_out = shape((count, lanes), f32)
     line_out = shape((1, channels), f32)
     both = pltpu.VMEM((count, 2 * lanes), bf16)
@@ -462,11 +482,35 @@
             name=name,
         )
 
+    def forward_call(k):
+        rows = pl.BlockSpec((pieces, run, lanes), lambda g: (0, k, g))
+        same = pl.BlockSpec((pieces, run, lanes), lambda g: (0, k, 0))
+        part = pl.BlockSpec((pieces * run, lanes), lambda g: (0, g))
+        part_out = shape((pieces * run, channels), bf16)
+        wide_part = pltpu.VMEM((size, pieces * run, lanes), f32)
+        thin_part = pltpu.VMEM((1, pieces * run, lanes), f32)
+        both_part = pltpu.VMEM((pieces * run, 2 * lanes), bf16)
+        own_part = pltpu.VMEM((pieces * run, lanes), f32)
+        begin = [ends] if k else [ends, sums, small]
+
+        def kernel(size, rank, *refs):
+            forward_kernel(size, rank, k == 0, *refs)
+
+        return call(
+            kernel,
+            "scan_forward",
+            [rows, rows, same, small, rows, line] + begin,
+            [part, part, states, ends],
+            [part_out, part_out, states_out, ends_out],
+            [both_part, wide_part, wide_part, thin_part, edge, own_part],
+        )
+
     def backward_call(first, span):
         def moved(spec):
             return pl.BlockSpec(spec.block_shape, lambda g: spec.index_map(g + first))
 
-        ins = [tall, tall, tall, fixed, small, ends, sums, small, states, line, square]
+        ins = [tall, tall, tall, fixed, small, ends, sums, small]
+        ins += [states] * chunks + [line, square]
         outs = [tall, tall, fixed, small, line]
         kept = [0, 1, 3, 4] if first else []
         aliases = {len(ins) + i: out for i, out in enumerate(kept)}
@@ -498,14 +542,7 @@
             [ends_out, sums_out, small_out, small_out],
             [both, wide, thin],
         ),
-        call(
-            forward_kernel,
-            "scan_forward",
-            [tall, tall, fixed, small, ends, sums, small, tall, line],
-            [tall, tall, states],
-            [tall_low, tall_low, states_out],
-            [both, wide, wide, thin, edge, own],
-        ),
+        tuple(forward_call(k) for k in range(chunks)),
         call(
             heads_kernel,
             "scan_heads",
@@ -585,7 +622,6 @@
     size = decay_log.shape[1]
     channels = input_proj.shape[1]
     quarter = count // lax.axis_size("chan")
-    half = count // 2
     me = lax.axis_index("chan")
     place = lax.axis_index("seq")
     dp_bits = [("dp", mask) for mask in bits_of("dp")]
@@ -598,11 +634,16 @@
     def block(values, r):
         return lax.dynamic_slice_in_dim(values, (me ^ r) * quarter, quarter)
 
-    def own_half(values, r):
-        return lax.dynamic_slice_in_dim(values, ((me >> 1) ^ r) * half, half)
+    shards = lax.axis_size("dp") * lax.axis_size("seq")
 
     def scatter(value, order):
-        return Scatter(value, order, shard_bits)
+        return Scatter(value.reshape(shards, -1, value.shape[-1]), order, shard_bits)
+
+    def side(values, r):
+        return lax.dynamic_slice_in_dim(values, ((me >> 1) ^ r) * 2 * quarter, 2 * quarter)
+
+    def of_side(values, r):
+        return lax.dynamic_slice_in_dim(values, ((me ^ r) & 1) * quarter, quarter)
 
     padded_ids = jnp.concatenate([jnp.full((width - 1,), -1, jnp.int32), segment_ids[0]], axis=0)
     window_ids = lax.dynamic_slice_in_dim(padded_ids, place * count, count + width - 1)
@@ -634,12 +675,12 @@
     )
     mixed = jax.nn.silu(convolved).astype(bf16)
     mixed_wide = mixed.astype(f32)
-    upper_halves = [own_half(upper, r) for r in range(2)]
+    upper_parts = [lax.optimization_barrier(side(upper, r)) for r in range(2)]
     grad_actives = []
 
     def upstream_parts(begun):
         grad_actives.extend(
-            transposed_right(after(item, begun), hidden_down) for item in upper_halves
+            transposed_right(after(item, begun), hidden_down) for item in upper_parts
         )
         return grad_actives
 
@@ -655,98 +696,92 @@
     ends, sums, end_total, product_total = scan_ends(rates, mixed_wide, scan_proj, decay_two)
     arriving = chained(product_total, end_total, 1)
     skip = skip_gain.astype(f32)[None]
-    gated, ssm_sum, before = scan_forward(
-        rates, mixed_wide, scan_proj, decay_two, ends, sums, arriving, gate_in, skip
-    )
-
-    hidden_sum = chan_scatter(lambda r: matmul(block(gated, r), output_proj).astype(bf16))
+
+    def at_home(blocks, dtype):
+        out = jnp.zeros((count, features), dtype)
+        for r, item in enumerate(blocks):
+            out = lax.dynamic_update_slice_in_dim(out, item.astype(dtype), (me ^ r) * quarter, 0)
+        return out
+
+    scan3 = [item.reshape(pieces, -1, item.shape[-1]) for item in (rates, mixed_wide, scan_proj)]
+    gate3 = gate_in.reshape(pieces, -1, channels)
+    gated, summed, before, unused = scan_forward[0](
+        *scan3, decay_two, gate3, skip, ends, sums, arriving
+    )
+
+    def output_part(r):
+        return matmul(side(gated, r), output_proj).astype(bf16)
+
+    far_part = output_part(1)
+    near_part = output_part(0)
+    hidden = chan_scatter(lambda r: of_side(far_part if r > 1 else near_part, r))
     rows_own = block(rows, 0).astype(f32)
     upper_own = block(upper, 0).astype(f32)
-    hidden_one = rows_own + hidden_sum
+    hidden_one = rows_own + hidden.total()
     scale_two, unit_two = unit_of(hidden_one)
-
-    def feed_forward(normed_part, grad_active):
+    normed_own = chan_gather((unit_two * gain_two).astype(bf16))
+
+    def feed_forward(blocks, r):
+        normed_part = lax.optimization_barrier(in_order(*blocks))
         gate_ffn = matmul(normed_part, hidden_gate)
         up_ffn = matmul(normed_part, hidden_up)
         gate_act_ffn = jax.nn.silu(gate_ffn)
         active = (gate_act_ffn * up_ffn).astype(bf16)
+        grad_active = grad_actives[r]
         grad_gate_ffn = (grad_active * up_ffn * silu_slope(gate_ffn)).astype(bf16)
         grad_up_ffn = (grad_active * gate_act_ffn).astype(bf16)
         grad_normed = (
             transposed_right(grad_gate_ffn, hidden_gate) + transposed_right(grad_up_ffn, hidden_up)
         ).astype(bf16)
-        return active, grad_gate_ffn, grad_up_ffn, grad_normed
-
-    halves = []
-
-    def half_forward(own, beside, r):
-        normed_half = lax.optimization_barrier(in_order(own, beside))
-        halves.append((normed_half,) + feed_forward(normed_half, grad_actives[r]))
-        return halves[-1]
-
-    normed_own = (unit_two * gain_two).astype(bf16)
-    normed_blocks = chan_gather(normed_own, lambda beside: half_forward(normed_own, beside, 0))
-    half_forward(*normed_blocks[2:], 1)
-
-    def quarter_of(items, r):
-        return lax.dynamic_slice_in_dim(items[r // 2], ((me ^ r) & 1) * quarter, quarter)
-
+        return normed_part, active, grad_gate_ffn, grad_up_ffn, grad_normed
+
+    ffn0 = feed_forward([normed_own.own, normed_own.beside], 0)
+    ffn1 = feed_forward(normed_own.blocks(ffn0)[2:], 1)
+    back = chan_scatter(lambda r: of_side((ffn1 if r > 1 else ffn0)[4], r))
     normed_two, active, grad_gate_ffn, grad_up_ffn = (
-        jnp.concatenate([item[k] for item in halves], axis=0) for k in range(4)
-    )
-    upper_two = jnp.concatenate(upper_halves, axis=0)
-    ffn_sums = []
-
-    def ffn_weights(begun):
-        left, right = after((normed_two, upper_two), begun)
-        sent = []
-        for value, order in (
-            (transposed_left(left, grad_up_ffn), usual),
-            (transposed_left(left, grad_gate_ffn), usual),
-            (transposed_left(right, active), other),
-        ):
-            ffn_sums.append(scatter(value, order))
-            sent.append(ffn_sums[-1].send())
-        return sent
-
-    grad_normed_two = chan_scatter(
-        lambda r: quarter_of([item[4] for item in halves], r), ffn_weights
-    )
+        jnp.concatenate([ffn0[k], ffn1[k]], axis=0) for k in range(4)
+    )
+    upper_two = jnp.concatenate(upper_parts, axis=0)
+    up_sum = scatter(transposed_left(after(normed_two, back.middle), grad_up_ffn), usual)
+    sent = up_sum.send()
+    gate_ffn_sum = scatter(transposed_left(after(normed_two, sent), grad_gate_ffn), usual)
+    sent = gate_ffn_sum.send()
+    down_sum = scatter(transposed_left(after(upper_two, sent), active), other)
+    sent = down_sum.send()
+    ffn_sums = [up_sum, gate_ffn_sum, down_sum]
+    grad_normed_two = back.total(sent)
     grad_unit_two = grad_normed_two * gain_two
     grad_hidden = upper_own + scale_two * (
         grad_unit_two - unit_two * jnp.mean(grad_unit_two * unit_two, axis=-1, keepdims=True)
     )
-
-    def placed(blocks, dtype):
-        whole = jnp.zeros((count, features), dtype)
-        for r, item in enumerate(blocks):
-            whole = lax.dynamic_update_slice_in_dim(
-                whole, item.astype(dtype), (me ^ r) * quarter, 0
-            )
-        return whole
-
-    results = []
-
-    def result_parts(begun):
-        for item in halves:
-            results.append(matmul(after(item[1], begun), hidden_down).astype(bf16))
-        results.append(swap(quarter_of(results, 3), "chan", 1))
-        results.append(swap(quarter_of(results, 1), "chan", 1))
-        return results[:2]
-
-    hidden_low = placed(chan_gather(grad_hidden.astype(bf16), result_parts), bf16)
-    result_middle = (
-        quarter_of(results, 2).astype(f32) + after(results[2], hidden_low).astype(f32)
-    ).astype(bf16)
-    result_far = swap(result_middle, "chan", 2)
+    low = chan_gather(grad_hidden.astype(bf16))
+    result_parts = [
+        matmul(after(item[1], low.own), hidden_down).astype(bf16) for item in (ffn0, ffn1)
+    ]
+    hidden_blocks = low.blocks(result_parts)
+    hidden_low = at_home(hidden_blocks, bf16)
+    own_part = (of_side(result_parts[0], 0).astype(f32) + hidden_one).astype(bf16)
+    upper_chip = me >> 1
+    near_rows = lax.dynamic_update_slice_in_dim(
+        result_parts[0], own_part, (me & 1) * quarter, 0
+    )
+    result_rows = jnp.concatenate(
+        [
+            jnp.where(upper_chip == 1, result_parts[1], near_rows),
+            jnp.where(upper_chip == 1, near_rows, result_parts[1]),
+        ],
+        axis=0,
+    )
+    result = lax.psum(after(result_rows, hidden_blocks[3]), "chan")
     gate_act = jax.nn.silu(gate_in)
     grad_gated = transposed_right(hidden_low, output_proj)
     grad_scanned = grad_gated * gate_act
-    grad_gate_in = (grad_gated * ssm_sum.astype(f32) * silu_slope(gate_in)).astype(bf16)
+    grad_gate_in = (grad_gated * summed.astype(f32) * silu_slope(gate_in)).astype(bf16)
     skip_grad = jnp.sum(grad_scanned * mixed_wide, axis=0)
     heads, head_total = scan_heads(
-        rates, after(grad_scanned, result_middle), scan_proj, decay_two, sums
-    )
+        rates, grad_scanned, scan_proj, decay_two, sums
+    )
+    head_total = after(head_total, [item.got for item in ffn_sums])
 
     mixer_sums = []
 
@@ -762,18 +797,10 @@
 
     leaving = chained(product_total, head_total, -1, [output_weights, gate_weights])
     sent = [item.send(leaving) for item in ffn_sums]
-    result_sum = (
-        quarter_of(results, 0).astype(f32)
-        + results[3].astype(f32)
-        + after(result_far, leaving).astype(f32)
-    )
-    result_own = (hidden_one + result_sum).astype(bf16)
-    result_across = swap(result_own, "chan", 2)
-    result_beside = swap(result_own, "chan", 1)
     step_padded = jnp.pad(step_proj, ((0, 2 * size), (0, 0)))
     scan_inputs = (rates, mixed_wide, grad_scanned, scan_proj, decay_two, heads, sums)
     first_scan, second_scan = scan_backward
-    begin = after(leaving, sent, result_own)
+    begin = after(leaving, sent)
     parts = first_scan(*scan_inputs, begin, before, skip, step_padded)
     terms = parts[2]
     sent = [item.send(terms) for item in ffn_sums]
@@ -782,26 +809,22 @@
     pre_low, direct, more_terms, decay_grad, step_bias_grad = second_scan(
         *scan_inputs, begin, before, skip, step_padded, *kept
     )
-    arrived = [item.terms[-1] for item in ffn_sums[:2] + mixer_sums]
-    more_terms = after(more_terms, arrived, result_across)
+    more_terms = after(more_terms, [item.got for item in ffn_sums[:2] + mixer_sums], result)
     proj_terms = terms + more_terms
 
     step_weight_grad = []
 
-    def step_weights():
-        step_weight_grad.append(transposed_left(step_low, pre_low).astype(bf16))
-        return step_weight_grad
-
-    results_whole = []
-
-    def result_place(begun):
-        sent = [item.send(begun) for item in mixer_sums]
-        across = after(result_across, begun, *sent)
-        blocks = [result_own, result_beside, across, swap(across, "chan", 1)]
-        results_whole.append(placed(blocks, bf16))
-        return results_whole + [ffn_sums[2].terms[-1]]
-
-    grad_projected = chan_total(proj_terms, step_weights, result_place).astype(bf16)
+    def mixer_round():
+        return [item.send() for item in mixer_sums]
+
+    gate_terms = []
+
+    def step_weights(begun):
+        step_weight_grad.append(transposed_left(after(step_low, begun), pre_low).astype(bf16))
+        gate_terms.append(transposed_right(after(grad_gate_in, begun), gate_proj).astype(bf16))
+        return step_weight_grad + gate_terms
+
+    grad_projected = chan_total(proj_terms, mixer_round, step_weights).astype(bf16)
     grad_mixed = transposed_right(grad_projected, state_proj) + direct
     grad_conv = grad_mixed * silu_slope(convolved)
     conv_bias_grad = jnp.sum(grad_conv, axis=0)
@@ -831,8 +854,6 @@
         ],
         axis=0,
     )
-    shards = lax.axis_size("dp") * lax.axis_size("seq")
-    shard = lax.axis_index("dp") * lax.axis_size("seq") + place
     low_rows = rank // shards
     low_parts = jnp.concatenate(
         [
@@ -846,77 +867,97 @@
         + jnp.pad(after(returned, low_parts), ((count - width + 1, 0), (0, 0)))
     ).astype(bf16)
 
+    lines = jnp.concatenate([state_grad[rank:], few.astype(bf16)], axis=0)
+    lines_used = lines.shape[0]
+
+    lines_used = lines.shape[0]
+
+    def token_part(r, sent):
+        return (
+            transposed_right(block(after(inner_low, sent), r), input_proj)
+            + transposed_right(block(after(grad_gate_in, proj_terms), r), gate_proj)
+        ).astype(bf16)
+
+    share = features // shards
+
     def token_part(r):
-        return (
-            transposed_right(block(inner_low, r), input_proj)
-            + transposed_right(block(grad_gate_in, r), gate_proj)
-        ).astype(bf16)
-
+        product = transposed_right(side(inner_low, r), input_proj)
+        return (product + side(gate_terms[0], r).astype(f32)).astype(bf16)
+
+    far_part = token_part(1)
+    near_part = token_part(0)
+    tokens_sum = chan_scatter(lambda r: of_side(far_part if r > 1 else near_part, r))
+    scale_one, unit_one = unit_of(rows_own)
+
+    input_weight = transposed_left(normed, after(inner_low, tokens_sum.middle)).astype(bf16)
+    half_width = channels // 2
+    input_blocks = input_weight.reshape(shards, share, channels)
     input_sums = []
-
-    def third_round(begun):
-        value = transposed_left(normed, after(inner_low, begun)).astype(bf16)
-        sent = []
-        value = jnp.concatenate([value.reshape(shards, -1, channels), low_parts], axis=1)
-        for k, order in ((0, usual), (1, other)):
-            part = value[:, :, k * (channels // 2) : (k + 1) * (channels // 2)]
-            input_sums.append(scatter(part.reshape(-1, channels // 2), order))
-            sent.append(input_sums[-1].send())
-        return (
-            sent
-            + [item.send(*sent) for item in mixer_sums]
-            + [item.total(*sent) for item in ffn_sums]
-        )
-
-    grad_normed = chan_scatter(token_part, third_round)
-    scale_one, unit_one = unit_of(rows_own)
-    gain_one_grad = jnp.sum(grad_normed * unit_one, axis=0)
-    gain_two_grad = jnp.sum(grad_normed_two * unit_two, axis=0)
+    sent = []
+    for k, order in ((0, usual), (1, other)):
+        columns = slice(k * half_width, (k + 1) * half_width)
+        value = jnp.concatenate([input_blocks[:, :, columns], low_parts[:, :, columns]], axis=1)
+        value = jnp.pad(value, ((0, 0), (0, -value.shape[1] % 16), (0, 0)))
+        input_sums.append(Scatter(value, order, shard_bits))
+        sent.append(input_sums[-1].send())
+    grad_normed = tokens_sum.total(sent)
     grad_unit_one = grad_normed * gain_one
     tokens_grad = grad_hidden + scale_one * (
         grad_unit_one - unit_one * jnp.mean(grad_unit_one * unit_one, axis=-1, keepdims=True)
     )
-    last = []
-
-    def fourth_round(begun):
-        last.extend(item.send(begun) for item in input_sums)
-        gains = jnp.concatenate([gain_one_grad, gain_two_grad]).astype(bf16)
-        gains = sum_all(gains, [("chan", 1), ("chan", 2)]).reshape(-1, channels)
-        lines = jnp.concatenate([state_grad[rank:], few.astype(bf16), gains], axis=0)
-        padded = jnp.pad(lines, ((0, -lines.shape[0] % 16), (0, 0)))
-        last.extend(item.total(begun, *last) for item in mixer_sums)
-        last.append(sum_all(padded, shard_bits).astype(f32))
-        return last
-
-    tokens_out = placed(chan_gather(tokens_grad.astype(bf16), fourth_round), f32)
-    vectors = last[-1]
-    input_parts = jnp.concatenate([item.total() for item in input_sums], axis=1)
-    input_rows = features // shards
-
-    def share(first):
-        whole = vectors[first : first + features // channels].reshape(features)
-        return lax.dynamic_slice_in_dim(whole, shard * input_rows, input_rows)
-
+    tokens_last = chan_gather(tokens_grad.astype(bf16))
+    gains = jnp.concatenate(
+        [jnp.sum(grad_normed * unit_one, axis=0), jnp.sum(grad_normed_two * unit_two, axis=0)]
+    )
+    gains = gains.reshape(-1, channels).astype(bf16)
+    sent = [item.send(tokens_last.own) for item in mixer_sums]
+    done = [item.total(sent) for item in ffn_sums[:2]]
+    blocks = tokens_last.blocks(done)
+    sent = [item.send(blocks[2]) for item in input_sums]
+    for mask in (1, 2):
+        gains = sum_step(gains, ("chan", mask), sent)
+    vectors = jnp.concatenate([lines, gains], axis=0)
+    vectors = jnp.pad(vectors, ((0, -vectors.shape[0] % 16), (0, 0)))
+    vectors = sum_step(vectors, shard_bits[0])
+    tokens_out = at_home(blocks, f32)
+    done.append(ffn_sums[2].total(blocks[3]))
+    while input_sums[0].order:
+        sent = [item.send(blocks[3]) for item in input_sums]
+    for bit in shard_bits[1:]:
+        vectors = sum_step(vectors, bit, sent)
+    done += [item.total(sent) for item in mixer_sums]
+    input_parts = [item.total(done) for item in input_sums]
+    first = share + 2 * low_rows
+    gains = vectors[lines_used:].astype(f32)
+    shard = lax.axis_index("dp") * lax.axis_size("seq") + place
+
+    def gain_share(k):
+        lines = features // channels
+        line = gains[k * lines : (k + 1) * lines].reshape(features)
+        return lax.dynamic_slice_in_dim(line, shard * share, share)
+
+    input_parts = jnp.concatenate([item[:first] for item in input_parts], axis=1)
+    vectors = vectors.astype(f32)
     at = 2 * size
     return (
-        results_whole[0][None],
+        result[None],
         tokens_out[None],
-        share(at + width + size + 3),
-        input_parts[:input_rows],
-        mixer_sums[1].total(),
+        gain_share(0),
+        input_parts[:share],
+        done[4],
         vectors[at : at + width].T,
         vectors[at + width],
-        input_parts[input_rows : input_rows + low_rows].T,
+        input_parts[share : share + low_rows].T,
         vectors[:at].T,
-        input_parts[input_rows + low_rows :],
+        input_parts[share + low_rows :],
         vectors[at + width + 1],
         vectors[at + width + 2 : at + width + 2 + size].T,
         vectors[at + width + size + 2],
-        mixer_sums[0].total().T,
-        share(at + width + size + 3 + features // channels),
-        ffn_sums[1].total(),
-        ffn_sums[0].total(),
-        ffn_sums[2].total().T,
+        done[3].T,
+        gain_share(1),
+        done[1],
+        done[0],
+        done[2].T,
     )
 
 

time: 588 us -> 563 us (0.957)
  waiting for transfers between devices: 125 us -> 83.7 us
  between operations: 3 us -> 16.2 us
  other arithmetic: 88.9 us -> 101 us
  matrix products: 102 us -> 91.8 us
    ppermute x54 -> x48, waiting for transfers between devices: 115 us -> 73.6 us  [swap(): lax.ppermute(value, axis, [(i, i ^ mask) for i in range(lax.axis_size(axi...]
    convert_element_type x23 -> x27, other arithmetic: 28.4 us -> 41 us  [the longest x14 28.4 us: send(): away = sum((part(t, 1 - mine).astype(f32) for t in self.terms)).astype(bf16)]
    dot_general x14 -> x12, matrix products: 42.3 us -> 35.9 us  [matmul(): return jnp.dot(left, right, preferred_element_type=f32)]
    dot_general x16 -> x11, matrix products: 37.3 us -> 31.4 us  [transposed_right(): lax.dot_general(left, right, (((1,), (1,)), ((), ())), preferred_element_...]
    add x7 -> x6, other arithmetic: 13.9 us -> 11.5 us  [total(): return sum((t.astype(f32) for t in self.terms))]
    unnamed x250 -> x224, local copies, waits for them, and re-layouts: 21.6 us -> 23.7 us
    ppermute x54 -> x48, starting transfers between devices: 40.6 us -> 40.1 us  [swap(): lax.ppermute(value, axis, [(i, i ^ mask) for i in range(lax.axis_size(axi...]
  transfers between devices with their start and end apart: 60 -> 55, of which waited for: 26 -> 18; matrix products, arithmetic and copies ran while one was open for 29% -> 33% of each run, Pallas kernels for 16% -> 16%
where the time goes in v3:
time: 563 us; the launch traced here: 552 us
  Pallas kernels  145 us (26%)
  other arithmetic  101 us (18%)
  matrix products  91.8 us (16%)
  waiting for transfers between devices  83.7 us (15%)
  starting transfers between devices  58.2 us (10%)
  local copies, waits for them, and re-layouts  56.1 us (10%)
  between operations  16.2 us (3%)
    ppermute x48, waiting for transfers between devices, swap(): lax.ppermute(value, axis, [(i, i ^ mask) for i in range(lax.axis_size(axi...  73.6 us
    ppermute x48, starting transfers between devices, swap(): lax.ppermute(value, axis, [(i, i ^ mask) for i in range(lax.axis_size(axi...  40.1 us
    dot_general x12, matrix products, matmul(): return jnp.dot(left, right, preferred_element_type=f32)  35.9 us
    pallas_call x1, Pallas kernels, per_device(): second_scan(*scan_inputs, begin, before, skip, step_padded, *kept)  34.9 us
    pallas_call x1, Pallas kernels, per_device(): parts = first_scan(*scan_inputs, begin, before, skip, step_padded)  34.5 us
    dot_general x11, matrix products, transposed_right(): lax.dot_general(left, right, (((1,), (1,)), ((), ())), preferred_element_...  31.4 us
    pallas_call x1, Pallas kernels, per_device(): scan_forward[0](*scan3, decay_two, gate3, skip, ends, sums, arriving)  30.6 us
    convert_element_type x14, other arithmetic, send(): away = sum((part(t, 1 - mine).astype(f32) for t in self.terms)).astype(bf16)  28.4 us
  transfers between devices with their start and end apart: 55, of which 18 were waited for; matrix products, arithmetic and copies ran while one was open for 33% of the time, Pallas kernels for 16%

profile of v3, /device:TPU:0, one launch (start us, length us, event | category | flops | bytes accessed | tf_op | source)
XLA Modules:
  0.0 552.2 jit_solution(7794413657527555393)
XLA Ops:
  8.7 6.7 %norm_rows.1 = bf16[1024,1536]{1,0:T(8,128)(2,1)} custom-call(bf16[1024,1536]{1,0:T(8,128)(2,1)} %bitcast.353, f32[1,1536]{1,0:T(1,128)} %broadcast_in_dim.63.gain), custom_call_target="tpu_custom_call" | custom-call | flops 9437184 | bytes 6291456 | tf_op jit(solution)/shard_map/norm_rows/pallas_call | solution.py:666
  15.4 5.2 convolution_convert_fusion.11
  21.8 4.9 collective-permute-start
  26.7 6.9 %fusion.90 = f32[1024,768]{1,0:T(8,128)} fusion(bf16[1024,1536]{1,0:T(8,128)(2,1)} %norm_rows.1, bf16[1536,768]{1,0:T(8,128)(2,1)} %param.22), kind=kOutput, calls=%fused_computation.285 | convolution fusion | flops 2415919104 | bytes 8650752 | tf_op jit(solution)/shard_map/dot_general | solution.py:28
  35.8 4.2 fusion.86
  55.6 18.2 %scan_ends.1 = (f32[16,8,768]{2,1,0:T(8,128)}, f32[8,768]{1,0:T(8,128)}, f32[16,768]{1,0:T(8,128)}, f32[16,768]{1,0:T(8,128)}) custom-call(f32[1024,768]{1,0:T(8,128)} %compare_select_fusion.rates.refs_0_, f32[1024,768]{1,0:T(8,128)} %get-tuple-element.185.mixed.refs_1_, f32[1024,128]{1,0:T(8,128)} %broadcast_select_fusion.6.proj.refs_3_, ...), custom_call_target="tpu_custom_call" | custom-call | flops 12582912 | tf_op jit(solution)/shard_map/scan_ends/pallas_call | solution.py:696
  81.3 5.7 %collective-permute-start.4 = (f32[2,16,768]{2,1,0:T(8,128)S(1)}, f32[2,16,768]{2,1,0:T(8,128)S(1)}, u32[]{:S(2)}, u32[]{:S(2)}) collective-permute-start(f32[2,16,768]{2,1,0:T(8,128)S(1)} %pad_maximum_fusion.8), channel_id=1, source_target_pairs={{0,8},{4,12},{1,9},{5,13},{2,10},{6,14},{3,11},{7,15},{16,24},{20,... | collective-permute-start | bytes 294920 | tf_op jit(solution)/shard_map/ppermute | solution.py:45
  89.4 30.6 %scan_forward.1 = (bf16[1024,768]{1,0:T(8,128)(2,1)}, bf16[1024,768]{1,0:T(8,128)(2,1)}, bf16[16,1040,768]{2,1,0:T(8,128)(2,1)}, f32[16,8,768]{2,1,0:T(8,128)}) custom-call(f32[8,128,768]{2,1,0:T(8,128)} %bitcast.351, f32[8,128,768]{2,1,0:T(8,128)} %bitcast.350, f32[8,128,128]{2,1,0:T(8,128)} %bitcast.352, ...), custom_call_target="tpu_custom_call" | custom-call | flops 12582912 | tf_op jit(solution)/shard_map/scan_forward/pallas_call | solution.py:708
  134.4 18.2 %collective-permute-done.7 = bf16[256,1536]{1,0:T(8,128)(2,1)} collective-permute-done((bf16[256,1536]{1,0:T(8,128)(2,1)}, bf16[256,1536]{1,0:T(8,128)(2,1)}, u32[]{:S(2)}, u32[]{:S(2)}) %collective-permute-start.7) | collective-permute-done | bytes 786464 | tf_op jit(solution)/shard_map/ppermute | solution.py:40
  152.6 4.0 multiply_reduce_fusion.7
  167.9 3.7 multiply_convert_fusion.5
  198.0 3.7 convolution_convert_fusion.3
  204.6 3.7 convolution_convert_fusion.2
  210.3 3.9 convolution_convert_fusion.1
  218.2 3.6 fusion.84
  228.8 11.9 %collective-permute-done.14 = bf16[256,1536]{1,0:T(8,128)(2,1)S(1)} collective-permute-done((bf16[256,1536]{1,0:T(8,128)(2,1)S(1)}, bf16[256,1536]{1,0:T(8,128)(2,1)S(1)}, u32[]{:S(2)}, u32[]{:S(2)}) %collective-permute-start.14) | collective-permute-done | bytes 786464 | tf_op jit(solution)/shard_map/ppermute | solution.py:40
  248.0 5.9 %multiply_reduce_fusion = (bf16[768]{0:T(1024)(128)(2,1)}, f32[1024,768]{1,0:T(8,128)}, bf16[1024,768]{1,0:T(8,128)(2,1)}) fusion(bf16[1024,768]{1,0:T(8,128)(2,1)S(1)} %copy-done.5, f32[1024,768]{1,0:T(8,128)S(1)} %copy-done.25, bf16[1024,768]{1,0:T(8,128)(2,1)S(1)} %copy-done.97, bf16[1024,1536]{1,0:T(8,128)(2,1)S(1)} %constant_dynamic-update-slice_fusion, ...), kind=kOutput, calls=%fused_computation.18 | convolution fusion | flops 2428501248 | bytes 16516608 | tf_op jit(solution)/shard_map/dot_general | solution.py:36
  253.9 20.5 %scan_heads.1 = (f32[16,8,768]{2,1,0:T(8,128)}, f32[16,768]{1,0:T(8,128)}) custom-call(f32[1024,768]{1,0:T(8,128)} %compare_select_fusion.rates.refs_0_, f32[1024,768]{1,0:T(8,128)} %get-tuple-element.177.slope.refs_2_, f32[1024,128]{1,0:T(8,128)} %broadcast_select_fusion.6.proj.refs_3_, f32[16,768]{1,0:T(8,128)} %bitcast_multiply_fusion.4.dec.refs_3_.refs_4_, ...), custom_call_target="tpu_custom_call" | custom-call | flops 12582912 | tf_op jit(solution)/shard_map/scan_heads/pallas_call | solution.py:781
  276.5 5.4 convolution_convert_fusion.6
  291.8 3.5 collective-permute-done.21
  308.4 34.5 %scan_backward.2 = (bf16[1024,768]{1,0:T(8,128)(2,1)}, f32[1024,768]{1,0:T(8,128)}, f32[1024,128]{1,0:T(8,128)}, f32[16,768]{1,0:T(8,128)}, f32[1,768]{1,0:T(1,128)}) custom-call(f32[1024,768]{1,0:T(8,128)} %compare_select_fusion.rates.refs_0_, f32[1024,768]{1,0:T(8,128)} %get-tuple-element.185.mixed.refs_1_, f32[1024,768]{1,0:T(8,128)} %get-tuple-element.177.slope.refs_2_, ...), custom_call_target="tpu_custom_call" | custom-call | flops 12582912 | tf_op jit(solution)/shard_map/scan_backward/pallas_call | solution.py:804
  352.5 34.9 %scan_backward.3 = (bf16[1024,768]{1,0:T(8,128)(2,1)}, f32[1024,768]{1,0:T(8,128)}, f32[1024,128]{1,0:T(8,128)}, f32[16,768]{1,0:T(8,128)}, f32[1,768]{1,0:T(1,128)}) custom-call(f32[1024,768]{1,0:T(8,128)} %compare_select_fusion.rates.refs_0_, ...), custom_call_target="tpu_custom_call", output_to_operand_aliasing={{0}: (11, {}), {1}: (12, {}), {3}: (13, {}), {4}: (14, {})} | custom-call | flops 12582912 | tf_op jit(solution)/shard_map/scan_backward/pallas_call | solution.py:809
  400.3 4.2 convolution_convert_fusion
  409.9 6.0 %multiply_reduce_fusion.1 = (bf16[768]{0:T(1024)(128)(2,1)}, bf16[768]{0:T(1024)(128)(2,1)}, bf16[768]{0:T(1024)(128)(2,1)}, bf16[768]{0:T(1024)(128)(2,1)}, bf16[768]{0:T(1024)(128)(2,1)}, /*index=5*/f32[1024,768]{1,0:T(8,128)S(1)}) fusion(f32[1027,768]{1,0:T(8,128)S(1)} %copy-done.3, f32[1024]{0:T(1024)S(1)} %copy-done.58, f32[1024]{0:T(1024)S(1)} %copy-done.56, ...), kind=kLoop, calls=%fused_computation.19 | loop fusion | flops 16511232 | bytes 25185792 | tf_op jit(solution)/shard_map/reduce_sum | solution.py:833
  428.2 3.5 fusion.1
  441.8 11.6 %collective-permute-done.34 = bf16[256,1536]{1,0:T(8,128)(2,1)S(1)} collective-permute-done((bf16[256,1536]{1,0:T(8,128)(2,1)S(1)}, bf16[256,1536]{1,0:T(8,128)(2,1)S(1)}, u32[]{:S(2)}, u32[]{:S(2)}) %collective-permute-start.34) | collective-permute-done | bytes 786464 | tf_op jit(solution)/shard_map/ppermute | solution.py:40
  465.9 3.5 fusion.39
  469.4 4.3 collective-permute-done.35
  482.0 3.5 broadcast_in_dim.68
  499.7 10.4 %collective-permute-done.46 = bf16[2,224,384]{2,1,0:T(8,128)(2,1)} collective-permute-done((bf16[2,224,384]{2,1,0:T(8,128)(2,1)S(1)}, bf16[2,224,384]{2,1,0:T(8,128)(2,1)}, u32[]{:S(2)}, u32[]{:S(2)}) %collective-permute-start.46) | collective-permute-done | bytes 344096 | tf_op jit(solution)/shard_map/ppermute | solution.py:40
  514.3 7.1 %collective-permute-done.45 = bf16[64,768]{1,0:T(8,128)(2,1)S(1)} collective-permute-done((bf16[64,768]{1,0:T(8,128)(2,1)S(1)}, bf16[64,768]{1,0:T(8,128)(2,1)S(1)}, u32[]{:S(2)}, u32[]{:S(2)}) %collective-permute-start.45) | collective-permute-done | bytes 98336 | tf_op jit(solution)/shard_map/ppermute | solution.py:40
  541.0 3.9 copy.66
  (479 shorter events, 238.0 us)
Async XLA Ops:
  7.2 380.3 %all-reduce.12.cloned.1.call-start = ((), (), s32[]{:S(2)}) async-start(), calls=%async_computation | async-start | bytes 6291456 | tf_op jit(solution)/shard_map/psum | solution.py:775
  132.8 19.8 %collective-permute-start.7 = (bf16[256,1536]{1,0:T(8,128)(2,1)}, bf16[256,1536]{1,0:T(8,128)(2,1)}, u32[]{:S(2)}, u32[]{:S(2)}) collective-permute-start(bf16[256,1536]{1,0:T(8,128)(2,1)} %add_convert_fusion.3), channel_id=1, source_target_pairs={{0,2},{1,3},{2,0},{3,1},{4,6},{5,7},{6,4},{7,5},{8,10},{9,11},{10,... | collective-permute-start | bytes 2359304 | tf_op jit(solution)/shard_map/ppermute | solution.py:40
  159.1 20.3 %collective-permute-start.8 = (bf16[256,1536]{1,0:T(8,128)(2,1)}, bf16[256,1536]{1,0:T(8,128)(2,1)}, u32[]{:S(2)}, u32[]{:S(2)}) collective-permute-start(bf16[256,1536]{1,0:T(8,128)(2,1)} %multiply_convert_fusion.8), channel_id=1, source_target_pairs={{0,2},{1,3},{2,0},{3,1},{4,6},{5,7},{6,4},{7,5},{8,10},{9,11},{10,... | collective-permute-start | bytes 2359304 | tf_op jit(solution)/shard_map/ppermute | solution.py:40
  194.6 21.1 %collective-permute-start.11 = (bf16[256,1536]{1,0:T(8,128)(2,1)S(1)}, bf16[256,1536]{1,0:T(8,128)(2,1)S(1)}, u32[]{:S(2)}, u32[]{:S(2)}) collective-permute-start(bf16[256,1536]{1,0:T(8,128)(2,1)S(1)} %constant_dynamic-slice_fusion.3), channel_id=1, source_target_pairs={{0,1},{1,0},{2,3},{3,2},{4,5},{5,4},{6,7},{7,6},{8,9},{9,8},{10,11... | collective-permute-start | bytes 2359304 | tf_op jit(solution)/shard_map/ppermute | solution.py:40
  196.4 19.6 %collective-permute-start.13 = (bf16[256,1536]{1,0:T(8,128)(2,1)S(1)}, bf16[256,1536]{1,0:T(8,128)(2,1)S(1)}, u32[]{:S(2)}, u32[]{:S(2)}) collective-permute-start(bf16[256,1536]{1,0:T(8,128)(2,1)S(1)} %add_convert_fusion.2), channel_id=1, source_target_pairs={{0,2},{1,3},{2,0},{3,1},{4,6},{5,7},{6,4},{7,5},{8,10},{9,11},{10,... | collective-permute-start | bytes 2359304 | tf_op jit(solution)/shard_map/ppermute | solution.py:40
  203.1 71.2 %collective-permute-start.17 = (bf16[2,2,192,1024]{3,2,1,0:T(8,128)(2,1)}, bf16[2,2,192,1024]{3,2,1,0:T(8,128)(2,1)S(1)}, u32[]{:S(2)}, u32[]{:S(2)}) collective-permute-start(bf16[2,2,192,1024]{3,2,1,0:T(8,128)(2,1)} %dynamic-slice_bitcast_fusion.2), channel_id=1, source_target_pairs={{0,16},{16,0},{1,17},{17,1},{2,18},{18,2},{3,19},{19,3},{4,20},{20... | collective-permute-start | bytes 4718600 | tf_op jit(solution)/shard_map/ppermute | solution.py:40
  209.6 64.7 %collective-permute-start.18 = (bf16[2,2,192,1024]{3,2,1,0:T(8,128)(2,1)}, bf16[2,2,192,1024]{3,2,1,0:T(8,128)(2,1)}, u32[]{:S(2)}, u32[]{:S(2)}) collective-permute-start(bf16[2,2,192,1024]{3,2,1,0:T(8,128)(2,1)} %dynamic-slice_bitcast_fusion.1), channel_id=1, source_target_pairs={{0,16},{16,0},{1,17},{17,1},{2,18},{18,2},{3,19},{19,3},{4,20},{20... | collective-permute-start | bytes 4718600 | tf_op jit(solution)/shard_map/ppermute | solution.py:40
  215.7 58.6 %collective-permute-start.19 = (bf16[2,2,192,1024]{3,2,1,0:T(8,128)(2,1)}, bf16[2,2,192,1024]{3,2,1,0:T(8,128)(2,1)}, u32[]{:S(2)}, u32[]{:S(2)}) collective-permute-start(bf16[2,2,192,1024]{3,2,1,0:T(8,128)(2,1)} %dynamic-slice_bitcast_fusion), channel_id=1, source_target_pairs={{0,4},{4,0},{8,12},{12,8},{1,5},{5,1},{9,13},{13,9},{2,6},{6,2},{1... | collective-permute-start | bytes 4718600 | tf_op jit(solution)/shard_map/ppermute | solution.py:40
  221.9 18.8 %collective-permute-start.14 = (bf16[256,1536]{1,0:T(8,128)(2,1)S(1)}, bf16[256,1536]{1,0:T(8,128)(2,1)S(1)}, u32[]{:S(2)}, u32[]{:S(2)}) collective-permute-start(bf16[256,1536]{1,0:T(8,128)(2,1)S(1)} %get-tuple-element.107), channel_id=1, source_target_pairs={{0,2},{1,3},{2,0},{3,1},{4,6},{5,7},{6,4},{7,5},{8,10},{9,11},{10,... | collective-permute-start | bytes 2359304 | tf_op jit(solution)/shard_map/ppermute | solution.py:40
  223.4 17.3 %collective-permute-start.15 = (bf16[256,1536]{1,0:T(8,128)(2,1)S(1)}, bf16[256,1536]{1,0:T(8,128)(2,1)S(1)}, u32[]{:S(2)}, u32[]{:S(2)}) collective-permute-start(bf16[256,1536]{1,0:T(8,128)(2,1)S(1)} %get-tuple-element.107), channel_id=1, source_target_pairs={{0,1},{1,0},{2,3},{3,2},{4,5},{5,4},{6,7},{7,6},{8,9},{9,8},{10,11... | collective-permute-start | bytes 2359304 | tf_op jit(solution)/shard_map/ppermute | solution.py:40
  298.6 44.3 %collective-permute-start.23 = (bf16[2,192,1024]{2,1,0:T(8,128)(2,1)}, bf16[2,192,1024]{2,1,0:T(8,128)(2,1)S(1)}, u32[]{:S(2)}, u32[]{:S(2)}) collective-permute-start(bf16[2,192,1024]{2,1,0:T(8,128)(2,1)} %fusion.31), channel_id=1, source_target_pairs={{0,4},{4,0},{8,12},{12,8},{1,5},{5,1},{9,13},{13,9},{2,6},{6,2},{1... | collective-permute-start | bytes 2359304 | tf_op jit(solution)/shard_map/ppermute | solution.py:40
  300.9 47.0 %collective-permute-start.22 = (bf16[2,192,1024]{2,1,0:T(8,128)(2,1)}, bf16[2,192,1024]{2,1,0:T(8,128)(2,1)}, u32[]{:S(2)}, u32[]{:S(2)}) collective-permute-start(bf16[2,192,1024]{2,1,0:T(8,128)(2,1)} %fusion.32), channel_id=1, source_target_pairs={{0,4},{4,0},{8,12},{12,8},{1,5},{5,1},{9,13},{13,9},{2,6},{6,2},{1... | collective-permute-start | bytes 2359304 | tf_op jit(solution)/shard_map/ppermute | solution.py:40
  303.0 84.5 %collective-permute-start.27 = (bf16[2,2,192,768]{3,2,1,0:T(8,128)(2,1)S(1)}, bf16[2,2,192,768]{3,2,1,0:T(8,128)(2,1)}, u32[]{:S(2)}, u32[]{:S(2)}) collective-permute-start(bf16[2,2,192,768]{3,2,1,0:T(8,128)(2,1)S(1)} %copy-done.33), channel_id=1, source_target_pairs={{0,16},{16,0},{1,17},{17,1},{2,18},{18,2},{3,19},{19,3},{4,20},{20... | collective-permute-start | bytes 3538952 | tf_op jit(solution)/shard_map/ppermute | solution.py:40
  304.4 83.0 %collective-permute-start.28 = (bf16[2,2,192,768]{3,2,1,0:T(8,128)(2,1)}, bf16[2,2,192,768]{3,2,1,0:T(8,128)(2,1)}, u32[]{:S(2)}, u32[]{:S(2)}) collective-permute-start(bf16[2,2,192,768]{3,2,1,0:T(8,128)(2,1)} %dynamic-slice_bitcast_fusion.5), channel_id=1, source_target_pairs={{0,4},{4,0},{8,12},{12,8},{1,5},{5,1},{9,13},{13,9},{2,6},{6,2},{1... | collective-permute-start | bytes 3538952 | tf_op jit(solution)/shard_map/ppermute | solution.py:40
  307.0 43.3 %collective-permute-start.24 = (bf16[2,192,1024]{2,1,0:T(8,128)(2,1)}, bf16[2,192,1024]{2,1,0:T(8,128)(2,1)}, u32[]{:S(2)}, u32[]{:S(2)}) collective-permute-start(bf16[2,192,1024]{2,1,0:T(8,128)(2,1)} %fusion.30), channel_id=1, source_target_pairs={{0,16},{16,0},{1,17},{17,1},{2,18},{18,2},{3,19},{19,3},{4,20},{20... | collective-permute-start | bytes 2359304 | tf_op jit(solution)/shard_map/ppermute | solution.py:40
  345.3 42.2 %collective-permute-start.26 = (bf16[192,1024]{1,0:T(8,128)(2,1)}, bf16[192,1024]{1,0:T(8,128)(2,1)}, u32[]{:S(2)}, u32[]{:S(2)}) collective-permute-start(bf16[192,1024]{1,0:T(8,128)(2,1)} %fusion.42), channel_id=1, source_target_pairs={{0,8},{4,12},{8,0},{12,4},{1,9},{5,13},{9,1},{13,5},{2,10},{6,14},... | collective-permute-start | bytes 1179656 | tf_op jit(solution)/shard_map/ppermute | solution.py:40
  350.0 37.5 %collective-permute-start.25 = (bf16[192,1024]{1,0:T(8,128)(2,1)}, bf16[192,1024]{1,0:T(8,128)(2,1)S(1)}, u32[]{:S(2)}, u32[]{:S(2)}) collective-permute-start(bf16[192,1024]{1,0:T(8,128)(2,1)} %fusion.43), channel_id=1, source_target_pairs={{0,8},{4,12},{8,0},{12,4},{1,9},{5,13},{9,1},{13,5},{2,10},{6,14},... | collective-permute-start | bytes 1179656 | tf_op jit(solution)/shard_map/ppermute | solution.py:40
  393.0 69.4 %collective-permute-start.37 = (bf16[2,192,768]{2,1,0:T(8,128)(2,1)}, bf16[2,192,768]{2,1,0:T(8,128)(2,1)}, u32[]{:S(2)}, u32[]{:S(2)}) collective-permute-start(bf16[2,192,768]{2,1,0:T(8,128)(2,1)} %fusion.36), channel_id=1, source_target_pairs={{0,4},{4,0},{8,12},{12,8},{1,5},{5,1},{9,13},{13,9},{2,6},{6,2},{1... | collective-permute-start | bytes 1769480 | tf_op jit(solution)/shard_map/ppermute | solution.py:40
  397.2 62.7 %collective-permute-start.38 = (bf16[2,192,768]{2,1,0:T(8,128)(2,1)}, bf16[2,192,768]{2,1,0:T(8,128)(2,1)}, u32[]{:S(2)}, u32[]{:S(2)}) collective-permute-start(bf16[2,192,768]{2,1,0:T(8,128)(2,1)} %fusion.35), channel_id=1, source_target_pairs={{0,16},{16,0},{1,17},{17,1},{2,18},{18,2},{3,19},{19,3},{4,20},{20... | collective-permute-start | bytes 1769480 | tf_op jit(solution)/shard_map/ppermute | solution.py:40
  434.0 19.4 %collective-permute-start.34 = (bf16[256,1536]{1,0:T(8,128)(2,1)S(1)}, bf16[256,1536]{1,0:T(8,128)(2,1)S(1)}, u32[]{:S(2)}, u32[]{:S(2)}) collective-permute-start(bf16[256,1536]{1,0:T(8,128)(2,1)S(1)} %add_convert_fusion), channel_id=1, source_target_pairs={{0,2},{1,3},{2,0},{3,1},{4,6},{5,7},{6,4},{7,5},{8,10},{9,11},{10,... | collective-permute-start | bytes 2359304 | tf_op jit(solution)/shard_map/ppermute | solution.py:40
  439.7 34.8 %collective-permute-start.42 = (bf16[2,2,224,384]{3,2,1,0:T(8,128)(2,1)}, bf16[2,2,224,384]{3,2,1,0:T(8,128)(2,1)}, u32[]{:S(2)}, u32[]{:S(2)}) collective-permute-start(bf16[2,2,224,384]{3,2,1,0:T(8,128)(2,1)} %dynamic-slice_bitcast_fusion.7), channel_id=1, source_target_pairs={{0,4},{4,0},{8,12},{12,8},{1,5},{5,1},{9,13},{13,9},{2,6},{6,2},{1... | collective-permute-start | bytes 2064392 | tf_op jit(solution)/shard_map/ppermute | solution.py:40
  455.0 18.7 %collective-permute-start.35 = (bf16[256,1536]{1,0:T(8,128)(2,1)S(1)}, bf16[256,1536]{1,0:T(8,128)(2,1)}, u32[]{:S(2)}, u32[]{:S(2)}) collective-permute-start(bf16[256,1536]{1,0:T(8,128)(2,1)S(1)} %fusion.27), channel_id=1, source_target_pairs={{0,2},{1,3},{2,0},{3,1},{4,6},{5,7},{6,4},{7,5},{8,10},{9,11},{10,... | collective-permute-start | bytes 2359304 | tf_op jit(solution)/shard_map/ppermute | solution.py:40
  456.3 18.2 %collective-permute-start.36 = (bf16[256,1536]{1,0:T(8,128)(2,1)S(1)}, bf16[256,1536]{1,0:T(8,128)(2,1)}, u32[]{:S(2)}, u32[]{:S(2)}) collective-permute-start(bf16[256,1536]{1,0:T(8,128)(2,1)S(1)} %fusion.27), channel_id=1, source_target_pairs={{0,1},{1,0},{2,3},{3,2},{4,5},{5,4},{6,7},{7,6},{8,9},{9,8},{10,11... | collective-permute-start | bytes 2359304 | tf_op jit(solution)/shard_map/ppermute | solution.py:40
  459.8 18.2 %collective-permute-start.41 = (bf16[2,2,224,384]{3,2,1,0:T(8,128)(2,1)}, bf16[2,2,224,384]{3,2,1,0:T(8,128)(2,1)}, u32[]{:S(2)}, u32[]{:S(2)}) collective-permute-start(bf16[2,2,224,384]{3,2,1,0:T(8,128)(2,1)} %dynamic-slice_bitcast_fusion.8), channel_id=1, source_target_pairs={{0,16},{16,0},{1,17},{17,1},{2,18},{18,2},{3,19},{19,3},{4,20},{20... | collective-permute-start | bytes 2064392 | tf_op jit(solution)/shard_map/ppermute | solution.py:40
  462.4 51.9 %collective-permute-start.50 = (bf16[192,1024]{1,0:T(8,128)(2,1)}, bf16[192,1024]{1,0:T(8,128)(2,1)}, u32[]{:S(2)}, u32[]{:S(2)}) collective-permute-start(bf16[192,1024]{1,0:T(8,128)(2,1)} %fusion.41), channel_id=1, source_target_pairs={{0,8},{4,12},{8,0},{12,4},{1,9},{5,13},{9,1},{13,5},{2,10},{6,14},... | collective-permute-start | bytes 1179656 | tf_op jit(solution)/shard_map/ppermute | solution.py:40
  473.8 39.8 %collective-permute-start.52 = (bf16[192,768]{1,0:T(8,128)(2,1)}, bf16[192,768]{1,0:T(8,128)(2,1)}, u32[]{:S(2)}, u32[]{:S(2)}) collective-permute-start(bf16[192,768]{1,0:T(8,128)(2,1)} %fusion.53), channel_id=1, source_target_pairs={{0,8},{4,12},{8,0},{12,4},{1,9},{5,13},{9,1},{13,5},{2,10},{6,14},... | collective-permute-start | bytes 884744 | tf_op jit(solution)/shard_map/ppermute | solution.py:40
  474.5 21.4 %collective-permute-start.39 = (bf16[256,1536]{1,0:T(8,128)(2,1)}, bf16[256,1536]{1,0:T(8,128)(2,1)}, u32[]{:S(2)}, u32[]{:S(2)}) collective-permute-start(bf16[256,1536]{1,0:T(8,128)(2,1)} %collective-permute-done.35), channel_id=1, source_target_pairs={{0,1},{1,0},{2,3},{3,2},{4,5},{5,4},{6,7},{7,6},{8,9},{9,8},{10,11... | collective-permute-start | bytes 2359304 | tf_op jit(solution)/shard_map/ppermute | solution.py:40
  478.0 19.0 %collective-permute-start.47 = (bf16[2,224,384]{2,1,0:T(8,128)(2,1)}, bf16[2,224,384]{2,1,0:T(8,128)(2,1)}, u32[]{:S(2)}, u32[]{:S(2)}) collective-permute-start(bf16[2,224,384]{2,1,0:T(8,128)(2,1)} %fusion.48), channel_id=1, source_target_pairs={{0,16},{16,0},{1,17},{17,1},{2,18},{18,2},{3,19},{19,3},{4,20},{20... | collective-permute-start | bytes 1032200 | tf_op jit(solution)/shard_map/ppermute | solution.py:40
  494.5 19.7 %collective-permute-start.51 = (bf16[192,768]{1,0:T(8,128)(2,1)}, bf16[192,768]{1,0:T(8,128)(2,1)}, u32[]{:S(2)}, u32[]{:S(2)}) collective-permute-start(bf16[192,768]{1,0:T(8,128)(2,1)} %fusion.54), channel_id=1, source_target_pairs={{0,8},{4,12},{8,0},{12,4},{1,9},{5,13},{9,1},{13,5},{2,10},{6,14},... | collective-permute-start | bytes 884744 | tf_op jit(solution)/shard_map/ppermute | solution.py:40
  497.0 24.4 %collective-permute-start.45 = (bf16[64,768]{1,0:T(8,128)(2,1)S(1)}, bf16[64,768]{1,0:T(8,128)(2,1)S(1)}, u32[]{:S(2)}, u32[]{:S(2)}) collective-permute-start(bf16[64,768]{1,0:T(8,128)(2,1)S(1)} %add_convert_fusion.9), channel_id=1, source_target_pairs={{0,8},{4,12},{8,0},{12,4},{1,9},{5,13},{9,1},{13,5},{2,10},{6,14},... | collective-permute-start | bytes 294920 | tf_op jit(solution)/shard_map/ppermute | solution.py:40
  510.2 28.3 %collective-permute-start.53 = (bf16[224,384]{1,0:T(8,128)(2,1)S(1)}, bf16[224,384]{1,0:T(8,128)(2,1)S(1)}, u32[]{:S(2)}, u32[]{:S(2)}) collective-permute-start(bf16[224,384]{1,0:T(8,128)(2,1)S(1)} %fusion.55), channel_id=1, source_target_pairs={{0,8},{4,12},{8,0},{12,4},{1,9},{5,13},{9,1},{13,5},{2,10},{6,14},... | collective-permute-start | bytes 516104 | tf_op jit(solution)/shard_map/ppermute | solution.py:40
  513.5 24.9 %collective-permute-start.49 = (bf16[224,384]{1,0:T(8,128)(2,1)S(1)}, bf16[224,384]{1,0:T(8,128)(2,1)}, u32[]{:S(2)}, u32[]{:S(2)}) collective-permute-start(bf16[224,384]{1,0:T(8,128)(2,1)S(1)} %fusion.56), channel_id=1, source_target_pairs={{0,8},{4,12},{8,0},{12,4},{1,9},{5,13},{9,1},{13,5},{2,10},{6,14},... | collective-permute-start | bytes 516104 | tf_op jit(solution)/shard_map/ppermute | solution.py:40
  (132 other events, 972.5 us)
Sparse Core Ops, SparseCore 0:
  282.1 71.4 all-reduce.11

commit v4 on v3

--- a/solution.py
+++ b/solution.py
@@ -65,8 +65,9 @@
 
 
 class Scatter:
-    def __init__(self, value, order, whole):
-        self.terms = [value.astype(bf16).reshape((2,) * len(whole) + value.shape[1:])]
+    def __init__(self, values, order, whole):
+        self.own = [v.astype(bf16).reshape((2,) * len(whole) + v.shape[1:]) for v in values]
+        self.arrived = []
         self.order = list(order)
         self.left = list(whole)
 
@@ -79,19 +80,29 @@
         def part(term, which):
             return lax.dynamic_index_in_dim(term, which, at, keepdims=False)
 
-        away = sum(part(t, 1 - mine).astype(f32) for t in self.terms).astype(bf16)
-        self.terms = [part(t, mine) for t in self.terms] + [swap(away, axis, mask)]
+        own = [part(t, 1 - mine) for t in self.own]
+        away = own[0] if len(own) == 1 else jnp.concatenate(own, axis=-1)
+        if self.arrived:
+            away = away.astype(f32) + sum(part(t, 1 - mine).astype(f32) for t in self.arrived)
+            away = away.astype(bf16)
+        self.own = [part(t, mine) for t in self.own]
+        self.arrived = [part(t, mine) for t in self.arrived] + [swap(away, axis, mask)]
         return away
 
     @property
     def got(self):
-        return self.terms[-1]
+        return self.arrived[-1]
 
     def total(self, *others):
         while self.order:
             self.send(*others)
-        self.terms[-1] = after(self.terms[-1], *others)
-        return sum(t.astype(f32) for t in self.terms)
+        self.arrived[-1] = after(self.arrived[-1], *others)
+        out, at = [], 0
+        for own in self.own:
+            columns = slice(at, at + own.shape[-1])
+            at += own.shape[-1]
+            out.append(own.astype(f32) + sum(t[..., columns].astype(f32) for t in self.arrived))
+        return out
 
 
 class chan_scatter:
@@ -135,6 +146,22 @@
 
 def step_rows(step, steps):
     return pl.ds(step, pieces, stride=steps)
+
+
+gap = 8
+
+
+def gapped_rows(step, steps):
+    return pl.ds(step, pieces, stride=steps + gap)
+
+
+def gapped_part(start, rows, steps):
+    return pl.ds(start + start // steps * gap, rows)
+
+
+def to_gapped(block, out, steps):
+    for s in range(pieces):
+        out[pl.ds(s * (steps + gap), steps), :] = block[pl.ds(s * steps, steps), :]
 
 
 def split_proj(proj, both, steps):
@@ -170,8 +197,10 @@
 
 
 def ends_kernel(size, rank, rates, mixed, proj, dec, ends, sums, end_total, product_total, *scratch):
-    both, eb, fb = scratch
+    both, eb, fb, rates_apart, mixed_apart = scratch
     steps = rates.shape[0] // pieces
+    to_gapped(rates, rates_apart, steps)
+    to_gapped(mixed, mixed_apart, steps)
 
     @pl.when(pl.program_id(0) == 0)
     def _():
@@ -184,8 +213,8 @@
     def body(i, carry):
         states, total = carry
         rows = pl.ds(pl.multiple_of(i * pieces, pieces), pieces)
-        rate = rates[step_rows(i, steps), :]
-        push = rate * mixed[step_rows(i, steps), :]
+        rate = rates_apart[gapped_rows(i, steps), :]
+        push = rate * mixed_apart[gapped_rows(i, steps), :]
         rate = rate + fb[0, rows, :]
         out = []
         for n in range(size):
@@ -209,7 +238,8 @@
         ends, sums, arriving = rest[:3]
     else:
         begin = rest[0]
-    gated, summed, before, final, both, eb, rb, fb, start, scanned = rest[-10:]
+    gated, summed, before, final, both, eb, rb, fb, start = rest[-12:-3]
+    scanned, rates_apart, mixed_apart = rest[-3:]
     steps = rates.shape[1]
     rates, mixed, proj, gate_in = (
         item.reshape(pieces * steps, lanes) for item in (rates, mixed, proj, gate_in)
@@ -222,6 +252,8 @@
         spread(both, rb, rank + size, size)
         spread(both, fb, 0, 1)
 
+    to_gapped(rates, rates_apart, steps)
+    to_gapped(mixed, mixed_apart, steps)
     decays = decay_rows(dec, size)
     if opening:
         reached = arriving[...]
@@ -232,9 +264,9 @@
 
     def body(i, states):
         rows = pl.ds(pl.multiple_of(i * 2 * pieces, 2 * pieces), 2 * pieces)
-        first, second = step_rows(2 * i, steps), step_rows(2 * i + 1, steps)
-        rate0, rate1 = rates[first, :], rates[second, :]
-        push0, push1 = rate0 * mixed[first, :], rate1 * mixed[second, :]
+        first, second = gapped_rows(2 * i, steps), gapped_rows(2 * i + 1, steps)
+        rate0, rate1 = rates_apart[first, :], rates_apart[second, :]
+        push0, push1 = rate0 * mixed_apart[first, :], rate1 * mixed_apart[second, :]
         apart = fb[0, rows, :]
         rate0, rate1 = rate0 + apart[:pieces], rate1 + apart[pieces:]
         low = jnp.zeros((pieces, lanes), f32)
@@ -260,18 +292,20 @@
         last = jnp.concatenate([states[n], states[n]], axis=0).astype(bf16)
         before[n, pl.ds(steps * pieces, 2 * pieces), :] = last
 
-    tall = min(256, steps * pieces)
+    tall = steps
     for k in range(steps * pieces // tall):
         rows = pl.ds(k * tall, tall)
-        total = scanned[rows, :] + skip[...] * mixed[rows, :]
+        total = scanned[gapped_part(k * tall, tall, steps), :] + skip[...] * mixed[rows, :]
         gate = gate_in[rows, :]
         gated[rows, :] = (total * (gate * jax.nn.sigmoid(gate))).astype(bf16)
         summed[rows, :] = total.astype(bf16)
 
 
 def heads_kernel(size, rank, rates, slope, proj, dec, sums, heads, head_total, *scratch):
-    both, rb, fb = scratch
+    both, rb, fb, rates_apart, slope_apart = scratch
     steps = rates.shape[0] // pieces
+    to_gapped(rates, rates_apart, steps)
+    to_gapped(slope, slope_apart, steps)
 
     @pl.when(pl.program_id(0) == 0)
     def _():
@@ -284,8 +318,8 @@
     def body(i, carried):
         step = steps - 1 - i
         rows = pl.ds(pl.multiple_of(step * pieces, pieces), pieces)
-        rate = rates[step_rows(step, steps), :] + fb[0, rows, :]
-        grad = slope[step_rows(step, steps), :]
+        rate = rates_apart[gapped_rows(step, steps), :] + fb[0, rows, :]
+        grad = slope_apart[gapped_rows(step, steps), :]
         return tuple(
             (carried[n] + rb[n, rows, :] * grad) * jnp.exp2(rate * decays[n]) for n in range(size)
         )
@@ -318,7 +352,7 @@
     rest = rest[chunks + 2 :]
     pre_low, direct, proj_grad, decay_grad, bias_grad = rest[:5]
     both, eb, rb, fb, stop, decay_sum, entry_terms, readout_terms = rest[5:13]
-    picks, rate_grad, drive_grad, terms_grad = rest[13:]
+    picks, rate_grad, drive_grad, terms_grad, rates_apart, mixed_apart, slope_apart = rest[13:]
     steps = rates.shape[0] // pieces
     count = steps * pieces
     pair = 2 * pieces
@@ -335,6 +369,9 @@
         for n in range(2 * size):
             picks[pl.ds(n * lanes, lanes), :] = (target == rank + n).astype(f32).astype(bf16)
 
+    to_gapped(rates, rates_apart, steps)
+    to_gapped(mixed, mixed_apart, steps)
+    to_gapped(slope, slope_apart, steps)
     decays = decay_rows(dec, size)
     reached = leaving[...]
     for s in reversed(range(pieces)):
@@ -351,10 +388,10 @@
         following = pl.ds(at + pair, pair)
         half = offset + place
         rows = pl.ds(pl.multiple_of(half * pair, pair), pair)
-        first, second = step_rows(2 * half, steps), step_rows(2 * half + 1, steps)
-        rate0, rate1 = rates[first, :], rates[second, :]
-        push0, push1 = rate0 * mixed[first, :], rate1 * mixed[second, :]
-        grad0, grad1 = slope[first, :], slope[second, :]
+        first, second = gapped_rows(2 * half, steps), gapped_rows(2 * half + 1, steps)
+        rate0, rate1 = rates_apart[first, :], rates_apart[second, :]
+        push0, push1 = rate0 * mixed_apart[first, :], rate1 * mixed_apart[second, :]
+        grad0, grad1 = slope_apart[first, :], slope_apart[second, :]
         apart = fb[0, rows, :]
         far0, far1 = rate0 + apart[:pieces], rate1 + apart[pieces:]
         zero = jnp.zeros((pieces, lanes), f32)
@@ -400,12 +437,13 @@
     pl.when(group > 0)(lambda: sweep(False))
     decay_grad[...] = jnp.sum(decay_sum[...], axis=1)
 
-    tall = min(256, count)
+    tall = steps
     bias_total = jnp.zeros((1, lanes), f32)
     for k in range(count // tall):
         rows = pl.ds(k * tall, tall)
-        rate, drives = rates[rows, :], drive_grad[rows, :]
-        pre = (rate_grad[rows, :] * ln2 + drives * mixed[rows, :]) * (1.0 - jnp.exp(-rate))
+        apart = gapped_part(k * tall, tall, steps)
+        rate, drives = rates[rows, :], drive_grad[apart, :]
+        pre = (rate_grad[apart, :] * ln2 + drives * mixed[rows, :]) * (1.0 - jnp.exp(-rate))
         bias_total = bias_total + jnp.sum(pre, axis=0, keepdims=True)
         low = pre.astype(bf16)
         pre_low[rows, :] = low
@@ -463,6 +501,7 @@
     terms = pltpu.VMEM((count, size * lanes), f32)
     edge = pltpu.VMEM((size, pieces, lanes), f32)
     own = pltpu.VMEM((count, lanes), f32)
+    apart = pltpu.VMEM((count + pieces * gap, lanes), f32)
     picks = pltpu.VMEM((2 * size * lanes, lanes), bf16)
     work = count * channels * size
 
@@ -490,7 +529,7 @@
         wide_part = pltpu.VMEM((size, pieces * run, lanes), f32)
         thin_part = pltpu.VMEM((1, pieces * run, lanes), f32)
         both_part = pltpu.VMEM((pieces * run, 2 * lanes), bf16)
-        own_part = pltpu.VMEM((pieces * run, lanes), f32)
+        own_part = pltpu.VMEM((pieces * (run + gap), lanes), f32)
         begin = [ends] if k else [ends, sums, small]
 
         def kernel(size, rank, *refs):
@@ -502,7 +541,7 @@
             [rows, rows, same, small, rows, line] + begin,
             [part, part, states, ends],
             [part_out, part_out, states_out, ends_out],
-            [both_part, wide_part, wide_part, thin_part, edge, own_part],
+            [both_part, wide_part, wide_part, thin_part, edge, own_part, own_part, own_part],
         )
 
     def backward_call(first, span):
@@ -526,12 +565,13 @@
             [moved(spec) for spec in ins] + held,
             [moved(spec) for spec in outs],
             [tall_low, tall_out, fixed_out, small_out, line_out],
-            [both, wide, wide, thin, edge, edge, terms, terms, picks, own, own, own],
+            [both, wide, wide, thin, edge, edge, terms, terms, picks, apart, apart, own]
+            + [apart] * 3,
             span,
             aliases,
         )
 
-    part = groups // 2
+    part = max(groups // 3, 1)
     backward_parts = (backward_call(0, part), backward_call(part, groups - part))
     return (
         call(
@@ -540,7 +580,7 @@
             [tall, tall, fixed, small],
             [ends, sums, small, small],
             [ends_out, sums_out, small_out, small_out],
-            [both, wide, thin],
+            [both, wide, thin, apart, apart],
         ),
         tuple(forward_call(k) for k in range(chunks)),
         call(
@@ -549,9 +589,102 @@
             [tall, tall, fixed, small, sums],
             [ends, small],
             [ends_out, small_out],
-            [both, wide, thin],
+            [both, wide, thin, apart, apart],
         ),
         backward_parts,
+    )
+
+
+def conv_kernel(width, low, state_proj, direct, inner, rim, taps, bias, mask, *rest):
+    inner_low, last, edge, sums, extended, masks = rest[:6]
+    slopes = rest[6:]
+    count = inner.shape[0]
+    tall = min(256, count)
+    pad = edge.shape[0]
+
+    @pl.when(pl.program_id(0) == 0)
+    def _():
+        for k in range(width - 1):
+            for at in range(0, count, tall):
+                rows = pl.ds(at, tall)
+                masks[k, rows, :] = jnp.broadcast_to(mask[rows, k : k + 1], (tall, lanes))
+
+    zeros = jnp.zeros((pad, lanes), f32)
+    extended[:pad, :] = rim[...]
+    for item in slopes:
+        item[:pad, :] = zeros
+        item[pl.ds(pad + count, pad), :] = zeros
+    for at in range(0, count, tall):
+        rows = pl.ds(at, tall)
+        extended[pl.ds(pad + at, tall), :] = inner[rows, :].astype(f32)
+    totals = [jnp.zeros((1, lanes), f32)] * (width + 1)
+    for at in range(0, count, tall):
+        rows = pl.ds(at, tall)
+        shifted_rows = [extended[pl.ds(pad + at - (width - 1 - k), tall), :] for k in range(width)]
+        held = [masks[k, rows, :] for k in range(width - 1)]
+        shifted_rows = [item * held[k] if k < width - 1 else item for k, item in enumerate(shifted_rows)]
+        convolved = bias[...] + sum(item * taps[k : k + 1, :] for k, item in enumerate(shifted_rows))
+        sigma = jax.nn.sigmoid(convolved)
+        grad = transposed_right(low[rows, :], state_proj[...]) + direct[rows, :]
+        grad = grad * (sigma * (1.0 + convolved * (1.0 - sigma)))
+        for k in range(width):
+            term = jnp.sum(grad * shifted_rows[k], axis=0, keepdims=True)
+            totals[k] = totals[k] + term
+            slopes[k][pl.ds(pad + at, tall), :] = grad * held[k] if k < width - 1 else grad
+        totals[width] = totals[width] + jnp.sum(grad, axis=0, keepdims=True)
+    sums[...] = zeros
+    for k in range(width + 1):
+        sums[k : k + 1, :] = totals[k]
+
+    def spread_back(at, rows):
+        return sum(
+            slopes[k][pl.ds(pad + at + width - 1 - k, rows), :] * taps[k : k + 1, :]
+            for k in range(width)
+        )
+
+    for at in range(0, count, tall):
+        inner_low[pl.ds(at, tall), :] = spread_back(at, tall).astype(bf16)
+    last[...] = spread_back(count - last.shape[0], last.shape[0])
+    edge[...] = spread_back(-pad, pad)
+
+
+def conv_call(count, channels, width):
+    pad = 8
+    tall = pl.BlockSpec((count, lanes), lambda g: (0, g))
+    fixed = pl.BlockSpec((count, lanes), lambda g: (0, 0))
+    eight = pl.BlockSpec((pad, lanes), lambda g: (0, g))
+    end = pl.BlockSpec((2 * pad, lanes), lambda g: (0, g))
+    shape = jax.ShapeDtypeStruct
+    return pl.pallas_call(
+        functools.partial(conv_kernel, width),
+        grid=(channels // lanes,),
+        in_specs=[
+            fixed,
+            pl.BlockSpec((lanes, lanes), lambda g: (g, 0)),
+            tall,
+            tall,
+            eight,
+            pl.BlockSpec((width, lanes), lambda g: (0, g)),
+            pl.BlockSpec((1, lanes), lambda g: (0, g)),
+            fixed,
+        ],
+        out_specs=[tall, end, eight, eight],
+        out_shape=[
+            shape((count, channels), bf16),
+            shape((2 * pad, channels), f32),
+            shape((pad, channels), f32),
+            shape((pad, channels), f32),
+        ],
+        scratch_shapes=[
+            pltpu.VMEM((pad + count, lanes), f32),
+            pltpu.VMEM((width - 1, count, lanes), f32),
+        ]
+        + [pltpu.VMEM((pad + count + pad, lanes), f32)] * width,
+        compiler_params=pltpu.CompilerParams(
+            dimension_semantics=("arbitrary",), vmem_limit_bytes=vmem_bytes
+        ),
+        cost_estimate=pl.CostEstimate(flops=count, bytes_accessed=0, transcendentals=0),
+        name="conv_backward",
     )
 
 
@@ -562,7 +695,7 @@
 
 
 def norm_call(count, features):
-    tall = min(count, 128)
+    tall = min(count, 256)
     return pl.pallas_call(
         norm_kernel,
         grid=(count // tall,),
@@ -636,8 +769,9 @@
 
     shards = lax.axis_size("dp") * lax.axis_size("seq")
 
-    def scatter(value, order):
-        return Scatter(value.reshape(shards, -1, value.shape[-1]), order, shard_bits)
+    def scatter(order, *values):
+        values = [value.reshape(shards, -1, value.shape[-1]) for value in values]
+        return Scatter(values, order, shard_bits)
 
     def side(values, r):
         return lax.dynamic_slice_in_dim(values, ((me >> 1) ^ r) * 2 * quarter, 2 * quarter)
@@ -742,13 +876,13 @@
         jnp.concatenate([ffn0[k], ffn1[k]], axis=0) for k in range(4)
     )
     upper_two = jnp.concatenate(upper_parts, axis=0)
-    up_sum = scatter(transposed_left(after(normed_two, back.middle), grad_up_ffn), usual)
-    sent = up_sum.send()
-    gate_ffn_sum = scatter(transposed_left(after(normed_two, sent), grad_gate_ffn), usual)
-    sent = gate_ffn_sum.send()
-    down_sum = scatter(transposed_left(after(upper_two, sent), active), other)
+    up_weight = transposed_left(after(normed_two, back.middle), grad_up_ffn).astype(bf16)
+    gate_weight = transposed_left(after(normed_two, up_weight), grad_gate_ffn).astype(bf16)
+    pair_sum = scatter(usual, up_weight, gate_weight)
+    sent = pair_sum.send()
+    down_sum = scatter(other, transposed_left(after(upper_two, sent), active))
     sent = down_sum.send()
-    ffn_sums = [up_sum, gate_ffn_sum, down_sum]
+    ffn_sums = [pair_sum, down_sum]
     grad_normed_two = back.total(sent)
     grad_unit_two = grad_normed_two * gain_two
     grad_hidden = upper_own + scale_two * (
@@ -760,62 +894,50 @@
     ]
     hidden_blocks = low.blocks(result_parts)
     hidden_low = at_home(hidden_blocks, bf16)
-    own_part = (of_side(result_parts[0], 0).astype(f32) + hidden_one).astype(bf16)
-    upper_chip = me >> 1
-    near_rows = lax.dynamic_update_slice_in_dim(
-        result_parts[0], own_part, (me & 1) * quarter, 0
-    )
-    result_rows = jnp.concatenate(
-        [
-            jnp.where(upper_chip == 1, result_parts[1], near_rows),
-            jnp.where(upper_chip == 1, near_rows, result_parts[1]),
-        ],
-        axis=0,
-    )
-    result = lax.psum(after(result_rows, hidden_blocks[3]), "chan")
+    result_far = after(result_parts[1], hidden_blocks[2])
+    results = chan_scatter(lambda r: of_side(result_far if r > 1 else result_parts[0], r))
     gate_act = jax.nn.silu(gate_in)
     grad_gated = transposed_right(hidden_low, output_proj)
     grad_scanned = grad_gated * gate_act
     grad_gate_in = (grad_gated * summed.astype(f32) * silu_slope(gate_in)).astype(bf16)
     skip_grad = jnp.sum(grad_scanned * mixed_wide, axis=0)
     heads, head_total = scan_heads(
-        rates, grad_scanned, scan_proj, decay_two, sums
-    )
-    head_total = after(head_total, [item.got for item in ffn_sums])
-
-    mixer_sums = []
+        rates, after(grad_scanned, results.middle), scan_proj, decay_two, sums
+    )
+    head_total = after(head_total, [item.got for item in ffn_sums], results.second)
+
+    mixer_weights = []
 
     def output_weights(begun):
-        value = transposed_left(after(hidden_low, begun), gated)
-        mixer_sums.append(scatter(value, usual))
-        return [mixer_sums[0].send()]
+        value = transposed_left(after(hidden_low, begun), gated).astype(bf16)
+        mixer_weights.append(value)
+        return mixer_weights
 
     def gate_weights(begun):
-        value = transposed_left(normed, after(grad_gate_in, begun))
-        mixer_sums.append(scatter(value, other))
-        return [mixer_sums[1].send()]
+        value = transposed_left(normed, after(grad_gate_in, begun)).astype(bf16)
+        mixer_weights.append(value)
+        return [value]
 
     leaving = chained(product_total, head_total, -1, [output_weights, gate_weights])
     sent = [item.send(leaving) for item in ffn_sums]
+    mixer_sum = scatter(usual, *mixer_weights)
+    result = chan_gather((hidden_one + results.total(leaving)).astype(bf16))
     step_padded = jnp.pad(step_proj, ((0, 2 * size), (0, 0)))
     scan_inputs = (rates, mixed_wide, grad_scanned, scan_proj, decay_two, heads, sums)
     first_scan, second_scan = scan_backward
-    begin = after(leaving, sent)
+    begin = after(leaving, sent, result.own)
     parts = first_scan(*scan_inputs, begin, before, skip, step_padded)
-    terms = parts[2]
-    sent = [item.send(terms) for item in ffn_sums]
+    terms = after(parts[2], pair_sum.got, down_sum.got, result.across)
+    sent = [item.send(terms) for item in ffn_sums + [mixer_sum]]
     begin = after(leaving, sent)
     kept = [parts[k] for k in (0, 1, 3, 4)]
     pre_low, direct, more_terms, decay_grad, step_bias_grad = second_scan(
         *scan_inputs, begin, before, skip, step_padded, *kept
     )
-    more_terms = after(more_terms, [item.got for item in ffn_sums[:2] + mixer_sums], result)
+    more_terms = after(more_terms, [pair_sum.got, down_sum.got, mixer_sum.got])
     proj_terms = terms + more_terms
 
     step_weight_grad = []
-
-    def mixer_round():
-        return [item.send() for item in mixer_sums]
 
     gate_terms = []
 
@@ -824,34 +946,25 @@
         gate_terms.append(transposed_right(after(grad_gate_in, begun), gate_proj).astype(bf16))
         return step_weight_grad + gate_terms
 
-    grad_projected = chan_total(proj_terms, mixer_round, step_weights).astype(bf16)
-    grad_mixed = transposed_right(grad_projected, state_proj) + direct
-    grad_conv = grad_mixed * silu_slope(convolved)
-    conv_bias_grad = jnp.sum(grad_conv, axis=0)
-    conv_taps_grad = jnp.stack(
-        [
-            jnp.sum(grad_conv * extended[offset : offset + count] * masks[offset], axis=0)
-            for offset in range(width)
-        ],
-        axis=0,
-    )
-    grad_extended = sum(
-        jnp.pad(
-            grad_conv * taps[offset] * masks[offset], ((offset, width - 1 - offset), (0, 0))
-        )
-        for offset in range(width)
-    )
-    spill = grad_extended[: width - 1]
-    returned = shifted(spill, "seq", -1)
-    state_grad = transposed_left(after(grad_projected, spill), mixed).astype(bf16)
+    grad_projected = chan_total(proj_terms, lambda: [mixer_sum.send()], step_weights).astype(bf16)
+    mask = jnp.concatenate(masks[: width - 1], axis=1)
+    mask = jnp.pad(mask, ((0, 0), (0, lanes - width + 1)))
+    rim_rows = jnp.pad(rim.astype(f32), ((8 - width + 1, 0), (0, 0)))
+    inner_low, last_rows, edge, conv_sums = conv_call(count, channels, width)(
+        grad_projected,
+        state_proj,
+        direct,
+        inner,
+        rim_rows,
+        taps,
+        conv_bias.astype(f32)[None],
+        mask,
+    )
+    returned = shifted(edge, "seq", -1)
+    state_grad = transposed_left(after(grad_projected, edge), mixed).astype(bf16)
+    singles = jnp.concatenate([step_bias_grad, skip_grad[None]], axis=0)
     few = jnp.concatenate(
-        [
-            conv_taps_grad,
-            conv_bias_grad[None],
-            step_bias_grad,
-            decay_grad * decay,
-            skip_grad[None],
-        ],
+        [conv_sums, decay_grad.reshape(size, channels) * decay, jnp.pad(singles, ((0, 6), (0, 0)))],
         axis=0,
     )
     low_rows = rank // shards
@@ -862,11 +975,8 @@
         ],
         axis=1,
     )
-    inner_low = (
-        grad_extended[width - 1 :]
-        + jnp.pad(after(returned, low_parts), ((count - width + 1, 0), (0, 0)))
-    ).astype(bf16)
-
+    last_rows = last_rows.at[-8:].add(after(returned, low_parts)).astype(bf16)
+    inner_low = lax.dynamic_update_slice_in_dim(inner_low, last_rows, count - 16, 0)
     lines = jnp.concatenate([state_grad[rank:], few.astype(bf16)], axis=0)
     lines_used = lines.shape[0]
 
@@ -881,10 +991,12 @@
     share = features // shards
 
     def token_part(r):
-        product = transposed_right(side(inner_low, r), input_proj)
+        product = transposed_right(side(inner_late if r == 0 else inner_low, r), input_proj)
         return (product + side(gate_terms[0], r).astype(f32)).astype(bf16)
 
     far_part = token_part(1)
+    sent = [mixer_sum.send(far_part)]
+    inner_late = after(inner_low, sent)
     near_part = token_part(0)
     tokens_sum = chan_scatter(lambda r: of_side(far_part if r > 1 else near_part, r))
     scale_one, unit_one = unit_of(rows_own)
@@ -898,9 +1010,10 @@
         columns = slice(k * half_width, (k + 1) * half_width)
         value = jnp.concatenate([input_blocks[:, :, columns], low_parts[:, :, columns]], axis=1)
         value = jnp.pad(value, ((0, 0), (0, -value.shape[1] % 16), (0, 0)))
-        input_sums.append(Scatter(value, order, shard_bits))
+        input_sums.append(Scatter([value], order, shard_bits))
         sent.append(input_sums[-1].send())
-    grad_normed = tokens_sum.total(sent)
+    result_whole = at_home(result.blocks(tokens_sum.middle), bf16)
+    grad_normed = tokens_sum.total(sent, result_whole)
     grad_unit_one = grad_normed * gain_one
     tokens_grad = grad_hidden + scale_one * (
         grad_unit_one - unit_one * jnp.mean(grad_unit_one * unit_one, axis=-1, keepdims=True)
@@ -910,23 +1023,20 @@
         [jnp.sum(grad_normed * unit_one, axis=0), jnp.sum(grad_normed_two * unit_two, axis=0)]
     )
     gains = gains.reshape(-1, channels).astype(bf16)
-    sent = [item.send(tokens_last.own) for item in mixer_sums]
-    done = [item.total(sent) for item in ffn_sums[:2]]
-    blocks = tokens_last.blocks(done)
-    sent = [item.send(blocks[2]) for item in input_sums]
-    for mask in (1, 2):
-        gains = sum_step(gains, ("chan", mask), sent)
+    gains = sum_step(gains, ("chan", 1))
+    sent = [item.send(tokens_last.own) for item in input_sums]
+    done = pair_sum.total(tokens_last.own)
+    blocks = tokens_last.blocks(done, gains, sent)
+    while input_sums[0].order:
+        sent = [item.send(blocks[2]) for item in input_sums]
+    gains = sum_step(gains, ("chan", 2))
+    gains = jnp.pad(gains, ((0, -gains.shape[0] % 16), (0, 0)))
     vectors = jnp.concatenate([lines, gains], axis=0)
-    vectors = jnp.pad(vectors, ((0, -vectors.shape[0] % 16), (0, 0)))
-    vectors = sum_step(vectors, shard_bits[0])
+    for bit in shard_bits:
+        vectors = sum_step(vectors, bit, sent)
     tokens_out = at_home(blocks, f32)
-    done.append(ffn_sums[2].total(blocks[3]))
-    while input_sums[0].order:
-        sent = [item.send(blocks[3]) for item in input_sums]
-    for bit in shard_bits[1:]:
-        vectors = sum_step(vectors, bit, sent)
-    done += [item.total(sent) for item in mixer_sums]
-    input_parts = [item.total(done) for item in input_sums]
+    done += down_sum.total(sent) + mixer_sum.total(sent)
+    input_parts = [item.total(done)[0] for item in input_sums]
     first = share + 2 * low_rows
     gains = vectors[lines_used:].astype(f32)
     shard = lax.axis_index("dp") * lax.axis_size("seq") + place
@@ -940,7 +1050,7 @@
     vectors = vectors.astype(f32)
     at = 2 * size
     return (
-        result[None],
+        result_whole[None],
         tokens_out[None],
         gain_share(0),
         input_parts[:share],
@@ -950,9 +1060,9 @@
         input_parts[share : share + low_rows].T,
         vectors[:at].T,
         input_parts[share + low_rows :],
-        vectors[at + width + 1],
-        vectors[at + width + 2 : at + width + 2 + size].T,
-        vectors[at + width + size + 2],
+        vectors[at + 8 + size],
+        vectors[at + 8 : at + 8 + size].T,
+        vectors[at + 9 + size],
         done[3].T,
         gain_share(1),
         done[1],

time: 563 us -> 549 us (0.975)
  other arithmetic: 101 us -> 84.9 us
  between operations: 16.2 us -> 2.61 us
  waiting for transfers between devices: 83.7 us -> 96 us
  local copies, waits for them, and re-layouts: 56.1 us -> 63.7 us
  Pallas kernels: 145 us -> 138 us
  starting transfers between devices: 58.2 us -> 63.9 us
    ppermute x48, waiting for transfers between devices: 73.6 us -> 86 us  [swap(): lax.ppermute(value, axis, [(i, i ^ mask) for i in range(lax.axis_size(axi...]
    squeeze x7 -> x18, local copies, waits for them, and re-layouts: 9.5 us -> 21.2 us  [part(): return lax.dynamic_index_in_dim(term, which, at, keepdims=False)]
    ppermute x6, starting transfers between devices: 18.1 us -> 29.2 us  [shifted(): lax.ppermute(value, axis, [(i, i + by) for i in range(size) if 0 <= i + b...]
    pallas_call x1, Pallas kernels: 34.5 us -> 25.5 us  [per_device(): parts = first_scan(*scan_inputs, begin, before, skip, step_padded)]
    convert_element_type x16 -> x12, other arithmetic: 29.7 us -> 22.2 us  [the longest x10 18.1 us: send(): away = away.astype(bf16)]
    reduce_sum x1 -> x0, other arithmetic: 5.99 us -> none  [per_device(): jnp.sum(grad_conv * extended[offset:offset + count] * masks[offset], axis=0)]
    pallas_call x1 -> x2, Pallas kernels: 20.5 us -> 25.5 us  [the longest x1 15.8 us: per_device(): scan_heads(rates, after(grad_scanned, results.middle), scan_proj, decay_t...]
    add x7 -> x5, other arithmetic: 12.4 us -> 8.82 us  [total(): own.astype(f32) + sum((t[..., columns].astype(f32) for t in self.arrived))]
  transfers between devices with their start and end apart: 55 -> 54, of which waited for: 18 -> 21; matrix products, arithmetic and copies ran while one was open for 33% -> 33% of each run, Pallas kernels for 16% -> 17%
where the time goes in v4:
time: 549 us; the launch traced here: 542 us
  Pallas kernels  138 us (25%)
  waiting for transfers between devices  96 us (17%)
  matrix products  93.5 us (17%)
  other arithmetic  84.9 us (15%)
  starting transfers between devices  63.9 us (12%)
  local copies, waits for them, and re-layouts  63.7 us (12%)
    ppermute x48, waiting for transfers between devices, swap(): lax.ppermute(value, axis, [(i, i ^ mask) for i in range(lax.axis_size(axi...  86 us
    pallas_call x1, Pallas kernels, per_device(): second_scan(*scan_inputs, begin, before, skip, step_padded, *kept)  39 us
    dot_general x12, matrix products, matmul(): return jnp.dot(left, right, preferred_element_type=f32)  36.2 us
    ppermute x48, starting transfers between devices, swap(): lax.ppermute(value, axis, [(i, i ^ mask) for i in range(lax.axis_size(axi...  34.7 us
    dot_general x10, matrix products, transposed_right(): lax.dot_general(left, right, (((1,), (1,)), ((), ())), preferred_element_...  31.4 us
    ppermute x6, starting transfers between devices, shifted(): lax.ppermute(value, axis, [(i, i + by) for i in range(size) if 0 <= i + b...  29.2 us
    pallas_call x1, Pallas kernels, per_device(): scan_forward[0](*scan3, decay_two, gate3, skip, ends, sums, arriving)  27.3 us
    dot_general x8, matrix products, transposed_left(): lax.dot_general(left, right, (((0,), (0,)), ((), ())), preferred_element_...  25.8 us
  transfers between devices with their start and end apart: 54, of which 21 were waited for; matrix products, arithmetic and copies ran while one was open for 33% of the time, Pallas kernels for 17%

profile of v4, /device:TPU:0, one launch (start us, length us, event | category | flops | bytes accessed | tf_op | source)
XLA Modules:
  0.0 542.3 jit_solution(5276721010654641037)
XLA Ops:
  2.1 4.7 norm_rows.1
  6.8 5.2 convolution_convert_fusion.11.inner
  13.2 4.9 collective-permute-start
  18.1 6.9 %fusion.100 = f32[1024,768]{1,0:T(8,128)} fusion(bf16[1024,1536]{1,0:T(8,128)(2,1)} %norm_rows.1, bf16[1536,768]{1,0:T(8,128)(2,1)} %param.24), kind=kOutput, calls=%fused_computation.293 | convolution fusion | flops 2415919104 | bytes 8650752 | tf_op jit(solution)/shard_map/dot_general | solution.py:28
  28.3 3.8 fusion.96
  44.2 3.5 compare_select_fusion.rates.refs_0_
  47.7 15.6 %scan_ends.1 = (f32[16,8,768]{2,1,0:T(8,128)}, f32[8,768]{1,0:T(8,128)}, f32[16,768]{1,0:T(8,128)}, f32[16,768]{1,0:T(8,128)}) custom-call(f32[1024,768]{1,0:T(8,128)} %compare_select_fusion.rates.refs_0_, f32[1024,768]{1,0:T(8,128)} %get-tuple-element.207.mixed.refs_1_, f32[1024,128]{1,0:T(8,128)} %broadcast_select_fusion.4.proj.refs_3_, ...), custom_call_target="tpu_custom_call" | custom-call | flops 12582912 | tf_op jit(solution)/shard_map/scan_ends/pallas_call | solution.py:830
  64.2 3.5 collective-permute-start.3
  70.7 16.3 %collective-permute-start.4 = (f32[2,16,768]{2,1,0:T(8,128)S(1)}, f32[2,16,768]{2,1,0:T(8,128)}, u32[]{:S(2)}, u32[]{:S(2)}) collective-permute-start(f32[2,16,768]{2,1,0:T(8,128)S(1)} %pad_maximum_fusion.9), channel_id=1, source_target_pairs={{0,8},{4,12},{1,9},{5,13},{2,10},{6,14},{3,11},{7,15},{16,24},{20,... | collective-permute-start | bytes 294920 | tf_op jit(solution)/shard_map/ppermute | solution.py:45
  89.1 27.3 %scan_forward.1 = (bf16[1024,768]{1,0:T(8,128)(2,1)}, bf16[1024,768]{1,0:T(8,128)(2,1)}, bf16[16,1040,768]{2,1,0:T(8,128)(2,1)}, f32[16,8,768]{2,1,0:T(8,128)}) custom-call(f32[8,128,768]{2,1,0:T(8,128)} %bitcast.313, f32[8,128,768]{2,1,0:T(8,128)} %bitcast.314, f32[8,128,128]{2,1,0:T(8,128)} %bitcast.315, ...), custom_call_target="tpu_custom_call" | custom-call | flops 12582912 | tf_op jit(solution)/shard_map/scan_forward/pallas_call | solution.py:842
  130.9 18.7 %collective-permute-done.7 = bf16[256,1536]{1,0:T(8,128)(2,1)} collective-permute-done((bf16[256,1536]{1,0:T(8,128)(2,1)}, bf16[256,1536]{1,0:T(8,128)(2,1)}, u32[]{:S(2)}, u32[]{:S(2)}) %collective-permute-start.7) | collective-permute-done | bytes 786464 | tf_op jit(solution)/shard_map/ppermute | solution.py:40
  163.7 3.7 multiply_convert_fusion.5
  195.3 3.7 convolution_convert_fusion.3
  199.1 3.8 convolution_convert_fusion.2
  207.9 3.9 convolution_convert_fusion.1
  223.3 14.5 %collective-permute-done.15 = bf16[256,1536]{1,0:T(8,128)(2,1)S(1)} collective-permute-done((bf16[256,1536]{1,0:T(8,128)(2,1)S(1)}, bf16[256,1536]{1,0:T(8,128)(2,1)S(1)}, u32[]{:S(2)}, u32[]{:S(2)}) %collective-permute-start.15) | collective-permute-done | bytes 786464 | tf_op jit(solution)/shard_map/ppermute | solution.py:40
  243.5 5.9 %multiply_reduce_fusion = (bf16[768]{0:T(1024)(128)(2,1)}, f32[1024,768]{1,0:T(8,128)}, bf16[1024,768]{1,0:T(8,128)(2,1)}) fusion(bf16[1024,768]{1,0:T(8,128)(2,1)S(1)} %copy-done.5, f32[1024,768]{1,0:T(8,128)S(1)} %copy-done.29, bf16[1024,768]{1,0:T(8,128)(2,1)S(1)} %copy-done.95, bf16[1024,1536]{1,0:T(8,128)(2,1)S(1)} %constant_dynamic-update-slice_fusion.4, ...), kind=kOutput, calls=%fused_computation.28 | convolution fusion | flops 2428501248 | bytes 16516608 | tf_op jit(solution)/shard_map/dot_general | solution.py:36
  249.3 15.8 %scan_heads.1 = (f32[16,8,768]{2,1,0:T(8,128)}, f32[16,768]{1,0:T(8,128)}) custom-call(f32[1024,768]{1,0:T(8,128)} %compare_select_fusion.rates.refs_0_, f32[1024,768]{1,0:T(8,128)} %get-tuple-element.128.slope.refs_2_, f32[1024,128]{1,0:T(8,128)} %broadcast_select_fusion.4.proj.refs_3_, f32[16,768]{1,0:T(8,128)} %bitcast_multiply_fusion.4.dec.refs_3_.refs_4_, ...), custom_call_target="tpu_custom_call" | custom-call | flops 12582912 | tf_op jit(solution)/shard_map/scan_heads/pallas_call | solution.py:904
  265.1 11.5 %collective-permute-done.20 = bf16[2,2,192,2048]{3,2,1,0:T(8,128)(2,1)} collective-permute-done((bf16[2,2,192,2048]{3,2,1,0:T(8,128)(2,1)}, bf16[2,2,192,2048]{3,2,1,0:T(8,128)(2,1)}, u32[]{:S(2)}, u32[]{:S(2)}) %collective-permute-start.20) | collective-permute-done | bytes 3145760 | tf_op jit(solution)/shard_map/ppermute | solution.py:40
  279.1 6.5 %convolution_convert_fusion.6 = bf16[1536,768]{1,0:T(8,128)(2,1)} fusion(bf16[1024,1536]{1,0:T(8,128)(2,1)} %copy-done.25, bf16[1024,768]{1,0:T(8,128)(2,1)} %get-tuple-element.116), kind=kOutput, calls=%fused_computation.7 | convolution fusion | flops 2417098752 | bytes 7077888 | tf_op jit(solution)/shard_map/dot_general | solution.py:32
  286.9 4.2 convolution_convert_fusion.5
  309.6 25.5 %scan_backward.2 = (bf16[1024,768]{1,0:T(8,128)(2,1)}, f32[1024,768]{1,0:T(8,128)}, f32[1024,128]{1,0:T(8,128)}, f32[16,768]{1,0:T(8,128)}, f32[1,768]{1,0:T(1,128)}) custom-call(f32[1024,768]{1,0:T(8,128)} %compare_select_fusion.rates.refs_0_, f32[1024,768]{1,0:T(8,128)} %get-tuple-element.207.mixed.refs_1_, f32[1024,768]{1,0:T(8,128)} %get-tuple-element.128.slope.refs_2_, ...), custom_call_target="tpu_custom_call" | custom-call | flops 12582912 | tf_op jit(solution)/shard_map/scan_backward/pallas_call | solution.py:929
  354.2 39.0 %scan_backward.3 = (bf16[1024,768]{1,0:T(8,128)(2,1)}, f32[1024,768]{1,0:T(8,128)}, f32[1024,128]{1,0:T(8,128)}, f32[16,768]{1,0:T(8,128)}, f32[1,768]{1,0:T(1,128)}) custom-call(f32[1024,768]{1,0:T(8,128)} %compare_select_fusion.rates.refs_0_, ...), custom_call_target="tpu_custom_call", output_to_operand_aliasing={{0}: (11, {}), {1}: (12, {}), {3}: (13, {}), {4}: (14, {})} | custom-call | flops 12582912 | tf_op jit(solution)/shard_map/scan_backward/pallas_call | solution.py:934
  408.5 4.0 convolution_convert_fusion
  417.5 9.8 %conv_backward.1 = (bf16[1024,768]{1,0:T(8,128)(2,1)}, f32[16,768]{1,0:T(8,128)}, f32[8,768]{1,0:T(8,128)}, f32[8,768]{1,0:T(8,128)}) custom-call(bf16[1024,128]{1,0:T(8,128)(2,1)} %add_convert_fusion.5.low, bf16[768,128]{1,0:T(8,128)(2,1)} %state_proj.1, f32[1024,768]{1,0:T(8,128)} %get-tuple-element.158.direct, bf16[1024,768]{1,0:T(8,128)(2,1)} %copy-done.7, ...), custom_call_target="tpu_custom_call" | custom-call | flops 1024 | tf_op jit(solution)/shard_map/conv_backward/pallas_call | solution.py:953
  429.7 5.1 collective-permute-done.33
  435.4 3.8 fusion.8
  466.1 8.5 %collective-permute-done.38 = bf16[256,1536]{1,0:T(8,128)(2,1)S(1)} collective-permute-done((bf16[256,1536]{1,0:T(8,128)(2,1)S(1)}, bf16[256,1536]{1,0:T(8,128)(2,1)S(1)}, u32[]{:S(2)}, u32[]{:S(2)}) %collective-permute-start.38) | collective-permute-done | bytes 786464 | tf_op jit(solution)/shard_map/ppermute | solution.py:40
  478.9 3.7 convert_add_fusion.10
  482.6 8.2 %collective-permute-done.43 = bf16[2,2,224,384]{3,2,1,0:T(8,128)(2,1)} collective-permute-done((bf16[2,2,224,384]{3,2,1,0:T(8,128)(2,1)}, bf16[2,2,224,384]{3,2,1,0:T(8,128)(2,1)}, u32[]{:S(2)}, u32[]{:S(2)}) %collective-permute-start.43) | collective-permute-done | bytes 688160 | tf_op jit(solution)/shard_map/ppermute | solution.py:40
  498.3 4.5 collective-permute-done.48
  511.9 3.5 broadcast_in_dim.74
  (482 shorter events, 240.2 us)
Async XLA Ops:
  13.2 13.3 %collective-permute-start = (bf16[3,768]{1,0:T(4,128)(2,1)S(1)}, bf16[3,768]{1,0:T(4,128)(2,1)S(1)}, u32[]{:S(2)}, u32[]{:S(2)}) collective-permute-start(bf16[3,768]{1,0:T(4,128)(2,1)S(1)} %slice.234), channel_id=1, source_target_pairs={{0,4},{4,8},{8,12},{1,5},{5,9},{9,13},{2,6},{6,10},{10,14},{3,7},{... | collective-permute-start | bytes 13832 | tf_op jit(solution)/shard_map/ppermute | solution.py:45
  70.7 17.0 %collective-permute-start.4 = (f32[2,16,768]{2,1,0:T(8,128)S(1)}, f32[2,16,768]{2,1,0:T(8,128)}, u32[]{:S(2)}, u32[]{:S(2)}) collective-permute-start(f32[2,16,768]{2,1,0:T(8,128)S(1)} %pad_maximum_fusion.9), channel_id=1, source_target_pairs={{0,8},{4,12},{1,9},{5,13},{2,10},{6,14},{3,11},{7,15},{16,24},{20,... | collective-permute-start | bytes 294920 | tf_op jit(solution)/shard_map/ppermute | solution.py:45
  129.4 20.3 %collective-permute-start.7 = (bf16[256,1536]{1,0:T(8,128)(2,1)}, bf16[256,1536]{1,0:T(8,128)(2,1)}, u32[]{:S(2)}, u32[]{:S(2)}) collective-permute-start(bf16[256,1536]{1,0:T(8,128)(2,1)} %add_convert_fusion.4), channel_id=1, source_target_pairs={{0,2},{1,3},{2,0},{3,1},{4,6},{5,7},{6,4},{7,5},{8,10},{9,11},{10,... | collective-permute-start | bytes 2359304 | tf_op jit(solution)/shard_map/ppermute | solution.py:40
  154.9 20.3 %collective-permute-start.10 = (bf16[256,1536]{1,0:T(8,128)(2,1)}, bf16[256,1536]{1,0:T(8,128)(2,1)}, u32[]{:S(2)}, u32[]{:S(2)}) collective-permute-start(bf16[256,1536]{1,0:T(8,128)(2,1)} %multiply_convert_fusion.8), channel_id=1, source_target_pairs={{0,2},{1,3},{2,0},{3,1},{4,6},{5,7},{6,4},{7,5},{8,10},{9,11},{10,... | collective-permute-start | bytes 2359304 | tf_op jit(solution)/shard_map/ppermute | solution.py:40
  191.9 20.2 %collective-permute-start.9 = (bf16[256,1536]{1,0:T(8,128)(2,1)S(1)}, bf16[256,1536]{1,0:T(8,128)(2,1)S(1)}, u32[]{:S(2)}, u32[]{:S(2)}) collective-permute-start(bf16[256,1536]{1,0:T(8,128)(2,1)S(1)} %constant_dynamic-slice_fusion.5), channel_id=1, source_target_pairs={{0,1},{1,0},{2,3},{3,2},{4,5},{5,4},{6,7},{7,6},{8,9},{9,8},{10,11... | collective-permute-start | bytes 2359304 | tf_op jit(solution)/shard_map/ppermute | solution.py:40
  193.7 19.7 %collective-permute-start.13 = (bf16[256,1536]{1,0:T(8,128)(2,1)S(1)}, bf16[256,1536]{1,0:T(8,128)(2,1)S(1)}, u32[]{:S(2)}, u32[]{:S(2)}) collective-permute-start(bf16[256,1536]{1,0:T(8,128)(2,1)S(1)} %add_convert_fusion.3), channel_id=1, source_target_pairs={{0,2},{1,3},{2,0},{3,1},{4,6},{5,7},{6,4},{7,5},{8,10},{9,11},{10,... | collective-permute-start | bytes 2359304 | tf_op jit(solution)/shard_map/ppermute | solution.py:40
  206.4 70.2 %collective-permute-start.20 = (bf16[2,2,192,2048]{3,2,1,0:T(8,128)(2,1)}, bf16[2,2,192,2048]{3,2,1,0:T(8,128)(2,1)}, u32[]{:S(2)}, u32[]{:S(2)}) collective-permute-start(bf16[2,2,192,2048]{3,2,1,0:T(8,128)(2,1)} %pad_maximum_fusion.2), channel_id=1, source_target_pairs={{0,16},{16,0},{1,17},{17,1},{2,18},{18,2},{3,19},{19,3},{4,20},{20... | collective-permute-start | bytes 9437192 | tf_op jit(solution)/shard_map/ppermute | solution.py:40
  212.0 53.1 %collective-permute-start.21 = (bf16[2,2,192,1024]{3,2,1,0:T(8,128)(2,1)S(1)}, bf16[2,2,192,1024]{3,2,1,0:T(8,128)(2,1)}, u32[]{:S(2)}, u32[]{:S(2)}) collective-permute-start(bf16[2,2,192,1024]{3,2,1,0:T(8,128)(2,1)S(1)} %dynamic-slice_bitcast_fusion), channel_id=1, source_target_pairs={{0,4},{4,0},{8,12},{12,8},{1,5},{5,1},{9,13},{13,9},{2,6},{6,2},{1... | collective-permute-start | bytes 4718600 | tf_op jit(solution)/shard_map/ppermute | solution.py:40
  218.8 19.0 %collective-permute-start.15 = (bf16[256,1536]{1,0:T(8,128)(2,1)S(1)}, bf16[256,1536]{1,0:T(8,128)(2,1)S(1)}, u32[]{:S(2)}, u32[]{:S(2)}) collective-permute-start(bf16[256,1536]{1,0:T(8,128)(2,1)S(1)} %get-tuple-element.127), channel_id=1, source_target_pairs={{0,2},{1,3},{2,0},{3,1},{4,6},{5,7},{6,4},{7,5},{8,10},{9,11},{10,... | collective-permute-start | bytes 2359304 | tf_op jit(solution)/shard_map/ppermute | solution.py:40
  219.7 18.1 %collective-permute-start.16 = (bf16[256,1536]{1,0:T(8,128)(2,1)S(1)}, bf16[256,1536]{1,0:T(8,128)(2,1)S(1)}, u32[]{:S(2)}, u32[]{:S(2)}) collective-permute-start(bf16[256,1536]{1,0:T(8,128)(2,1)S(1)} %get-tuple-element.127), channel_id=1, source_target_pairs={{0,1},{1,0},{2,3},{3,2},{4,5},{5,4},{6,7},{7,6},{8,9},{9,8},{10,11... | collective-permute-start | bytes 2359304 | tf_op jit(solution)/shard_map/ppermute | solution.py:40
  238.9 62.9 %collective-permute-start.14 = (bf16[256,1536]{1,0:T(8,128)(2,1)}, bf16[256,1536]{1,0:T(8,128)(2,1)}, u32[]{:S(2)}, u32[]{:S(2)}) collective-permute-start(bf16[256,1536]{1,0:T(8,128)(2,1)} %constant_dynamic-slice_fusion.3), channel_id=1, source_target_pairs={{0,1},{1,0},{2,3},{3,2},{4,5},{5,4},{6,7},{7,6},{8,9},{9,8},{10,11... | collective-permute-start | bytes 2359304 | tf_op jit(solution)/shard_map/ppermute | solution.py:40
  241.3 35.3 %collective-permute-start.18 = (bf16[256,1536]{1,0:T(8,128)(2,1)}, bf16[256,1536]{1,0:T(8,128)(2,1)S(1)}, u32[]{:S(2)}, u32[]{:S(2)}) collective-permute-start(bf16[256,1536]{1,0:T(8,128)(2,1)} %add_convert_fusion.2), channel_id=1, source_target_pairs={{0,2},{1,3},{2,0},{3,1},{4,6},{5,7},{6,4},{7,5},{8,10},{9,11},{10,... | collective-permute-start | bytes 2359304 | tf_op jit(solution)/shard_map/ppermute | solution.py:40
  300.1 35.9 %collective-permute-start.26 = (bf16[2,192,2048]{2,1,0:T(8,128)(2,1)}, bf16[2,192,2048]{2,1,0:T(8,128)(2,1)}, u32[]{:S(2)}, u32[]{:S(2)}) collective-permute-start(bf16[2,192,2048]{2,1,0:T(8,128)(2,1)} %fusion.7), channel_id=1, source_target_pairs={{0,4},{4,0},{8,12},{12,8},{1,5},{5,1},{9,13},{13,9},{2,6},{6,2},{1... | collective-permute-start | bytes 4718600 | tf_op jit(solution)/shard_map/ppermute | solution.py:40
  303.7 31.4 %collective-permute-start.27 = (bf16[2,192,1024]{2,1,0:T(8,128)(2,1)S(1)}, bf16[2,192,1024]{2,1,0:T(8,128)(2,1)S(1)}, u32[]{:S(2)}, u32[]{:S(2)}) collective-permute-start(bf16[2,192,1024]{2,1,0:T(8,128)(2,1)S(1)} %fusion.40), channel_id=1, source_target_pairs={{0,16},{16,0},{1,17},{17,1},{2,18},{18,2},{3,19},{19,3},{4,20},{20... | collective-permute-start | bytes 2359304 | tf_op jit(solution)/shard_map/ppermute | solution.py:40
  307.6 27.4 %collective-permute-start.24 = (bf16[256,1536]{1,0:T(8,128)(2,1)}, bf16[256,1536]{1,0:T(8,128)(2,1)S(1)}, u32[]{:S(2)}, u32[]{:S(2)}) collective-permute-start(bf16[256,1536]{1,0:T(8,128)(2,1)} %add_convert_fusion.1), channel_id=1, source_target_pairs={{0,2},{1,3},{2,0},{3,1},{4,6},{5,7},{6,4},{7,5},{8,10},{9,11},{10,... | collective-permute-start | bytes 2359304 | tf_op jit(solution)/shard_map/ppermute | solution.py:40
  340.6 57.7 %collective-permute-start.30 = (bf16[2,2,192,1536]{3,2,1,0:T(8,128)(2,1)}, bf16[2,2,192,1536]{3,2,1,0:T(8,128)(2,1)}, u32[]{:S(2)}, u32[]{:S(2)}) collective-permute-start(bf16[2,2,192,1536]{3,2,1,0:T(8,128)(2,1)} %pad_maximum_fusion.3), channel_id=1, source_target_pairs={{0,16},{16,0},{1,17},{17,1},{2,18},{18,2},{3,19},{19,3},{4,20},{20... | collective-permute-start | bytes 7077896 | tf_op jit(solution)/shard_map/ppermute | solution.py:40
  347.3 50.9 %collective-permute-start.28 = (bf16[192,2048]{1,0:T(8,128)(2,1)S(1)}, bf16[192,2048]{1,0:T(8,128)(2,1)}, u32[]{:S(2)}, u32[]{:S(2)}) collective-permute-start(bf16[192,2048]{1,0:T(8,128)(2,1)S(1)} %fusion.39), channel_id=1, source_target_pairs={{0,8},{4,12},{8,0},{12,4},{1,9},{5,13},{9,1},{13,5},{2,10},{6,14},... | collective-permute-start | bytes 2359304 | tf_op jit(solution)/shard_map/ppermute | solution.py:40
  351.1 47.2 %collective-permute-start.29 = (bf16[192,1024]{1,0:T(8,128)(2,1)S(1)}, bf16[192,1024]{1,0:T(8,128)(2,1)}, u32[]{:S(2)}, u32[]{:S(2)}) collective-permute-start(bf16[192,1024]{1,0:T(8,128)(2,1)S(1)} %fusion.48), channel_id=1, source_target_pairs={{0,8},{4,12},{8,0},{12,4},{1,9},{5,13},{9,1},{13,5},{2,10},{6,14},... | collective-permute-start | bytes 1179656 | tf_op jit(solution)/shard_map/ppermute | solution.py:40
  354.2 106.8 %collective-permute-start.25 = (bf16[256,1536]{1,0:T(8,128)(2,1)}, bf16[256,1536]{1,0:T(8,128)(2,1)}, u32[]{:S(2)}, u32[]{:S(2)}) collective-permute-start(bf16[256,1536]{1,0:T(8,128)(2,1)} %add_convert_fusion.1), channel_id=1, source_target_pairs={{0,1},{1,0},{2,3},{3,2},{4,5},{5,4},{6,7},{7,6},{8,9},{9,8},{10,11... | collective-permute-start | bytes 2359304 | tf_op jit(solution)/shard_map/ppermute | solution.py:40
  405.7 38.6 %collective-permute-start.36 = (bf16[2,192,1536]{2,1,0:T(8,128)(2,1)}, bf16[2,192,1536]{2,1,0:T(8,128)(2,1)}, u32[]{:S(2)}, u32[]{:S(2)}) collective-permute-start(bf16[2,192,1536]{2,1,0:T(8,128)(2,1)} %fusion.16), channel_id=1, source_target_pairs={{0,4},{4,0},{8,12},{12,8},{1,5},{5,1},{9,13},{13,9},{2,6},{6,2},{1... | collective-permute-start | bytes 3538952 | tf_op jit(solution)/shard_map/ppermute | solution.py:40
  440.1 13.4 %collective-permute-start.34 = (bf16[256,1536]{1,0:T(8,128)(2,1)}, bf16[256,1536]{1,0:T(8,128)(2,1)}, u32[]{:S(2)}, u32[]{:S(2)}) collective-permute-start(bf16[256,1536]{1,0:T(8,128)(2,1)} %constant_dynamic-slice_fusion.1), channel_id=1, source_target_pairs={{0,1},{1,0},{2,3},{3,2},{4,5},{5,4},{6,7},{7,6},{8,9},{9,8},{10,11... | collective-permute-start | bytes 2359304 | tf_op jit(solution)/shard_map/ppermute | solution.py:40
  446.5 61.8 %collective-permute-start.52 = (bf16[192,1536]{1,0:T(8,128)(2,1)}, bf16[192,1536]{1,0:T(8,128)(2,1)}, u32[]{:S(2)}, u32[]{:S(2)}) collective-permute-start(bf16[192,1536]{1,0:T(8,128)(2,1)} %fusion.44), channel_id=1, source_target_pairs={{0,8},{4,12},{8,0},{12,4},{1,9},{5,13},{9,1},{13,5},{2,10},{6,14},... | collective-permute-start | bytes 1769480 | tf_op jit(solution)/shard_map/ppermute | solution.py:40
  451.1 15.0 %collective-permute-start.37 = (bf16[256,1536]{1,0:T(8,128)(2,1)S(1)}, bf16[256,1536]{1,0:T(8,128)(2,1)S(1)}, u32[]{:S(2)}, u32[]{:S(2)}) collective-permute-start(bf16[256,1536]{1,0:T(8,128)(2,1)S(1)} %constant_dynamic-slice_fusion), channel_id=1, source_target_pairs={{0,1},{1,0},{2,3},{3,2},{4,5},{5,4},{6,7},{7,6},{8,9},{9,8},{10,11... | collective-permute-start | bytes 2359304 | tf_op jit(solution)/shard_map/ppermute | solution.py:40
  454.8 19.8 %collective-permute-start.38 = (bf16[256,1536]{1,0:T(8,128)(2,1)S(1)}, bf16[256,1536]{1,0:T(8,128)(2,1)S(1)}, u32[]{:S(2)}, u32[]{:S(2)}) collective-permute-start(bf16[256,1536]{1,0:T(8,128)(2,1)S(1)} %add_convert_fusion), channel_id=1, source_target_pairs={{0,2},{1,3},{2,0},{3,1},{4,6},{5,7},{6,4},{7,5},{8,10},{9,11},{10,... | collective-permute-start | bytes 2359304 | tf_op jit(solution)/shard_map/ppermute | solution.py:40
  462.5 28.3 %collective-permute-start.43 = (bf16[2,2,224,384]{3,2,1,0:T(8,128)(2,1)}, bf16[2,2,224,384]{3,2,1,0:T(8,128)(2,1)}, u32[]{:S(2)}, u32[]{:S(2)}) collective-permute-start(bf16[2,2,224,384]{3,2,1,0:T(8,128)(2,1)} %dynamic-slice_bitcast_fusion.11), channel_id=1, source_target_pairs={{0,4},{4,0},{8,12},{12,8},{1,5},{5,1},{9,13},{13,9},{2,6},{6,2},{1... | collective-permute-start | bytes 2064392 | tf_op jit(solution)/shard_map/ppermute | solution.py:40
  465.4 27.9 %collective-permute-start.42 = (bf16[2,2,224,384]{3,2,1,0:T(8,128)(2,1)}, bf16[2,2,224,384]{3,2,1,0:T(8,128)(2,1)}, u32[]{:S(2)}, u32[]{:S(2)}) collective-permute-start(bf16[2,2,224,384]{3,2,1,0:T(8,128)(2,1)} %dynamic-slice_bitcast_fusion.12), channel_id=1, source_target_pairs={{0,16},{16,0},{1,17},{17,1},{2,18},{18,2},{3,19},{19,3},{4,20},{20... | collective-permute-start | bytes 2064392 | tf_op jit(solution)/shard_map/ppermute | solution.py:40
  477.0 20.6 %collective-permute-start.39 = (bf16[256,1536]{1,0:T(8,128)(2,1)}, bf16[256,1536]{1,0:T(8,128)(2,1)}, u32[]{:S(2)}, u32[]{:S(2)}) collective-permute-start(bf16[256,1536]{1,0:T(8,128)(2,1)} %fusion.35), channel_id=1, source_target_pairs={{0,2},{1,3},{2,0},{3,1},{4,6},{5,7},{6,4},{7,5},{8,10},{9,11},{10,... | collective-permute-start | bytes 2359304 | tf_op jit(solution)/shard_map/ppermute | solution.py:40
  478.8 19.5 %collective-permute-start.40 = (bf16[256,1536]{1,0:T(8,128)(2,1)}, bf16[256,1536]{1,0:T(8,128)(2,1)}, u32[]{:S(2)}, u32[]{:S(2)}) collective-permute-start(bf16[256,1536]{1,0:T(8,128)(2,1)} %fusion.35), channel_id=1, source_target_pairs={{0,1},{1,0},{2,3},{3,2},{4,5},{5,4},{6,7},{7,6},{8,9},{9,8},{10,11... | collective-permute-start | bytes 2359304 | tf_op jit(solution)/shard_map/ppermute | solution.py:40
  498.3 41.3 %collective-permute-start.44 = (bf16[256,1536]{1,0:T(8,128)(2,1)}, bf16[256,1536]{1,0:T(8,128)(2,1)}, u32[]{:S(2)}, u32[]{:S(2)}) collective-permute-start(bf16[256,1536]{1,0:T(8,128)(2,1)} %collective-permute-done.39), channel_id=1, source_target_pairs={{0,1},{1,0},{2,3},{3,2},{4,5},{5,4},{6,7},{7,6},{8,9},{9,8},{10,11... | collective-permute-start | bytes 2359304 | tf_op jit(solution)/shard_map/ppermute | solution.py:40
  503.8 28.2 %collective-permute-start.53 = (bf16[224,384]{1,0:T(8,128)(2,1)S(1)}, bf16[224,384]{1,0:T(8,128)(2,1)S(1)}, u32[]{:S(2)}, u32[]{:S(2)}) collective-permute-start(bf16[224,384]{1,0:T(8,128)(2,1)S(1)} %fusion.57), channel_id=1, source_target_pairs={{0,8},{4,12},{8,0},{12,4},{1,9},{5,13},{9,1},{13,5},{2,10},{6,14},... | collective-permute-start | bytes 516104 | tf_op jit(solution)/shard_map/ppermute | solution.py:40
  507.9 24.1 %collective-permute-start.51 = (bf16[224,384]{1,0:T(8,128)(2,1)S(1)}, bf16[224,384]{1,0:T(8,128)(2,1)S(1)}, u32[]{:S(2)}, u32[]{:S(2)}) collective-permute-start(bf16[224,384]{1,0:T(8,128)(2,1)S(1)} %fusion.59), channel_id=1, source_target_pairs={{0,8},{4,12},{8,0},{12,4},{1,9},{5,13},{9,1},{13,5},{2,10},{6,14},... | collective-permute-start | bytes 516104 | tf_op jit(solution)/shard_map/ppermute | solution.py:40
  509.4 21.4 %collective-permute-start.49 = (bf16[80,768]{1,0:T(8,128)(2,1)S(1)}, bf16[80,768]{1,0:T(8,128)(2,1)S(1)}, u32[]{:S(2)}, u32[]{:S(2)}) collective-permute-start(bf16[80,768]{1,0:T(8,128)(2,1)S(1)} %add_convert_fusion.10), channel_id=1, source_target_pairs={{0,8},{4,12},{8,0},{12,4},{1,9},{5,13},{9,1},{13,5},{2,10},{6,14},... | collective-permute-start | bytes 368648 | tf_op jit(solution)/shard_map/ppermute | solution.py:40
  (128 other events, 848.4 us)

commit v5 on v4

--- a/solution.py
+++ b/solution.py
@@ -691,7 +691,7 @@
 def norm_kernel(rows, gain, out):
     values = rows[...].astype(f32)
     scale = lax.rsqrt(jnp.mean(values * values, axis=-1, keepdims=True) + epsilon)
-    out[...] = (values * scale * gain[...]).astype(bf16)
+    out[...] = (values * scale * gain[...].astype(f32)[None, :]).astype(bf16)
 
 
 def norm_call(count, features):
@@ -701,7 +701,7 @@
         grid=(count // tall,),
         in_specs=[
             pl.BlockSpec((tall, features), lambda i: (i, 0)),
-            pl.BlockSpec((1, features), lambda i: (0, 0)),
+            pl.BlockSpec((features,), lambda i: (0,)),
         ],
         out_specs=pl.BlockSpec((tall, features), lambda i: (i, 0)),
         out_shape=jax.ShapeDtypeStruct((count, features), bf16),
@@ -797,7 +797,7 @@
 
     gain_one = first_gain.astype(f32)
     gain_two = second_gain.astype(f32)
-    normed = norm_call(count, features)(rows, gain_one[None])
+    normed = norm_call(count, features)(rows, first_gain)
     inner = matmul(normed, input_proj).astype(bf16)
     rim = shifted(inner[count - width + 1 :], "seq", 1)
     gate_in = matmul(normed, gate_proj)
@@ -904,7 +904,7 @@
     heads, head_total = scan_heads(
         rates, after(grad_scanned, results.middle), scan_proj, decay_two, sums
     )
-    head_total = after(head_total, [item.got for item in ffn_sums], results.second)
+    head_total = after(head_total, down_sum.got, results.second)
 
     mixer_weights = []
 
@@ -916,7 +916,7 @@
     def gate_weights(begun):
         value = transposed_left(normed, after(grad_gate_in, begun)).astype(bf16)
         mixer_weights.append(value)
-        return [value]
+        return [value, pair_sum.got]
 
     leaving = chained(product_total, head_total, -1, [output_weights, gate_weights])
     sent = [item.send(leaving) for item in ffn_sums]
@@ -1027,15 +1027,17 @@
     sent = [item.send(tokens_last.own) for item in input_sums]
     done = pair_sum.total(tokens_last.own)
     blocks = tokens_last.blocks(done, gains, sent)
+    gains = sum_step(gains, ("chan", 2), blocks[2])
+    gains = jnp.pad(gains, ((0, -gains.shape[0] % 16), (0, 0)))
+    vectors = jnp.concatenate([lines, gains], axis=0)
     while input_sums[0].order:
         sent = [item.send(blocks[2]) for item in input_sums]
-    gains = sum_step(gains, ("chan", 2))
-    gains = jnp.pad(gains, ((0, -gains.shape[0] % 16), (0, 0)))
-    vectors = jnp.concatenate([lines, gains], axis=0)
-    for bit in shard_bits:
-        vectors = sum_step(vectors, bit, sent)
+    for bit in usual[:-1]:
+        vectors = sum_step(vectors, bit)
+    early = vectors
+    vectors = sum_step(vectors, usual[-1])
     tokens_out = at_home(blocks, f32)
-    done += down_sum.total(sent) + mixer_sum.total(sent)
+    done += down_sum.total(sent, early) + mixer_sum.total(sent, early)
     input_parts = [item.total(done)[0] for item in input_sums]
     first = share + 2 * low_rows
     gains = vectors[lines_used:].astype(f32)

time: 549 us -> 535 us (0.974)
    unnamed x219 -> x225, local copies, waits for them, and re-layouts: 21.2 us -> 20.6 us
  transfers between devices with their start and end apart: 54 -> 54, of which waited for: 21 -> 22; matrix products, arithmetic and copies ran while one was open for 33% -> 33% of each run, Pallas kernels for 17% -> 17%
where the time goes in v5:
time: 535 us; the launch traced here: 527 us
  Pallas kernels  138 us (26%)
  matrix products  93.5 us (17%)
  waiting for transfers between devices  93 us (17%)
  other arithmetic  80.6 us (15%)
  starting transfers between devices  60.6 us (11%)
  local copies, waits for them, and re-layouts  59.1 us (11%)
    ppermute x48, waiting for transfers between devices, swap(): lax.ppermute(value, axis, [(i, i ^ mask) for i in range(lax.axis_size(axi...  81.1 us
    pallas_call x1, Pallas kernels, per_device(): second_scan(*scan_inputs, begin, before, skip, step_padded, *kept)  39 us
    dot_general x12, matrix products, matmul(): return jnp.dot(left, right, preferred_element_type=f32)  36.2 us
    ppermute x48, starting transfers between devices, swap(): lax.ppermute(value, axis, [(i, i ^ mask) for i in range(lax.axis_size(axi...  31.4 us
    dot_general x10, matrix products, transposed_right(): lax.dot_general(left, right, (((1,), (1,)), ((), ())), preferred_element_...  31.4 us
    ppermute x6, starting transfers between devices, shifted(): lax.ppermute(value, axis, [(i, i + by) for i in range(size) if 0 <= i + b...  29.2 us
    pallas_call x1, Pallas kernels, per_device(): scan_forward[0](*scan3, decay_two, gate3, skip, ends, sums, arriving)  27.3 us
    dot_general x8, matrix products, transposed_left(): lax.dot_general(left, right, (((0,), (0,)), ((), ())), preferred_element_...  25.8 us
  transfers between devices with their start and end apart: 54, of which 22 were waited for; matrix products, arithmetic and copies ran while one was open for 33% of the time, Pallas kernels for 17%

profile of v5, /device:TPU:0, one launch (start us, length us, event | category | flops | bytes accessed | tf_op | source)
XLA Modules:
  0.0 527.5 jit_solution(908405335528847867)
XLA Ops:
  0.7 4.9 norm_rows.1
  5.5 5.2 convolution_convert_fusion.11.inner
  11.9 4.9 collective-permute-start
  16.9 6.9 %fusion.100 = f32[1024,768]{1,0:T(8,128)} fusion(bf16[1024,1536]{1,0:T(8,128)(2,1)} %norm_rows.1, bf16[1536,768]{1,0:T(8,128)(2,1)} %param.24), kind=kOutput, calls=%fused_computation.293 | convolution fusion | flops 2415919104 | bytes 8650752 | tf_op jit(solution)/shard_map/dot_general | solution.py:28
  27.0 3.8 fusion.96
  43.0 3.5 compare_select_fusion.rates.refs_0_
  46.5 15.6 %scan_ends.1 = (f32[16,8,768]{2,1,0:T(8,128)}, f32[8,768]{1,0:T(8,128)}, f32[16,768]{1,0:T(8,128)}, f32[16,768]{1,0:T(8,128)}) custom-call(f32[1024,768]{1,0:T(8,128)} %compare_select_fusion.rates.refs_0_, f32[1024,768]{1,0:T(8,128)} %get-tuple-element.203.mixed.refs_1_, f32[1024,128]{1,0:T(8,128)} %broadcast_select_fusion.4.proj.refs_3_, ...), custom_call_target="tpu_custom_call" | custom-call | flops 12582912 | tf_op jit(solution)/shard_map/scan_ends/pallas_call | solution.py:830
  62.9 3.5 collective-permute-start.3
  69.5 16.3 %collective-permute-start.4 = (f32[2,16,768]{2,1,0:T(8,128)S(1)}, f32[2,16,768]{2,1,0:T(8,128)}, u32[]{:S(2)}, u32[]{:S(2)}) collective-permute-start(f32[2,16,768]{2,1,0:T(8,128)S(1)} %pad_maximum_fusion.9), channel_id=1, source_target_pairs={{0,8},{4,12},{1,9},{5,13},{2,10},{6,14},{3,11},{7,15},{16,24},{20,... | collective-permute-start | bytes 294920 | tf_op jit(solution)/shard_map/ppermute | solution.py:45
  87.9 27.3 %scan_forward.1 = (bf16[1024,768]{1,0:T(8,128)(2,1)}, bf16[1024,768]{1,0:T(8,128)(2,1)}, bf16[16,1040,768]{2,1,0:T(8,128)(2,1)}, f32[16,8,768]{2,1,0:T(8,128)}) custom-call(f32[8,128,768]{2,1,0:T(8,128)} %bitcast.313, f32[8,128,768]{2,1,0:T(8,128)} %bitcast.314, f32[8,128,128]{2,1,0:T(8,128)} %bitcast.315, ...), custom_call_target="tpu_custom_call" | custom-call | flops 12582912 | tf_op jit(solution)/shard_map/scan_forward/pallas_call | solution.py:842
  129.7 18.7 %collective-permute-done.7 = bf16[256,1536]{1,0:T(8,128)(2,1)} collective-permute-done((bf16[256,1536]{1,0:T(8,128)(2,1)}, bf16[256,1536]{1,0:T(8,128)(2,1)}, u32[]{:S(2)}, u32[]{:S(2)}) %collective-permute-start.7) | collective-permute-done | bytes 786464 | tf_op jit(solution)/shard_map/ppermute | solution.py:40
  162.4 3.7 multiply_convert_fusion.5
  194.1 3.7 convolution_convert_fusion.3
  197.9 3.8 convolution_convert_fusion.2
  206.8 3.9 convolution_convert_fusion.1
  222.2 14.5 %collective-permute-done.15 = bf16[256,1536]{1,0:T(8,128)(2,1)S(1)} collective-permute-done((bf16[256,1536]{1,0:T(8,128)(2,1)S(1)}, bf16[256,1536]{1,0:T(8,128)(2,1)S(1)}, u32[]{:S(2)}, u32[]{:S(2)}) %collective-permute-start.15) | collective-permute-done | bytes 786464 | tf_op jit(solution)/shard_map/ppermute | solution.py:40
  242.3 5.9 %multiply_reduce_fusion = (bf16[768]{0:T(1024)(128)(2,1)}, f32[1024,768]{1,0:T(8,128)}, bf16[1024,768]{1,0:T(8,128)(2,1)}) fusion(bf16[1024,768]{1,0:T(8,128)(2,1)S(1)} %copy-done.5, f32[1024,768]{1,0:T(8,128)S(1)} %copy-done.30, bf16[1024,768]{1,0:T(8,128)(2,1)S(1)} %copy-done.98, bf16[1024,1536]{1,0:T(8,128)(2,1)S(1)} %constant_dynamic-update-slice_fusion.4, ...), kind=kOutput, calls=%fused_computation.28 | convolution fusion | flops 2428501248 | bytes 16516608 | tf_op jit(solution)/shard_map/dot_general | solution.py:36
  248.2 15.8 %scan_heads.1 = (f32[16,8,768]{2,1,0:T(8,128)}, f32[16,768]{1,0:T(8,128)}) custom-call(f32[1024,768]{1,0:T(8,128)} %compare_select_fusion.rates.refs_0_, f32[1024,768]{1,0:T(8,128)} %get-tuple-element.126.slope.refs_2_, f32[1024,128]{1,0:T(8,128)} %broadcast_select_fusion.4.proj.refs_3_, f32[16,768]{1,0:T(8,128)} %bitcast_multiply_fusion.4.dec.refs_3_.refs_4_, ...), custom_call_target="tpu_custom_call" | custom-call | flops 12582912 | tf_op jit(solution)/shard_map/scan_heads/pallas_call | solution.py:904
  266.5 6.5 %convolution_convert_fusion.6 = bf16[1536,768]{1,0:T(8,128)(2,1)} fusion(bf16[1024,1536]{1,0:T(8,128)(2,1)} %copy-done.24, bf16[1024,768]{1,0:T(8,128)(2,1)} %get-tuple-element.114), kind=kOutput, calls=%fused_computation.7 | convolution fusion | flops 2417098752 | bytes 7077888 | tf_op jit(solution)/shard_map/dot_general | solution.py:32
  274.3 4.2 convolution_convert_fusion.5
  278.5 4.6 collective-permute-done.22
  296.5 25.5 %scan_backward.2 = (bf16[1024,768]{1,0:T(8,128)(2,1)}, f32[1024,768]{1,0:T(8,128)}, f32[1024,128]{1,0:T(8,128)}, f32[16,768]{1,0:T(8,128)}, f32[1,768]{1,0:T(1,128)}) custom-call(f32[1024,768]{1,0:T(8,128)} %compare_select_fusion.rates.refs_0_, f32[1024,768]{1,0:T(8,128)} %get-tuple-element.203.mixed.refs_1_, f32[1024,768]{1,0:T(8,128)} %get-tuple-element.126.slope.refs_2_, ...), custom_call_target="tpu_custom_call" | custom-call | flops 12582912 | tf_op jit(solution)/shard_map/scan_backward/pallas_call | solution.py:929
  342.1 39.0 %scan_backward.3 = (bf16[1024,768]{1,0:T(8,128)(2,1)}, f32[1024,768]{1,0:T(8,128)}, f32[1024,128]{1,0:T(8,128)}, f32[16,768]{1,0:T(8,128)}, f32[1,768]{1,0:T(1,128)}) custom-call(f32[1024,768]{1,0:T(8,128)} %compare_select_fusion.rates.refs_0_, ...), custom_call_target="tpu_custom_call", output_to_operand_aliasing={{0}: (11, {}), {1}: (12, {}), {3}: (13, {}), {4}: (14, {})} | custom-call | flops 12582912 | tf_op jit(solution)/shard_map/scan_backward/pallas_call | solution.py:934
  397.6 4.0 convolution_convert_fusion
  407.0 9.8 %conv_backward.1 = (bf16[1024,768]{1,0:T(8,128)(2,1)}, f32[16,768]{1,0:T(8,128)}, f32[8,768]{1,0:T(8,128)}, f32[8,768]{1,0:T(8,128)}) custom-call(bf16[1024,128]{1,0:T(8,128)(2,1)} %add_convert_fusion.5.low, bf16[768,128]{1,0:T(8,128)(2,1)} %state_proj.1, f32[1024,768]{1,0:T(8,128)} %get-tuple-element.156.direct, bf16[1024,768]{1,0:T(8,128)(2,1)} %copy-done.7, ...), custom_call_target="tpu_custom_call" | custom-call | flops 1024 | tf_op jit(solution)/shard_map/conv_backward/pallas_call | solution.py:953
  419.1 5.1 collective-permute-done.33
  424.8 3.8 fusion.8
  456.1 8.3 %collective-permute-done.38 = bf16[256,1536]{1,0:T(8,128)(2,1)S(1)} collective-permute-done((bf16[256,1536]{1,0:T(8,128)(2,1)S(1)}, bf16[256,1536]{1,0:T(8,128)(2,1)S(1)}, u32[]{:S(2)}, u32[]{:S(2)}) %collective-permute-start.38) | collective-permute-done | bytes 786464 | tf_op jit(solution)/shard_map/ppermute | solution.py:40
  468.1 3.7 convert_add_fusion.10
  471.8 8.5 %collective-permute-done.43 = bf16[2,2,224,384]{3,2,1,0:T(8,128)(2,1)} collective-permute-done((bf16[2,2,224,384]{3,2,1,0:T(8,128)(2,1)}, bf16[2,2,224,384]{3,2,1,0:T(8,128)(2,1)}, u32[]{:S(2)}, u32[]{:S(2)}) %collective-permute-start.43) | collective-permute-done | bytes 688160 | tf_op jit(solution)/shard_map/ppermute | solution.py:40
  488.4 4.0 collective-permute-done.51
  506.9 6.1 %collective-permute-done.47 = bf16[80,768]{1,0:T(8,128)(2,1)S(1)} collective-permute-done((bf16[80,768]{1,0:T(8,128)(2,1)S(1)}, bf16[80,768]{1,0:T(8,128)(2,1)S(1)}, u32[]{:S(2)}, u32[]{:S(2)}) %collective-permute-start.47) | collective-permute-done | bytes 122912 | tf_op jit(solution)/shard_map/ppermute | solution.py:40
  (487 shorter events, 229.9 us)
Async XLA Ops:
  11.9 13.3 %collective-permute-start = (bf16[3,768]{1,0:T(4,128)(2,1)S(1)}, bf16[3,768]{1,0:T(4,128)(2,1)S(1)}, u32[]{:S(2)}, u32[]{:S(2)}) collective-permute-start(bf16[3,768]{1,0:T(4,128)(2,1)S(1)} %slice.234), channel_id=1, source_target_pairs={{0,4},{4,8},{8,12},{1,5},{5,9},{9,13},{2,6},{6,10},{10,14},{3,7},{... | collective-permute-start | bytes 13832 | tf_op jit(solution)/shard_map/ppermute | solution.py:45
  69.5 17.0 %collective-permute-start.4 = (f32[2,16,768]{2,1,0:T(8,128)S(1)}, f32[2,16,768]{2,1,0:T(8,128)}, u32[]{:S(2)}, u32[]{:S(2)}) collective-permute-start(f32[2,16,768]{2,1,0:T(8,128)S(1)} %pad_maximum_fusion.9), channel_id=1, source_target_pairs={{0,8},{4,12},{1,9},{5,13},{2,10},{6,14},{3,11},{7,15},{16,24},{20,... | collective-permute-start | bytes 294920 | tf_op jit(solution)/shard_map/ppermute | solution.py:45
  128.2 20.3 %collective-permute-start.7 = (bf16[256,1536]{1,0:T(8,128)(2,1)}, bf16[256,1536]{1,0:T(8,128)(2,1)}, u32[]{:S(2)}, u32[]{:S(2)}) collective-permute-start(bf16[256,1536]{1,0:T(8,128)(2,1)} %add_convert_fusion.4), channel_id=1, source_target_pairs={{0,2},{1,3},{2,0},{3,1},{4,6},{5,7},{6,4},{7,5},{8,10},{9,11},{10,... | collective-permute-start | bytes 2359304 | tf_op jit(solution)/shard_map/ppermute | solution.py:40
  153.7 20.3 %collective-permute-start.10 = (bf16[256,1536]{1,0:T(8,128)(2,1)}, bf16[256,1536]{1,0:T(8,128)(2,1)}, u32[]{:S(2)}, u32[]{:S(2)}) collective-permute-start(bf16[256,1536]{1,0:T(8,128)(2,1)} %multiply_convert_fusion.8), channel_id=1, source_target_pairs={{0,2},{1,3},{2,0},{3,1},{4,6},{5,7},{6,4},{7,5},{8,10},{9,11},{10,... | collective-permute-start | bytes 2359304 | tf_op jit(solution)/shard_map/ppermute | solution.py:40
  190.7 20.2 %collective-permute-start.9 = (bf16[256,1536]{1,0:T(8,128)(2,1)S(1)}, bf16[256,1536]{1,0:T(8,128)(2,1)S(1)}, u32[]{:S(2)}, u32[]{:S(2)}) collective-permute-start(bf16[256,1536]{1,0:T(8,128)(2,1)S(1)} %constant_dynamic-slice_fusion.5), channel_id=1, source_target_pairs={{0,1},{1,0},{2,3},{3,2},{4,5},{5,4},{6,7},{7,6},{8,9},{9,8},{10,11... | collective-permute-start | bytes 2359304 | tf_op jit(solution)/shard_map/ppermute | solution.py:40
  192.5 19.7 %collective-permute-start.13 = (bf16[256,1536]{1,0:T(8,128)(2,1)S(1)}, bf16[256,1536]{1,0:T(8,128)(2,1)S(1)}, u32[]{:S(2)}, u32[]{:S(2)}) collective-permute-start(bf16[256,1536]{1,0:T(8,128)(2,1)S(1)} %add_convert_fusion.3), channel_id=1, source_target_pairs={{0,2},{1,3},{2,0},{3,1},{4,6},{5,7},{6,4},{7,5},{8,10},{9,11},{10,... | collective-permute-start | bytes 2359304 | tf_op jit(solution)/shard_map/ppermute | solution.py:40
  205.2 73.3 %collective-permute-start.23 = (bf16[2,2,192,2048]{3,2,1,0:T(8,128)(2,1)}, bf16[2,2,192,2048]{3,2,1,0:T(8,128)(2,1)}, u32[]{:S(2)}, u32[]{:S(2)}) collective-permute-start(bf16[2,2,192,2048]{3,2,1,0:T(8,128)(2,1)} %pad_maximum_fusion.2), channel_id=1, source_target_pairs={{0,16},{16,0},{1,17},{17,1},{2,18},{18,2},{3,19},{19,3},{4,20},{20... | collective-permute-start | bytes 9437192 | tf_op jit(solution)/shard_map/ppermute | solution.py:40
  210.8 53.1 %collective-permute-start.20 = (bf16[2,2,192,1024]{3,2,1,0:T(8,128)(2,1)S(1)}, bf16[2,2,192,1024]{3,2,1,0:T(8,128)(2,1)}, u32[]{:S(2)}, u32[]{:S(2)}) collective-permute-start(bf16[2,2,192,1024]{3,2,1,0:T(8,128)(2,1)S(1)} %dynamic-slice_bitcast_fusion), channel_id=1, source_target_pairs={{0,4},{4,0},{8,12},{12,8},{1,5},{5,1},{9,13},{13,9},{2,6},{6,2},{1... | collective-permute-start | bytes 4718600 | tf_op jit(solution)/shard_map/ppermute | solution.py:40
  217.6 19.0 %collective-permute-start.15 = (bf16[256,1536]{1,0:T(8,128)(2,1)S(1)}, bf16[256,1536]{1,0:T(8,128)(2,1)S(1)}, u32[]{:S(2)}, u32[]{:S(2)}) collective-permute-start(bf16[256,1536]{1,0:T(8,128)(2,1)S(1)} %get-tuple-element.125), channel_id=1, source_target_pairs={{0,2},{1,3},{2,0},{3,1},{4,6},{5,7},{6,4},{7,5},{8,10},{9,11},{10,... | collective-permute-start | bytes 2359304 | tf_op jit(solution)/shard_map/ppermute | solution.py:40
  218.5 18.1 %collective-permute-start.16 = (bf16[256,1536]{1,0:T(8,128)(2,1)S(1)}, bf16[256,1536]{1,0:T(8,128)(2,1)S(1)}, u32[]{:S(2)}, u32[]{:S(2)}) collective-permute-start(bf16[256,1536]{1,0:T(8,128)(2,1)S(1)} %get-tuple-element.125), channel_id=1, source_target_pairs={{0,1},{1,0},{2,3},{3,2},{4,5},{5,4},{6,7},{7,6},{8,9},{9,8},{10,11... | collective-permute-start | bytes 2359304 | tf_op jit(solution)/shard_map/ppermute | solution.py:40
  237.7 52.0 %collective-permute-start.14 = (bf16[256,1536]{1,0:T(8,128)(2,1)}, bf16[256,1536]{1,0:T(8,128)(2,1)}, u32[]{:S(2)}, u32[]{:S(2)}) collective-permute-start(bf16[256,1536]{1,0:T(8,128)(2,1)} %constant_dynamic-slice_fusion.3), channel_id=1, source_target_pairs={{0,1},{1,0},{2,3},{3,2},{4,5},{5,4},{6,7},{7,6},{8,9},{9,8},{10,11... | collective-permute-start | bytes 2359304 | tf_op jit(solution)/shard_map/ppermute | solution.py:40
  240.1 23.8 %collective-permute-start.18 = (bf16[256,1536]{1,0:T(8,128)(2,1)}, bf16[256,1536]{1,0:T(8,128)(2,1)S(1)}, u32[]{:S(2)}, u32[]{:S(2)}) collective-permute-start(bf16[256,1536]{1,0:T(8,128)(2,1)} %add_convert_fusion.2), channel_id=1, source_target_pairs={{0,2},{1,3},{2,0},{3,1},{4,6},{5,7},{6,4},{7,5},{8,10},{9,11},{10,... | collective-permute-start | bytes 2359304 | tf_op jit(solution)/shard_map/ppermute | solution.py:40
  289.4 34.7 %collective-permute-start.26 = (bf16[2,192,2048]{2,1,0:T(8,128)(2,1)}, bf16[2,192,2048]{2,1,0:T(8,128)(2,1)}, u32[]{:S(2)}, u32[]{:S(2)}) collective-permute-start(bf16[2,192,2048]{2,1,0:T(8,128)(2,1)} %fusion.7), channel_id=1, source_target_pairs={{0,4},{4,0},{8,12},{12,8},{1,5},{5,1},{9,13},{13,9},{2,6},{6,2},{1... | collective-permute-start | bytes 4718600 | tf_op jit(solution)/shard_map/ppermute | solution.py:40
  291.6 30.4 %collective-permute-start.27 = (bf16[2,192,1024]{2,1,0:T(8,128)(2,1)S(1)}, bf16[2,192,1024]{2,1,0:T(8,128)(2,1)S(1)}, u32[]{:S(2)}, u32[]{:S(2)}) collective-permute-start(bf16[2,192,1024]{2,1,0:T(8,128)(2,1)S(1)} %fusion.40), channel_id=1, source_target_pairs={{0,16},{16,0},{1,17},{17,1},{2,18},{18,2},{3,19},{19,3},{4,20},{20... | collective-permute-start | bytes 2359304 | tf_op jit(solution)/shard_map/ppermute | solution.py:40
  294.6 27.5 %collective-permute-start.24 = (bf16[256,1536]{1,0:T(8,128)(2,1)}, bf16[256,1536]{1,0:T(8,128)(2,1)S(1)}, u32[]{:S(2)}, u32[]{:S(2)}) collective-permute-start(bf16[256,1536]{1,0:T(8,128)(2,1)} %add_convert_fusion.1), channel_id=1, source_target_pairs={{0,2},{1,3},{2,0},{3,1},{4,6},{5,7},{6,4},{7,5},{8,10},{9,11},{10,... | collective-permute-start | bytes 2359304 | tf_op jit(solution)/shard_map/ppermute | solution.py:40
  327.8 59.9 %collective-permute-start.30 = (bf16[2,2,192,1536]{3,2,1,0:T(8,128)(2,1)}, bf16[2,2,192,1536]{3,2,1,0:T(8,128)(2,1)}, u32[]{:S(2)}, u32[]{:S(2)}) collective-permute-start(bf16[2,2,192,1536]{3,2,1,0:T(8,128)(2,1)} %pad_maximum_fusion.3), channel_id=1, source_target_pairs={{0,16},{16,0},{1,17},{17,1},{2,18},{18,2},{3,19},{19,3},{4,20},{20... | collective-permute-start | bytes 7077896 | tf_op jit(solution)/shard_map/ppermute | solution.py:40
  335.2 52.5 %collective-permute-start.28 = (bf16[192,2048]{1,0:T(8,128)(2,1)S(1)}, bf16[192,2048]{1,0:T(8,128)(2,1)}, u32[]{:S(2)}, u32[]{:S(2)}) collective-permute-start(bf16[192,2048]{1,0:T(8,128)(2,1)S(1)} %fusion.39), channel_id=1, source_target_pairs={{0,8},{4,12},{8,0},{12,4},{1,9},{5,13},{9,1},{13,5},{2,10},{6,14},... | collective-permute-start | bytes 2359304 | tf_op jit(solution)/shard_map/ppermute | solution.py:40
  338.5 49.2 %collective-permute-start.29 = (bf16[192,1024]{1,0:T(8,128)(2,1)S(1)}, bf16[192,1024]{1,0:T(8,128)(2,1)}, u32[]{:S(2)}, u32[]{:S(2)}) collective-permute-start(bf16[192,1024]{1,0:T(8,128)(2,1)S(1)} %fusion.48), channel_id=1, source_target_pairs={{0,8},{4,12},{8,0},{12,4},{1,9},{5,13},{9,1},{13,5},{2,10},{6,14},... | collective-permute-start | bytes 1179656 | tf_op jit(solution)/shard_map/ppermute | solution.py:40
  342.1 108.2 %collective-permute-start.25 = (bf16[256,1536]{1,0:T(8,128)(2,1)}, bf16[256,1536]{1,0:T(8,128)(2,1)}, u32[]{:S(2)}, u32[]{:S(2)}) collective-permute-start(bf16[256,1536]{1,0:T(8,128)(2,1)} %add_convert_fusion.1), channel_id=1, source_target_pairs={{0,1},{1,0},{2,3},{3,2},{4,5},{5,4},{6,7},{7,6},{8,9},{9,8},{10,11... | collective-permute-start | bytes 2359304 | tf_op jit(solution)/shard_map/ppermute | solution.py:40
  395.1 38.7 %collective-permute-start.36 = (bf16[2,192,1536]{2,1,0:T(8,128)(2,1)}, bf16[2,192,1536]{2,1,0:T(8,128)(2,1)}, u32[]{:S(2)}, u32[]{:S(2)}) collective-permute-start(bf16[2,192,1536]{2,1,0:T(8,128)(2,1)} %fusion.16), channel_id=1, source_target_pairs={{0,4},{4,0},{8,12},{12,8},{1,5},{5,1},{9,13},{13,9},{2,6},{6,2},{1... | collective-permute-start | bytes 3538952 | tf_op jit(solution)/shard_map/ppermute | solution.py:40
  429.6 13.6 %collective-permute-start.34 = (bf16[256,1536]{1,0:T(8,128)(2,1)}, bf16[256,1536]{1,0:T(8,128)(2,1)}, u32[]{:S(2)}, u32[]{:S(2)}) collective-permute-start(bf16[256,1536]{1,0:T(8,128)(2,1)} %constant_dynamic-slice_fusion.1), channel_id=1, source_target_pairs={{0,1},{1,0},{2,3},{3,2},{4,5},{5,4},{6,7},{7,6},{8,9},{9,8},{10,11... | collective-permute-start | bytes 2359304 | tf_op jit(solution)/shard_map/ppermute | solution.py:40
  436.1 77.0 %collective-permute-start.52 = (bf16[192,1536]{1,0:T(8,128)(2,1)}, bf16[192,1536]{1,0:T(8,128)(2,1)}, u32[]{:S(2)}, u32[]{:S(2)}) collective-permute-start(bf16[192,1536]{1,0:T(8,128)(2,1)} %fusion.44), channel_id=1, source_target_pairs={{0,8},{4,12},{8,0},{12,4},{1,9},{5,13},{9,1},{13,5},{2,10},{6,14},... | collective-permute-start | bytes 1769480 | tf_op jit(solution)/shard_map/ppermute | solution.py:40
  440.8 15.3 %collective-permute-start.37 = (bf16[256,1536]{1,0:T(8,128)(2,1)S(1)}, bf16[256,1536]{1,0:T(8,128)(2,1)S(1)}, u32[]{:S(2)}, u32[]{:S(2)}) collective-permute-start(bf16[256,1536]{1,0:T(8,128)(2,1)S(1)} %constant_dynamic-slice_fusion), channel_id=1, source_target_pairs={{0,1},{1,0},{2,3},{3,2},{4,5},{5,4},{6,7},{7,6},{8,9},{9,8},{10,11... | collective-permute-start | bytes 2359304 | tf_op jit(solution)/shard_map/ppermute | solution.py:40
  444.5 19.8 %collective-permute-start.38 = (bf16[256,1536]{1,0:T(8,128)(2,1)S(1)}, bf16[256,1536]{1,0:T(8,128)(2,1)S(1)}, u32[]{:S(2)}, u32[]{:S(2)}) collective-permute-start(bf16[256,1536]{1,0:T(8,128)(2,1)S(1)} %add_convert_fusion), channel_id=1, source_target_pairs={{0,2},{1,3},{2,0},{3,1},{4,6},{5,7},{6,4},{7,5},{8,10},{9,11},{10,... | collective-permute-start | bytes 2359304 | tf_op jit(solution)/shard_map/ppermute | solution.py:40
  451.6 28.6 %collective-permute-start.43 = (bf16[2,2,224,384]{3,2,1,0:T(8,128)(2,1)}, bf16[2,2,224,384]{3,2,1,0:T(8,128)(2,1)}, u32[]{:S(2)}, u32[]{:S(2)}) collective-permute-start(bf16[2,2,224,384]{3,2,1,0:T(8,128)(2,1)} %dynamic-slice_bitcast_fusion.11), channel_id=1, source_target_pairs={{0,4},{4,0},{8,12},{12,8},{1,5},{5,1},{9,13},{13,9},{2,6},{6,2},{1... | collective-permute-start | bytes 2064392 | tf_op jit(solution)/shard_map/ppermute | solution.py:40
  454.5 28.0 %collective-permute-start.42 = (bf16[2,2,224,384]{3,2,1,0:T(8,128)(2,1)}, bf16[2,2,224,384]{3,2,1,0:T(8,128)(2,1)}, u32[]{:S(2)}, u32[]{:S(2)}) collective-permute-start(bf16[2,2,224,384]{3,2,1,0:T(8,128)(2,1)} %dynamic-slice_bitcast_fusion.12), channel_id=1, source_target_pairs={{0,16},{16,0},{1,17},{17,1},{2,18},{18,2},{3,19},{19,3},{4,20},{20... | collective-permute-start | bytes 2064392 | tf_op jit(solution)/shard_map/ppermute | solution.py:40
  466.8 19.4 %collective-permute-start.39 = (bf16[256,1536]{1,0:T(8,128)(2,1)}, bf16[256,1536]{1,0:T(8,128)(2,1)}, u32[]{:S(2)}, u32[]{:S(2)}) collective-permute-start(bf16[256,1536]{1,0:T(8,128)(2,1)} %fusion.35), channel_id=1, source_target_pairs={{0,2},{1,3},{2,0},{3,1},{4,6},{5,7},{6,4},{7,5},{8,10},{9,11},{10,... | collective-permute-start | bytes 2359304 | tf_op jit(solution)/shard_map/ppermute | solution.py:40
  468.0 18.2 %collective-permute-start.40 = (bf16[256,1536]{1,0:T(8,128)(2,1)}, bf16[256,1536]{1,0:T(8,128)(2,1)}, u32[]{:S(2)}, u32[]{:S(2)}) collective-permute-start(bf16[256,1536]{1,0:T(8,128)(2,1)} %fusion.35), channel_id=1, source_target_pairs={{0,1},{1,0},{2,3},{3,2},{4,5},{5,4},{6,7},{7,6},{8,9},{9,8},{10,11... | collective-permute-start | bytes 2359304 | tf_op jit(solution)/shard_map/ppermute | solution.py:40
  486.2 38.6 %collective-permute-start.44 = (bf16[256,1536]{1,0:T(8,128)(2,1)}, bf16[256,1536]{1,0:T(8,128)(2,1)}, u32[]{:S(2)}, u32[]{:S(2)}) collective-permute-start(bf16[256,1536]{1,0:T(8,128)(2,1)} %collective-permute-done.39), channel_id=1, source_target_pairs={{0,1},{1,0},{2,3},{3,2},{4,5},{5,4},{6,7},{7,6},{8,9},{9,8},{10,11... | collective-permute-start | bytes 2359304 | tf_op jit(solution)/shard_map/ppermute | solution.py:40
  486.9 17.0 %collective-permute-start.46 = (bf16[80,768]{1,0:T(8,128)(2,1)}, bf16[80,768]{1,0:T(8,128)(2,1)S(1)}, u32[]{:S(2)}, u32[]{:S(2)}) collective-permute-start(bf16[80,768]{1,0:T(8,128)(2,1)} %pad_dynamic-update-slice_fusion), channel_id=1, source_target_pairs={{0,16},{16,0},{1,17},{17,1},{2,18},{18,2},{3,19},{19,3},{4,20},{20... | collective-permute-start | bytes 368648 | tf_op jit(solution)/shard_map/ppermute | solution.py:40
  493.3 24.7 %collective-permute-start.53 = (bf16[224,384]{1,0:T(8,128)(2,1)S(1)}, bf16[224,384]{1,0:T(8,128)(2,1)S(1)}, u32[]{:S(2)}, u32[]{:S(2)}) collective-permute-start(bf16[224,384]{1,0:T(8,128)(2,1)S(1)} %fusion.57), channel_id=1, source_target_pairs={{0,8},{4,12},{8,0},{12,4},{1,9},{5,13},{9,1},{13,5},{2,10},{6,14},... | collective-permute-start | bytes 516104 | tf_op jit(solution)/shard_map/ppermute | solution.py:40
  496.8 21.2 %collective-permute-start.50 = (bf16[224,384]{1,0:T(8,128)(2,1)S(1)}, bf16[224,384]{1,0:T(8,128)(2,1)S(1)}, u32[]{:S(2)}, u32[]{:S(2)}) collective-permute-start(bf16[224,384]{1,0:T(8,128)(2,1)S(1)} %fusion.59), channel_id=1, source_target_pairs={{0,8},{4,12},{8,0},{12,4},{1,9},{5,13},{9,1},{13,5},{2,10},{6,14},... | collective-permute-start | bytes 516104 | tf_op jit(solution)/shard_map/ppermute | solution.py:40
  (131 other events, 891.4 us)

commit v6 on v5

--- a/solution.py
+++ b/solution.py
@@ -222,7 +222,7 @@
         return tuple(out), total + rate
 
     zero = jnp.zeros((pieces, lanes), f32)
-    states, total = lax.fori_loop(0, steps, body, ((zero,) * size, zero), unroll=4)
+    states, total = lax.fori_loop(0, steps, body, ((zero,) * size, zero), unroll=8)
     for n in range(size):
         ends[n] = states[n]
     sums[...] = total
@@ -286,7 +286,7 @@
         scanned[second, :] = high
         return tuple(out)
 
-    states = lax.fori_loop(0, steps // 2, body, tuple(begin[n] for n in range(size)))
+    states = lax.fori_loop(0, steps // 2, body, tuple(begin[n] for n in range(size)), unroll=2)
     for n in range(size):
         final[n] = states[n]
         last = jnp.concatenate([states[n], states[n]], axis=0).astype(bf16)
@@ -325,7 +325,7 @@
         )
 
     zero = jnp.zeros((pieces, lanes), f32)
-    carried = lax.fori_loop(0, steps, body, (zero,) * size, unroll=4)
+    carried = lax.fori_loop(0, steps, body, (zero,) * size, unroll=8)
     for n in range(size):
         heads[n] = carried[n]
     reached = heads[:, pieces - 1, :]
@@ -431,7 +431,7 @@
         carried = tuple(stop[n] for n in range(size))
         for k in reversed(range(chunks)):
             step = functools.partial(body, fresh, stored_states[k], k * span)
-            carried = lax.fori_loop(0, span, step, carried)
+            carried = lax.fori_loop(0, span, step, carried, unroll=2)
 
     pl.when(group == 0)(lambda: sweep(True))
     pl.when(group > 0)(lambda: sweep(False))

time: 535 us -> 532 us (level)
  no operation moved by 1% of the time
where the time goes in v6:
time: 532 us; the launch traced here: 524 us
  Pallas kernels  133 us (25%)
  waiting for transfers between devices  93.8 us (18%)
  matrix products  93.5 us (18%)
  other arithmetic  80.6 us (15%)
  starting transfers between devices  61.8 us (12%)
  local copies, waits for them, and re-layouts  59.1 us (11%)
    ppermute x48, waiting for transfers between devices, swap(): lax.ppermute(value, axis, [(i, i ^ mask) for i in range(lax.axis_size(axi...  82.1 us
    pallas_call x1, Pallas kernels, per_device(): second_scan(*scan_inputs, begin, before, skip, step_padded, *kept)  37.5 us
    dot_general x12, matrix products, matmul(): return jnp.dot(left, right, preferred_element_type=f32)  36.2 us
    ppermute x48, starting transfers between devices, swap(): lax.ppermute(value, axis, [(i, i ^ mask) for i in range(lax.axis_size(axi...  32.7 us
    dot_general x10, matrix products, transposed_right(): lax.dot_general(left, right, (((1,), (1,)), ((), ())), preferred_element_...  31.4 us
    ppermute x6, starting transfers between devices, shifted(): lax.ppermute(value, axis, [(i, i + by) for i in range(size) if 0 <= i + b...  29.2 us
    dot_general x8, matrix products, transposed_left(): lax.dot_general(left, right, (((0,), (0,)), ((), ())), preferred_element_...  25.8 us
    pallas_call x1, Pallas kernels, per_device(): scan_forward[0](*scan3, decay_two, gate3, skip, ends, sums, arriving)  25.8 us
  transfers between devices with their start and end apart: 54, of which 22 were waited for; matrix products, arithmetic and copies ran while one was open for 33% of the time, Pallas kernels for 17%

profile of v6, /device:TPU:0, one launch (start us, length us, event | category | flops | bytes accessed | tf_op | source)
XLA Modules:
  0.0 524.1 jit_solution(17318883700148040694)
XLA Ops:
  0.7 4.9 norm_rows.1
  5.5 5.2 convolution_convert_fusion.11.inner
  11.9 4.9 collective-permute-start
  16.9 6.9 %fusion.100 = f32[1024,768]{1,0:T(8,128)} fusion(bf16[1024,1536]{1,0:T(8,128)(2,1)} %norm_rows.1, bf16[1536,768]{1,0:T(8,128)(2,1)} %param.24), kind=kOutput, calls=%fused_computation.293 | convolution fusion | flops 2415919104 | bytes 8650752 | tf_op jit(solution)/shard_map/dot_general | solution.py:28
  27.0 3.8 fusion.96
  43.0 3.5 compare_select_fusion.rates.refs_0_
  46.5 14.9 %scan_ends.1 = (f32[16,8,768]{2,1,0:T(8,128)}, f32[8,768]{1,0:T(8,128)}, f32[16,768]{1,0:T(8,128)}, f32[16,768]{1,0:T(8,128)}) custom-call(f32[1024,768]{1,0:T(8,128)} %compare_select_fusion.rates.refs_0_, f32[1024,768]{1,0:T(8,128)} %get-tuple-element.203.mixed.refs_1_, f32[1024,128]{1,0:T(8,128)} %broadcast_select_fusion.4.proj.refs_3_, ...), custom_call_target="tpu_custom_call" | custom-call | flops 12582912 | tf_op jit(solution)/shard_map/scan_ends/pallas_call | solution.py:830
  62.2 3.5 collective-permute-start.3
  68.7 16.4 %collective-permute-start.4 = (f32[2,16,768]{2,1,0:T(8,128)S(1)}, f32[2,16,768]{2,1,0:T(8,128)}, u32[]{:S(2)}, u32[]{:S(2)}) collective-permute-start(f32[2,16,768]{2,1,0:T(8,128)S(1)} %pad_maximum_fusion.9), channel_id=1, source_target_pairs={{0,8},{4,12},{1,9},{5,13},{2,10},{6,14},{3,11},{7,15},{16,24},{20,... | collective-permute-start | bytes 294920 | tf_op jit(solution)/shard_map/ppermute | solution.py:45
  87.1 25.8 %scan_forward.1 = (bf16[1024,768]{1,0:T(8,128)(2,1)}, bf16[1024,768]{1,0:T(8,128)(2,1)}, bf16[16,1040,768]{2,1,0:T(8,128)(2,1)}, f32[16,8,768]{2,1,0:T(8,128)}) custom-call(f32[8,128,768]{2,1,0:T(8,128)} %bitcast.313, f32[8,128,768]{2,1,0:T(8,128)} %bitcast.314, f32[8,128,128]{2,1,0:T(8,128)} %bitcast.315, ...), custom_call_target="tpu_custom_call" | custom-call | flops 12582912 | tf_op jit(solution)/shard_map/scan_forward/pallas_call | solution.py:842
  127.4 18.7 %collective-permute-done.7 = bf16[256,1536]{1,0:T(8,128)(2,1)} collective-permute-done((bf16[256,1536]{1,0:T(8,128)(2,1)}, bf16[256,1536]{1,0:T(8,128)(2,1)}, u32[]{:S(2)}, u32[]{:S(2)}) %collective-permute-start.7) | collective-permute-done | bytes 786464 | tf_op jit(solution)/shard_map/ppermute | solution.py:40
  160.2 3.7 multiply_convert_fusion.5
  191.8 3.7 convolution_convert_fusion.3
  195.6 3.8 convolution_convert_fusion.2
  204.5 3.9 convolution_convert_fusion.1
  219.9 14.5 %collective-permute-done.15 = bf16[256,1536]{1,0:T(8,128)(2,1)S(1)} collective-permute-done((bf16[256,1536]{1,0:T(8,128)(2,1)S(1)}, bf16[256,1536]{1,0:T(8,128)(2,1)S(1)}, u32[]{:S(2)}, u32[]{:S(2)}) %collective-permute-start.15) | collective-permute-done | bytes 786464 | tf_op jit(solution)/shard_map/ppermute | solution.py:40
  240.0 5.9 %multiply_reduce_fusion = (bf16[768]{0:T(1024)(128)(2,1)}, f32[1024,768]{1,0:T(8,128)}, bf16[1024,768]{1,0:T(8,128)(2,1)}) fusion(bf16[1024,768]{1,0:T(8,128)(2,1)S(1)} %copy-done.5, f32[1024,768]{1,0:T(8,128)S(1)} %copy-done.30, bf16[1024,768]{1,0:T(8,128)(2,1)S(1)} %copy-done.98, bf16[1024,1536]{1,0:T(8,128)(2,1)S(1)} %constant_dynamic-update-slice_fusion.4, ...), kind=kOutput, calls=%fused_computation.28 | convolution fusion | flops 2428501248 | bytes 16516608 | tf_op jit(solution)/shard_map/dot_general | solution.py:36
  245.9 14.8 %scan_heads.1 = (f32[16,8,768]{2,1,0:T(8,128)}, f32[16,768]{1,0:T(8,128)}) custom-call(f32[1024,768]{1,0:T(8,128)} %compare_select_fusion.rates.refs_0_, f32[1024,768]{1,0:T(8,128)} %get-tuple-element.126.slope.refs_2_, f32[1024,128]{1,0:T(8,128)} %broadcast_select_fusion.4.proj.refs_3_, f32[16,768]{1,0:T(8,128)} %bitcast_multiply_fusion.4.dec.refs_3_.refs_4_, ...), custom_call_target="tpu_custom_call" | custom-call | flops 12582912 | tf_op jit(solution)/shard_map/scan_heads/pallas_call | solution.py:904
  263.3 6.5 %convolution_convert_fusion.6 = bf16[1536,768]{1,0:T(8,128)(2,1)} fusion(bf16[1024,1536]{1,0:T(8,128)(2,1)} %copy-done.24, bf16[1024,768]{1,0:T(8,128)(2,1)} %get-tuple-element.114), kind=kOutput, calls=%fused_computation.7 | convolution fusion | flops 2417098752 | bytes 7077888 | tf_op jit(solution)/shard_map/dot_general | solution.py:32
  271.1 4.2 convolution_convert_fusion.5
  275.3 4.6 collective-permute-done.22
  293.3 24.8 %scan_backward.2 = (bf16[1024,768]{1,0:T(8,128)(2,1)}, f32[1024,768]{1,0:T(8,128)}, f32[1024,128]{1,0:T(8,128)}, f32[16,768]{1,0:T(8,128)}, f32[1,768]{1,0:T(1,128)}) custom-call(f32[1024,768]{1,0:T(8,128)} %compare_select_fusion.rates.refs_0_, f32[1024,768]{1,0:T(8,128)} %get-tuple-element.203.mixed.refs_1_, f32[1024,768]{1,0:T(8,128)} %get-tuple-element.126.slope.refs_2_, ...), custom_call_target="tpu_custom_call" | custom-call | flops 12582912 | tf_op jit(solution)/shard_map/scan_backward/pallas_call | solution.py:929
  338.2 37.5 %scan_backward.3 = (bf16[1024,768]{1,0:T(8,128)(2,1)}, f32[1024,768]{1,0:T(8,128)}, f32[1024,128]{1,0:T(8,128)}, f32[16,768]{1,0:T(8,128)}, f32[1,768]{1,0:T(1,128)}) custom-call(f32[1024,768]{1,0:T(8,128)} %compare_select_fusion.rates.refs_0_, ...), custom_call_target="tpu_custom_call", output_to_operand_aliasing={{0}: (11, {}), {1}: (12, {}), {3}: (13, {}), {4}: (14, {})} | custom-call | flops 12582912 | tf_op jit(solution)/shard_map/scan_backward/pallas_call | solution.py:934
  379.1 4.8 collective-permute-done.29
  394.4 4.0 convolution_convert_fusion
  403.4 9.8 %conv_backward.1 = (bf16[1024,768]{1,0:T(8,128)(2,1)}, f32[16,768]{1,0:T(8,128)}, f32[8,768]{1,0:T(8,128)}, f32[8,768]{1,0:T(8,128)}) custom-call(bf16[1024,128]{1,0:T(8,128)(2,1)} %add_convert_fusion.5.low, bf16[768,128]{1,0:T(8,128)(2,1)} %state_proj.1, f32[1024,768]{1,0:T(8,128)} %get-tuple-element.156.direct, bf16[1024,768]{1,0:T(8,128)(2,1)} %copy-done.7, ...), custom_call_target="tpu_custom_call" | custom-call | flops 1024 | tf_op jit(solution)/shard_map/conv_backward/pallas_call | solution.py:953
  415.6 4.8 collective-permute-done.33
  421.0 3.8 fusion.8
  452.9 8.3 %collective-permute-done.38 = bf16[256,1536]{1,0:T(8,128)(2,1)S(1)} collective-permute-done((bf16[256,1536]{1,0:T(8,128)(2,1)S(1)}, bf16[256,1536]{1,0:T(8,128)(2,1)S(1)}, u32[]{:S(2)}, u32[]{:S(2)}) %collective-permute-start.38) | collective-permute-done | bytes 786464 | tf_op jit(solution)/shard_map/ppermute | solution.py:40
  464.9 3.7 convert_add_fusion.10
  468.6 8.0 %collective-permute-done.43 = bf16[2,2,224,384]{3,2,1,0:T(8,128)(2,1)} collective-permute-done((bf16[2,2,224,384]{3,2,1,0:T(8,128)(2,1)}, bf16[2,2,224,384]{3,2,1,0:T(8,128)(2,1)}, u32[]{:S(2)}, u32[]{:S(2)}) %collective-permute-start.43) | collective-permute-done | bytes 688160 | tf_op jit(solution)/shard_map/ppermute | solution.py:40
  503.7 5.7 %collective-permute-done.47 = bf16[80,768]{1,0:T(8,128)(2,1)S(1)} collective-permute-done((bf16[80,768]{1,0:T(8,128)(2,1)S(1)}, bf16[80,768]{1,0:T(8,128)(2,1)S(1)}, u32[]{:S(2)}, u32[]{:S(2)}) %collective-permute-start.47) | collective-permute-done | bytes 122912 | tf_op jit(solution)/shard_map/ppermute | solution.py:40
  (487 shorter events, 232.3 us)
Async XLA Ops:
  11.9 13.3 %collective-permute-start = (bf16[3,768]{1,0:T(4,128)(2,1)S(1)}, bf16[3,768]{1,0:T(4,128)(2,1)S(1)}, u32[]{:S(2)}, u32[]{:S(2)}) collective-permute-start(bf16[3,768]{1,0:T(4,128)(2,1)S(1)} %slice.234), channel_id=1, source_target_pairs={{0,4},{4,8},{8,12},{1,5},{5,9},{9,13},{2,6},{6,10},{10,14},{3,7},{... | collective-permute-start | bytes 13832 | tf_op jit(solution)/shard_map/ppermute | solution.py:45
  68.7 17.0 %collective-permute-start.4 = (f32[2,16,768]{2,1,0:T(8,128)S(1)}, f32[2,16,768]{2,1,0:T(8,128)}, u32[]{:S(2)}, u32[]{:S(2)}) collective-permute-start(f32[2,16,768]{2,1,0:T(8,128)S(1)} %pad_maximum_fusion.9), channel_id=1, source_target_pairs={{0,8},{4,12},{1,9},{5,13},{2,10},{6,14},{3,11},{7,15},{16,24},{20,... | collective-permute-start | bytes 294920 | tf_op jit(solution)/shard_map/ppermute | solution.py:45
  125.9 20.3 %collective-permute-start.7 = (bf16[256,1536]{1,0:T(8,128)(2,1)}, bf16[256,1536]{1,0:T(8,128)(2,1)}, u32[]{:S(2)}, u32[]{:S(2)}) collective-permute-start(bf16[256,1536]{1,0:T(8,128)(2,1)} %add_convert_fusion.4), channel_id=1, source_target_pairs={{0,2},{1,3},{2,0},{3,1},{4,6},{5,7},{6,4},{7,5},{8,10},{9,11},{10,... | collective-permute-start | bytes 2359304 | tf_op jit(solution)/shard_map/ppermute | solution.py:40
  151.4 20.3 %collective-permute-start.10 = (bf16[256,1536]{1,0:T(8,128)(2,1)}, bf16[256,1536]{1,0:T(8,128)(2,1)}, u32[]{:S(2)}, u32[]{:S(2)}) collective-permute-start(bf16[256,1536]{1,0:T(8,128)(2,1)} %multiply_convert_fusion.8), channel_id=1, source_target_pairs={{0,2},{1,3},{2,0},{3,1},{4,6},{5,7},{6,4},{7,5},{8,10},{9,11},{10,... | collective-permute-start | bytes 2359304 | tf_op jit(solution)/shard_map/ppermute | solution.py:40
  188.5 20.2 %collective-permute-start.9 = (bf16[256,1536]{1,0:T(8,128)(2,1)S(1)}, bf16[256,1536]{1,0:T(8,128)(2,1)S(1)}, u32[]{:S(2)}, u32[]{:S(2)}) collective-permute-start(bf16[256,1536]{1,0:T(8,128)(2,1)S(1)} %constant_dynamic-slice_fusion.5), channel_id=1, source_target_pairs={{0,1},{1,0},{2,3},{3,2},{4,5},{5,4},{6,7},{7,6},{8,9},{9,8},{10,11... | collective-permute-start | bytes 2359304 | tf_op jit(solution)/shard_map/ppermute | solution.py:40
  190.3 19.7 %collective-permute-start.13 = (bf16[256,1536]{1,0:T(8,128)(2,1)S(1)}, bf16[256,1536]{1,0:T(8,128)(2,1)S(1)}, u32[]{:S(2)}, u32[]{:S(2)}) collective-permute-start(bf16[256,1536]{1,0:T(8,128)(2,1)S(1)} %add_convert_fusion.3), channel_id=1, source_target_pairs={{0,2},{1,3},{2,0},{3,1},{4,6},{5,7},{6,4},{7,5},{8,10},{9,11},{10,... | collective-permute-start | bytes 2359304 | tf_op jit(solution)/shard_map/ppermute | solution.py:40
  203.0 72.4 %collective-permute-start.23 = (bf16[2,2,192,2048]{3,2,1,0:T(8,128)(2,1)}, bf16[2,2,192,2048]{3,2,1,0:T(8,128)(2,1)}, u32[]{:S(2)}, u32[]{:S(2)}) collective-permute-start(bf16[2,2,192,2048]{3,2,1,0:T(8,128)(2,1)} %pad_maximum_fusion.2), channel_id=1, source_target_pairs={{0,16},{16,0},{1,17},{17,1},{2,18},{18,2},{3,19},{19,3},{4,20},{20... | collective-permute-start | bytes 9437192 | tf_op jit(solution)/shard_map/ppermute | solution.py:40
  208.6 52.2 %collective-permute-start.20 = (bf16[2,2,192,1024]{3,2,1,0:T(8,128)(2,1)S(1)}, bf16[2,2,192,1024]{3,2,1,0:T(8,128)(2,1)}, u32[]{:S(2)}, u32[]{:S(2)}) collective-permute-start(bf16[2,2,192,1024]{3,2,1,0:T(8,128)(2,1)S(1)} %dynamic-slice_bitcast_fusion), channel_id=1, source_target_pairs={{0,4},{4,0},{8,12},{12,8},{1,5},{5,1},{9,13},{13,9},{2,6},{6,2},{1... | collective-permute-start | bytes 4718600 | tf_op jit(solution)/shard_map/ppermute | solution.py:40
  215.4 19.0 %collective-permute-start.15 = (bf16[256,1536]{1,0:T(8,128)(2,1)S(1)}, bf16[256,1536]{1,0:T(8,128)(2,1)S(1)}, u32[]{:S(2)}, u32[]{:S(2)}) collective-permute-start(bf16[256,1536]{1,0:T(8,128)(2,1)S(1)} %get-tuple-element.125), channel_id=1, source_target_pairs={{0,2},{1,3},{2,0},{3,1},{4,6},{5,7},{6,4},{7,5},{8,10},{9,11},{10,... | collective-permute-start | bytes 2359304 | tf_op jit(solution)/shard_map/ppermute | solution.py:40
  216.3 18.1 %collective-permute-start.16 = (bf16[256,1536]{1,0:T(8,128)(2,1)S(1)}, bf16[256,1536]{1,0:T(8,128)(2,1)S(1)}, u32[]{:S(2)}, u32[]{:S(2)}) collective-permute-start(bf16[256,1536]{1,0:T(8,128)(2,1)S(1)} %get-tuple-element.125), channel_id=1, source_target_pairs={{0,1},{1,0},{2,3},{3,2},{4,5},{5,4},{6,7},{7,6},{8,9},{9,8},{10,11... | collective-permute-start | bytes 2359304 | tf_op jit(solution)/shard_map/ppermute | solution.py:40
  235.5 51.1 %collective-permute-start.14 = (bf16[256,1536]{1,0:T(8,128)(2,1)}, bf16[256,1536]{1,0:T(8,128)(2,1)}, u32[]{:S(2)}, u32[]{:S(2)}) collective-permute-start(bf16[256,1536]{1,0:T(8,128)(2,1)} %constant_dynamic-slice_fusion.3), channel_id=1, source_target_pairs={{0,1},{1,0},{2,3},{3,2},{4,5},{5,4},{6,7},{7,6},{8,9},{9,8},{10,11... | collective-permute-start | bytes 2359304 | tf_op jit(solution)/shard_map/ppermute | solution.py:40
  237.9 22.9 %collective-permute-start.18 = (bf16[256,1536]{1,0:T(8,128)(2,1)}, bf16[256,1536]{1,0:T(8,128)(2,1)S(1)}, u32[]{:S(2)}, u32[]{:S(2)}) collective-permute-start(bf16[256,1536]{1,0:T(8,128)(2,1)} %add_convert_fusion.2), channel_id=1, source_target_pairs={{0,2},{1,3},{2,0},{3,1},{4,6},{5,7},{6,4},{7,5},{8,10},{9,11},{10,... | collective-permute-start | bytes 2359304 | tf_op jit(solution)/shard_map/ppermute | solution.py:40
  286.2 34.7 %collective-permute-start.26 = (bf16[2,192,2048]{2,1,0:T(8,128)(2,1)}, bf16[2,192,2048]{2,1,0:T(8,128)(2,1)}, u32[]{:S(2)}, u32[]{:S(2)}) collective-permute-start(bf16[2,192,2048]{2,1,0:T(8,128)(2,1)} %fusion.7), channel_id=1, source_target_pairs={{0,4},{4,0},{8,12},{12,8},{1,5},{5,1},{9,13},{13,9},{2,6},{6,2},{1... | collective-permute-start | bytes 4718600 | tf_op jit(solution)/shard_map/ppermute | solution.py:40
  288.4 29.8 %collective-permute-start.27 = (bf16[2,192,1024]{2,1,0:T(8,128)(2,1)S(1)}, bf16[2,192,1024]{2,1,0:T(8,128)(2,1)S(1)}, u32[]{:S(2)}, u32[]{:S(2)}) collective-permute-start(bf16[2,192,1024]{2,1,0:T(8,128)(2,1)S(1)} %fusion.40), channel_id=1, source_target_pairs={{0,16},{16,0},{1,17},{17,1},{2,18},{18,2},{3,19},{19,3},{4,20},{20... | collective-permute-start | bytes 2359304 | tf_op jit(solution)/shard_map/ppermute | solution.py:40
  291.4 26.8 %collective-permute-start.24 = (bf16[256,1536]{1,0:T(8,128)(2,1)}, bf16[256,1536]{1,0:T(8,128)(2,1)S(1)}, u32[]{:S(2)}, u32[]{:S(2)}) collective-permute-start(bf16[256,1536]{1,0:T(8,128)(2,1)} %add_convert_fusion.1), channel_id=1, source_target_pairs={{0,2},{1,3},{2,0},{3,1},{4,6},{5,7},{6,4},{7,5},{8,10},{9,11},{10,... | collective-permute-start | bytes 2359304 | tf_op jit(solution)/shard_map/ppermute | solution.py:40
  324.6 59.2 %collective-permute-start.30 = (bf16[2,2,192,1536]{3,2,1,0:T(8,128)(2,1)}, bf16[2,2,192,1536]{3,2,1,0:T(8,128)(2,1)}, u32[]{:S(2)}, u32[]{:S(2)}) collective-permute-start(bf16[2,2,192,1536]{3,2,1,0:T(8,128)(2,1)} %pad_maximum_fusion.3), channel_id=1, source_target_pairs={{0,16},{16,0},{1,17},{17,1},{2,18},{18,2},{3,19},{19,3},{4,20},{20... | collective-permute-start | bytes 7077896 | tf_op jit(solution)/shard_map/ppermute | solution.py:40
  331.3 52.5 %collective-permute-start.28 = (bf16[192,2048]{1,0:T(8,128)(2,1)S(1)}, bf16[192,2048]{1,0:T(8,128)(2,1)}, u32[]{:S(2)}, u32[]{:S(2)}) collective-permute-start(bf16[192,2048]{1,0:T(8,128)(2,1)S(1)} %fusion.39), channel_id=1, source_target_pairs={{0,8},{4,12},{8,0},{12,4},{1,9},{5,13},{9,1},{13,5},{2,10},{6,14},... | collective-permute-start | bytes 2359304 | tf_op jit(solution)/shard_map/ppermute | solution.py:40
  335.2 48.6 %collective-permute-start.29 = (bf16[192,1024]{1,0:T(8,128)(2,1)S(1)}, bf16[192,1024]{1,0:T(8,128)(2,1)}, u32[]{:S(2)}, u32[]{:S(2)}) collective-permute-start(bf16[192,1024]{1,0:T(8,128)(2,1)S(1)} %fusion.48), channel_id=1, source_target_pairs={{0,8},{4,12},{8,0},{12,4},{1,9},{5,13},{9,1},{13,5},{2,10},{6,14},... | collective-permute-start | bytes 1179656 | tf_op jit(solution)/shard_map/ppermute | solution.py:40
  338.2 108.8 %collective-permute-start.25 = (bf16[256,1536]{1,0:T(8,128)(2,1)}, bf16[256,1536]{1,0:T(8,128)(2,1)}, u32[]{:S(2)}, u32[]{:S(2)}) collective-permute-start(bf16[256,1536]{1,0:T(8,128)(2,1)} %add_convert_fusion.1), channel_id=1, source_target_pairs={{0,1},{1,0},{2,3},{3,2},{4,5},{5,4},{6,7},{7,6},{8,9},{9,8},{10,11... | collective-permute-start | bytes 2359304 | tf_op jit(solution)/shard_map/ppermute | solution.py:40
  391.2 38.7 %collective-permute-start.36 = (bf16[2,192,1536]{2,1,0:T(8,128)(2,1)}, bf16[2,192,1536]{2,1,0:T(8,128)(2,1)}, u32[]{:S(2)}, u32[]{:S(2)}) collective-permute-start(bf16[2,192,1536]{2,1,0:T(8,128)(2,1)} %fusion.16), channel_id=1, source_target_pairs={{0,4},{4,0},{8,12},{12,8},{1,5},{5,1},{9,13},{13,9},{2,6},{6,2},{1... | collective-permute-start | bytes 3538952 | tf_op jit(solution)/shard_map/ppermute | solution.py:40
  425.8 14.2 %collective-permute-start.34 = (bf16[256,1536]{1,0:T(8,128)(2,1)}, bf16[256,1536]{1,0:T(8,128)(2,1)}, u32[]{:S(2)}, u32[]{:S(2)}) collective-permute-start(bf16[256,1536]{1,0:T(8,128)(2,1)} %constant_dynamic-slice_fusion.1), channel_id=1, source_target_pairs={{0,1},{1,0},{2,3},{3,2},{4,5},{5,4},{6,7},{7,6},{8,9},{9,8},{10,11... | collective-permute-start | bytes 2359304 | tf_op jit(solution)/shard_map/ppermute | solution.py:40
  432.2 77.3 %collective-permute-start.52 = (bf16[192,1536]{1,0:T(8,128)(2,1)}, bf16[192,1536]{1,0:T(8,128)(2,1)}, u32[]{:S(2)}, u32[]{:S(2)}) collective-permute-start(bf16[192,1536]{1,0:T(8,128)(2,1)} %fusion.44), channel_id=1, source_target_pairs={{0,8},{4,12},{8,0},{12,4},{1,9},{5,13},{9,1},{13,5},{2,10},{6,14},... | collective-permute-start | bytes 1769480 | tf_op jit(solution)/shard_map/ppermute | solution.py:40
  437.6 15.3 %collective-permute-start.37 = (bf16[256,1536]{1,0:T(8,128)(2,1)S(1)}, bf16[256,1536]{1,0:T(8,128)(2,1)S(1)}, u32[]{:S(2)}, u32[]{:S(2)}) collective-permute-start(bf16[256,1536]{1,0:T(8,128)(2,1)S(1)} %constant_dynamic-slice_fusion), channel_id=1, source_target_pairs={{0,1},{1,0},{2,3},{3,2},{4,5},{5,4},{6,7},{7,6},{8,9},{9,8},{10,11... | collective-permute-start | bytes 2359304 | tf_op jit(solution)/shard_map/ppermute | solution.py:40
  441.3 19.8 %collective-permute-start.38 = (bf16[256,1536]{1,0:T(8,128)(2,1)S(1)}, bf16[256,1536]{1,0:T(8,128)(2,1)S(1)}, u32[]{:S(2)}, u32[]{:S(2)}) collective-permute-start(bf16[256,1536]{1,0:T(8,128)(2,1)S(1)} %add_convert_fusion), channel_id=1, source_target_pairs={{0,2},{1,3},{2,0},{3,1},{4,6},{5,7},{6,4},{7,5},{8,10},{9,11},{10,... | collective-permute-start | bytes 2359304 | tf_op jit(solution)/shard_map/ppermute | solution.py:40
  448.4 28.1 %collective-permute-start.43 = (bf16[2,2,224,384]{3,2,1,0:T(8,128)(2,1)}, bf16[2,2,224,384]{3,2,1,0:T(8,128)(2,1)}, u32[]{:S(2)}, u32[]{:S(2)}) collective-permute-start(bf16[2,2,224,384]{3,2,1,0:T(8,128)(2,1)} %dynamic-slice_bitcast_fusion.11), channel_id=1, source_target_pairs={{0,4},{4,0},{8,12},{12,8},{1,5},{5,1},{9,13},{13,9},{2,6},{6,2},{1... | collective-permute-start | bytes 2064392 | tf_op jit(solution)/shard_map/ppermute | solution.py:40
  451.3 28.0 %collective-permute-start.42 = (bf16[2,2,224,384]{3,2,1,0:T(8,128)(2,1)}, bf16[2,2,224,384]{3,2,1,0:T(8,128)(2,1)}, u32[]{:S(2)}, u32[]{:S(2)}) collective-permute-start(bf16[2,2,224,384]{3,2,1,0:T(8,128)(2,1)} %dynamic-slice_bitcast_fusion.12), channel_id=1, source_target_pairs={{0,16},{16,0},{1,17},{17,1},{2,18},{18,2},{3,19},{19,3},{4,20},{20... | collective-permute-start | bytes 2064392 | tf_op jit(solution)/shard_map/ppermute | solution.py:40
  463.6 19.4 %collective-permute-start.39 = (bf16[256,1536]{1,0:T(8,128)(2,1)}, bf16[256,1536]{1,0:T(8,128)(2,1)}, u32[]{:S(2)}, u32[]{:S(2)}) collective-permute-start(bf16[256,1536]{1,0:T(8,128)(2,1)} %fusion.35), channel_id=1, source_target_pairs={{0,2},{1,3},{2,0},{3,1},{4,6},{5,7},{6,4},{7,5},{8,10},{9,11},{10,... | collective-permute-start | bytes 2359304 | tf_op jit(solution)/shard_map/ppermute | solution.py:40
  464.8 18.2 %collective-permute-start.40 = (bf16[256,1536]{1,0:T(8,128)(2,1)}, bf16[256,1536]{1,0:T(8,128)(2,1)}, u32[]{:S(2)}, u32[]{:S(2)}) collective-permute-start(bf16[256,1536]{1,0:T(8,128)(2,1)} %fusion.35), channel_id=1, source_target_pairs={{0,1},{1,0},{2,3},{3,2},{4,5},{5,4},{6,7},{7,6},{8,9},{9,8},{10,11... | collective-permute-start | bytes 2359304 | tf_op jit(solution)/shard_map/ppermute | solution.py:40
  483.0 38.4 %collective-permute-start.44 = (bf16[256,1536]{1,0:T(8,128)(2,1)}, bf16[256,1536]{1,0:T(8,128)(2,1)}, u32[]{:S(2)}, u32[]{:S(2)}) collective-permute-start(bf16[256,1536]{1,0:T(8,128)(2,1)} %collective-permute-done.39), channel_id=1, source_target_pairs={{0,1},{1,0},{2,3},{3,2},{4,5},{5,4},{6,7},{7,6},{8,9},{9,8},{10,11... | collective-permute-start | bytes 2359304 | tf_op jit(solution)/shard_map/ppermute | solution.py:40
  483.7 16.6 %collective-permute-start.46 = (bf16[80,768]{1,0:T(8,128)(2,1)}, bf16[80,768]{1,0:T(8,128)(2,1)S(1)}, u32[]{:S(2)}, u32[]{:S(2)}) collective-permute-start(bf16[80,768]{1,0:T(8,128)(2,1)} %pad_dynamic-update-slice_fusion), channel_id=1, source_target_pairs={{0,16},{16,0},{1,17},{17,1},{2,18},{18,2},{3,19},{19,3},{4,20},{20... | collective-permute-start | bytes 368648 | tf_op jit(solution)/shard_map/ppermute | solution.py:40
  489.6 24.8 %collective-permute-start.53 = (bf16[224,384]{1,0:T(8,128)(2,1)S(1)}, bf16[224,384]{1,0:T(8,128)(2,1)S(1)}, u32[]{:S(2)}, u32[]{:S(2)}) collective-permute-start(bf16[224,384]{1,0:T(8,128)(2,1)S(1)} %fusion.57), channel_id=1, source_target_pairs={{0,8},{4,12},{8,0},{12,4},{1,9},{5,13},{9,1},{13,5},{2,10},{6,14},... | collective-permute-start | bytes 516104 | tf_op jit(solution)/shard_map/ppermute | solution.py:40
  493.6 20.8 %collective-permute-start.50 = (bf16[224,384]{1,0:T(8,128)(2,1)S(1)}, bf16[224,384]{1,0:T(8,128)(2,1)S(1)}, u32[]{:S(2)}, u32[]{:S(2)}) collective-permute-start(bf16[224,384]{1,0:T(8,128)(2,1)S(1)} %fusion.59), channel_id=1, source_target_pairs={{0,8},{4,12},{8,0},{12,4},{1,9},{5,13},{9,1},{13,5},{2,10},{6,14},... | collective-permute-start | bytes 516104 | tf_op jit(solution)/shard_map/ppermute | solution.py:40
  (131 other events, 889.9 us)
